TPU v7x, 256 devices: a whole 4x4x8 slice. The times are simulated.
256 devices in a mesh: strip: 16 (over z, x_lo), period: 16 (over y, x_hi, core).
Axes of the slice: x: 4 (x_hi: 2, x_lo: 2; x = x_hi * 2 + x_lo), y: 4, z: 8, core: 2. Of those that a mesh axis runs over, the one named last changes fastest.
Arguments:
- u_start: float32 [16, 64, 64, 128], P('strip', 'period'), may hold values from 0 to 0.02
- dual_prec: float32 [5, 16, 64, 64, 128], P(None, 'strip', 'period'), may hold values from 0 to 0.5
- dual_bound: float32 [16, 64, 64, 128], P('strip', 'period'), may hold values from 0 to 0.5
- dual_cap: float32 [64], P('period'), may hold values from 0 to 2
- capacity: float32 [64], P('period'), may hold values from 0.005 to 0.03
- block_value: float32 [16, 64, 128], P('strip'), may hold values from -6 to 6
- ton_class: int32 [16, 64, 128], P('strip'), may hold values from 0 to 7
- density: float32 [8], replicated, may hold values from 1 to 3
- slope_code: int32 [16, 128], P('strip'), may hold values from 0 to 15
- omega_start: float32 [1], replicated, may hold values from 0.5 to 2
Outputs:
- mined_share: float32 [16, 64, 64, 128], P('strip', 'period')
- arc_prices: float32 [5, 16, 64, 64, 128], P(None, 'strip', 'period')
- bound_prices: float32 [16, 64, 64, 128], P('strip', 'period')
- capacity_prices: float32 [64], P('period')
- primal_weight: float32 [1], replicated
All inputs are finite; a program needn't handle non-finite values.
Results may differ from a plain program's by a relative error of at most 0.0001.
Values sent between devices are 32-bit elements; how exact they have to be, the bound alone decides.
No kernel may reach another device: no remote copies, remote signals or barrier semaphores. Data moves between devices by JAX's collectives and lax.ppermute only.
A program may use at most 64 MiB of HBM per device.

v0:
```python
import math

import jax
import jax.numpy as jnp
from jax import lax
from jax.sharding import PartitionSpec as P

OUTER = 2
INNER = 3


ARC_OFFSETS = ((0, 0), (1, 0), (-1, 0), (0, 1), (0, -1))
RATE = math.log(1.1) / 12.0
EPS = 1e-06
SLOPE = 11.0


def from_behind(value, axis, by):
    devices = lax.axis_size(axis)
    pairs = [(i, i + by) for i in range(devices) if 0 <= i + by < devices]
    return lax.ppermute(value, axis, pairs)


def carried_in(value, axis, combine, identity, reverse):
    devices, index = (lax.axis_size(axis), lax.axis_index(axis))
    everything = lax.all_gather(value, axis)
    start = jnp.broadcast_to(jnp.asarray(identity, value.dtype), value.shape)

    def lap(k, before):
        at = devices - 1 - k if reverse else k
        reached = at > index if reverse else at < index
        new = combine(before, everything[at])
        return jnp.where(reached, new, before)

    return lax.fori_loop(0, devices, lap, start)


def padded_2(value, sides, width):
    for axis, dim in sides:
        devices, length = (lax.axis_size(axis), value.shape[dim])
        up = [(i, (i + 1) % devices) for i in range(devices - 1)]
        down = [(j, i) for i, j in up]
        last = lax.slice_in_dim(value, length - width, length, axis=dim)
        first = lax.slice_in_dim(value, 0, width, axis=dim)
        before = lax.ppermute(last, axis, up)
        after = lax.ppermute(first, axis, down)
        value = jnp.concatenate([before, value, after], axis=dim)
    return value


def arc_masks(code_rows, first_row, total_rows, depth_cells, across):
    row_ids = (first_row + jnp.arange(code_rows.shape[0]))[:, None, None]
    depth_ids = jnp.arange(depth_cells)[None, :, None]
    col_ids = jnp.arange(across)[None, None, :]
    pattern = code_rows[:, None, :]
    mask_list = []
    for arc_index, (step_x, step_y) in enumerate(ARC_OFFSETS):
        inside = (
            (row_ids >= 0)
            & (row_ids < total_rows)
            & (row_ids + step_x >= 0)
            & (row_ids + step_x < total_rows)
        )
        inside = inside & (col_ids + step_y >= 0) & (col_ids + step_y < across) & (depth_ids >= 1)
        if arc_index > 0:
            inside = inside & (pattern // 2 ** (arc_index - 1) % 2 == 1)
        mask_list.append(inside.astype(jnp.float32))
    return jnp.stack(mask_list)


def tonnage(ton_class, density):
    class_ids = jnp.arange(density.shape[0])
    class_table = (1.0 + class_ids.astype(jnp.float32)) * density
    onehot = (class_ids[:, None, None, None] == ton_class[None]).astype(jnp.float32)
    return jnp.einsum("k,kxzy->xzy", class_table, onehot, precision=lax.Precision.HIGHEST)


def upper_cell(values_in, step_y):
    depth_cells = values_in.shape[2]
    across = values_in.shape[3]
    padded = jnp.pad(values_in, ((0, 0), (0, 0), (1, 0), (1, 1)))
    return padded[:, :, 0:depth_cells, 1 + step_y : 1 + step_y + across]


def lower_cell(values_in, step_y):
    depth_cells = values_in.shape[2]
    across = values_in.shape[3]
    padded = jnp.pad(values_in, ((0, 0), (0, 0), (0, 1), (1, 1)))
    return padded[:, :, 1 : depth_cells + 1, 1 - step_y : 1 - step_y + across]


def adjoint(arc_duals, from_left, from_right, bound_duals):
    result = jnp.sum(arc_duals, axis=0) + bound_duals
    for arc_index, (step_x, step_y) in enumerate(ARC_OFFSETS):
        source = arc_duals[arc_index]
        if step_x == 1:
            source = jnp.concatenate([from_left, source[:-1]], axis=0)
        elif step_x == -1:
            source = jnp.concatenate([source[1:], from_right], axis=0)
        result = result - lower_cell(source, step_y)
    return result


def send_rims(arc_duals):
    from_left = from_behind(arc_duals[1, -1:], "strip", 1)
    from_right = from_behind(arc_duals[2, :1], "strip", -1)
    return (from_left, from_right)


def capacity_sum(row_local):
    return lax.psum(row_local, "strip")


def add_pair(earlier, later):
    return earlier + later


def per_device(
    u_start,
    dual_prec,
    dual_bound,
    dual_cap,
    capacity,
    block_value,
    ton_class,
    density,
    slope_code,
    omega_start,
):
    rows_here = u_start.shape[0]
    periods_here = u_start.shape[1]
    depth_cells = u_start.shape[2]
    across = u_start.shape[3]
    total_rows = lax.axis_size("strip") * rows_here
    total_periods = lax.axis_size("period") * periods_here
    blocks_all = float(total_rows * depth_cells * across)
    root_blocks = math.sqrt(blocks_all)
    zero_plane = jnp.zeros((rows_here, depth_cells, across), jnp.float32)
    arc_active = arc_masks(
        slope_code, lax.axis_index("strip") * rows_here, total_rows, depth_cells, across
    )[:, :, None]
    tonnage_grid = tonnage(ton_class, density)
    tons_col = tonnage_grid[:, None]
    tons_all = lax.psum(jnp.sum(tonnage_grid), "strip")
    period_ids = (lax.axis_index("period") * periods_here + jnp.arange(periods_here)).astype(
        jnp.float32
    )[None, :, None, None]
    profit = block_value[:, None] * jnp.exp(-RATE * period_ids)
    primal = u_start
    arc_duals = dual_prec * arc_active
    bound_duals = dual_bound
    cap_duals = dual_cap
    weight = omega_start[0]
    for restart in range(OUTER):
        primal_first, duals_first, bound_first, cap_first = (
            primal,
            arc_duals,
            bound_duals,
            cap_duals,
        )
        primal_sum = jnp.zeros_like(primal)
        duals_sum = jnp.zeros_like(arc_duals)
        bound_sum = jnp.zeros_like(bound_duals)
        cap_sum = jnp.zeros_like(cap_duals)
        move_primal = jnp.float32(0.0)
        move_dual = jnp.float32(0.0)
        for sweep_index in range(INNER):
            from_left, from_right = send_rims(arc_duals)
            gradient_x = adjoint(arc_duals, from_left, from_right, bound_duals)
            local_tail = jnp.flip(jnp.cumsum(jnp.flip(gradient_x, 1), axis=1), 1)
            later_sum = carried_in(local_tail[:, 0], "period", add_pair, zero_plane, True)
            gradient_u = (
                local_tail
                + later_sum[:, None]
                + tons_col * cap_duals[None, :, None, None] / root_blocks
            )
            step_primal = 1.0 / (
                weight * (SLOPE * (total_periods - period_ids) + tons_col / root_blocks)
            )
            primal_new = jnp.maximum(primal - step_primal * (gradient_u - profit), 0.0)
            extrapolated = 2.0 * primal_new - primal
            local_head = jnp.cumsum(extrapolated, axis=1)
            earlier_sum = carried_in(local_head[:, -1], "period", add_pair, zero_plane, False)
            cumulative = local_head + earlier_sum[:, None]
            padded = padded_2(cumulative, (("strip", 0),), 1)
            step_prec = weight / (2.0 * (period_ids + 1.0))
            step_bound = weight / (period_ids + 1.0)
            new_list = []
            for arc_index, (step_x, step_y) in enumerate(ARC_OFFSETS):
                ahead_cells = upper_cell(padded[1 + step_x : 1 + step_x + rows_here], step_y)
                new_list.append(
                    jnp.maximum(arc_duals[arc_index] + step_prec * (cumulative - ahead_cells), 0.0)
                    * arc_active[arc_index]
                )
            duals_new = jnp.stack(new_list)
            bound_new = jnp.maximum(bound_duals + step_bound * (cumulative - 1.0), 0.0)
            primal_sum = primal_sum + primal_new
            duals_sum = duals_sum + duals_new
            bound_sum = bound_sum + bound_new
            row_local = jnp.einsum(
                "xzy,xtzy->t", tonnage_grid, extrapolated, precision=lax.Precision.HIGHEST
            )
            row_total = capacity_sum(row_local)
            cap_new = jnp.maximum(
                cap_duals + weight * (row_total - blocks_all * capacity) / tons_all, 0.0
            )
            cap_sum = cap_sum + cap_new
            primal, arc_duals, bound_duals, cap_duals = (primal_new, duals_new, bound_new, cap_new)
        cap_mean = cap_sum / INNER
        move_cap = jnp.sum((cap_mean - cap_first) ** 2)
        primal_mean = primal_sum / INNER
        duals_mean = duals_sum / INNER
        bound_mean = bound_sum / INNER
        move_primal = jnp.sum((primal_mean - primal_first) ** 2)
        move_dual = jnp.sum((duals_mean - duals_first) ** 2) + jnp.sum(
            (bound_mean - bound_first) ** 2
        )
        first_strip = (lax.axis_index("strip") == 0).astype(jnp.float32)
        primal_move, dual_move = lax.psum(
            (move_primal, move_dual + first_strip * move_cap), ("strip", "period")
        )
        weight = jnp.sqrt(weight * jnp.sqrt((dual_move + EPS) / (primal_move + EPS)))
        primal = primal_mean
        arc_duals = duals_mean
        bound_duals = bound_mean
        cap_duals = cap_mean
    return (primal, arc_duals, bound_duals, cap_duals, jnp.reshape(weight, (1,)))


def solution(mesh):
    in_specs = (
        P("strip", "period", None, None),
        P(None, "strip", "period", None, None),
        P("strip", "period", None, None),
        P("period"),
        P("period"),
        P("strip", None, None),
        P("strip", None, None),
        P(),
        P("strip", None),
        P(),
    )
    out_specs = (
        P("strip", "period", None, None),
        P(None, "strip", "period", None, None),
        P("strip", "period", None, None),
        P("period"),
        P(),
    )
    return jax.shard_map(
        per_device, mesh=mesh, in_specs=in_specs, out_specs=out_specs, check_vma=False
    )
```

profile of v0, /device:TPU:1, one launch (start us, length us, event | category | flops | bytes accessed | tf_op | source)
XLA Modules:
  0.0 859.0 jit_solution(16282473171194095518)
XLA Ops:
  13.6 28.3 %all_gather.36 = f32[16,1,64,128]{3,2,1,0:T(8,128)S(1)} all-gather(f32[1,1,64,128]{3,2,1,0:T(8,128)S(1)} %slice.384), channel_id=1, replica_groups=mesh['strip'=16,'period'=16] {'period'}, dimensions={0}, use_global_device_ids=true | all-gather | bytes 557056 | tf_op jit(solution)/shard_map/all_gather | solution.py:26
  43.5 21.6 %all_gather.37 = f32[16,1,64,128]{3,2,1,0:T(8,128)S(1)} all-gather(f32[1,1,64,128]{3,2,1,0:T(8,128)S(1)} %slice.385), channel_id=1, replica_groups=mesh['strip'=16,'period'=16] {'period'}, dimensions={0}, use_global_device_ids=true | all-gather | bytes 557056 | tf_op jit(solution)/shard_map/all_gather | solution.py:26
  72.1 29.8 %all-reduce.50 = (f32[4]{0:T(128)S(1)}, f32[]{:T(128)}) all-reduce(f32[4]{0:T(128)S(1)} %convolution_bitcast_fusion.5, f32[]{:T(128)} %get-tuple-element.1514), channel_id=1, replica_groups=mesh['strip'=16,'period'=16] {'strip'}, use_global_device_ids=true, to_apply=%region_10.11 | all-reduce | flops 5 | bytes 40 | tf_op jit(solution)/shard_map/psum | solution.py:111
  111.0 35.1 %all_gather.38 = f32[16,1,64,128]{3,2,1,0:T(8,128)} all-gather(f32[1,1,64,128]{3,2,1,0:T(8,128)S(1)} %slice.386), channel_id=1, replica_groups=mesh['strip'=16,'period'=16] {'period'}, dimensions={0}, use_global_device_ids=true | all-gather | bytes 557056 | tf_op jit(solution)/shard_map/all_gather | solution.py:26
  146.2 12.2 %while.182 = (s32[]{:T(128)}, f32[1,64,128]{2,1,0:T(8,128)S(1)}, s32[]{:T(128)}, f32[16,1,64,128]{3,2,1,0:T(8,128)}, s32[]{:T(128)}, /*index=5*/s32[]{:T(128)}, s32[]{:T(128)}, s32[]{:T(128)}) while((s32[]{:T(128)}, f32[1,64,128]{2,1,0:T(8,128)S(1)}, s32[]{:T(128)}, f32[16,1,64,128]{3,2,1,0:T(8,128)}, s32[]{:T(128)}, ...), condition=%wide.region_9.10_spmd.clone, body=%wide.region_8.9_spmd.clone.sunk | while | flops 24584 | bytes 98459 | solution.py:35
  158.6 23.0 %all_gather.39 = f32[16,1,64,128]{3,2,1,0:T(8,128)} all-gather(f32[1,1,64,128]{3,2,1,0:T(8,128)S(1)} %slice.387), channel_id=1, replica_groups=mesh['strip'=16,'period'=16] {'period'}, dimensions={0}, use_global_device_ids=true | all-gather | bytes 557056 | tf_op jit(solution)/shard_map/all_gather | solution.py:26
  200.6 27.3 %psum.79 = f32[4]{0:T(128)S(1)} all-reduce(f32[4]{0:T(128)S(1)} %convolution_bitcast_fusion.4), channel_id=1, replica_groups=mesh['strip'=16,'period'=16] {'strip'}, use_global_device_ids=true, to_apply=%region_19.20 | all-reduce | flops 4 | bytes 32 | tf_op jit(solution)/shard_map/psum | solution.py:111
  238.4 34.6 %all_gather.40 = f32[16,1,64,128]{3,2,1,0:T(8,128)} all-gather(f32[1,1,64,128]{3,2,1,0:T(8,128)S(1)} %slice.388), channel_id=1, replica_groups=mesh['strip'=16,'period'=16] {'period'}, dimensions={0}, use_global_device_ids=true | all-gather | bytes 557056 | tf_op jit(solution)/shard_map/all_gather | solution.py:26
  273.0 12.2 %while.184 = (s32[]{:T(128)}, f32[1,64,128]{2,1,0:T(8,128)S(1)}, s32[]{:T(128)}, f32[16,1,64,128]{3,2,1,0:T(8,128)}, s32[]{:T(128)}, /*index=5*/s32[]{:T(128)}, s32[]{:T(128)}, s32[]{:T(128)}) while((s32[]{:T(128)}, f32[1,64,128]{2,1,0:T(8,128)S(1)}, s32[]{:T(128)}, f32[16,1,64,128]{3,2,1,0:T(8,128)}, s32[]{:T(128)}, ...), condition=%wide.region_18.19_spmd.clone, body=%wide.region_17.18_spmd.clone.sunk | while | flops 24584 | bytes 98459 | solution.py:35
  286.1 23.0 %all_gather.41 = f32[16,1,64,128]{3,2,1,0:T(8,128)} all-gather(f32[1,1,64,128]{3,2,1,0:T(8,128)S(1)} %slice.389), channel_id=1, replica_groups=mesh['strip'=16,'period'=16] {'period'}, dimensions={0}, use_global_device_ids=true | all-gather | bytes 557056 | tf_op jit(solution)/shard_map/all_gather | solution.py:26
  309.1 12.2 %while.185 = (s32[]{:T(128)}, f32[1,64,128]{2,1,0:T(8,128)S(1)}, s32[]{:T(128)}, f32[16,1,64,128]{3,2,1,0:T(8,128)}, s32[]{:T(128)}, /*index=5*/s32[]{:T(128)}) while((s32[]{:T(128)}, f32[1,64,128]{2,1,0:T(8,128)S(1)}, s32[]{:T(128)}, f32[16,1,64,128]{3,2,1,0:T(8,128)}, s32[]{:T(128)}, /*index=5*/s32[]{:T(128)}) %tuple.454), condition=%wide.region_22.23_spmd.clone, body=%wide.region_21.22_spmd.clone.sunk | while | flops 24580 | bytes 98397 | solution.py:35
  328.1 28.6 %psum.80 = f32[4]{0:T(128)S(1)} all-reduce(f32[4]{0:T(128)S(1)} %convolution_bitcast_fusion.3), channel_id=1, replica_groups=mesh['strip'=16,'period'=16] {'strip'}, use_global_device_ids=true, to_apply=%region_25.26 | all-reduce | flops 4 | bytes 32 | tf_op jit(solution)/shard_map/psum | solution.py:111
  362.2 82.8 %all-reduce.49 = (f32[]{:T(128)}, f32[]{:T(128)}) all-reduce(f32[]{:T(128)S(6)} %add.1330, f32[]{:T(128)} %get-tuple-element.1469), channel_id=1, replica_groups=mesh['strip'=16,'period'=16] {'strip','period'}, use_global_device_ids=true, to_apply=%region_27.28 | all-reduce | flops 2 | bytes 16 | tf_op jit(solution)/shard_map/psum | solution.py:219
  455.7 24.9 %all_gather.42 = f32[16,1,64,128]{3,2,1,0:T(8,128)S(1)} all-gather(f32[1,1,64,128]{3,2,1,0:T(8,128)S(1)} %slice.395), channel_id=1, replica_groups=mesh['strip'=16,'period'=16] {'period'}, dimensions={0}, use_global_device_ids=true | all-gather | bytes 557056 | tf_op jit(solution)/shard_map/all_gather | solution.py:26
  481.5 22.4 %all_gather.43 = f32[16,1,64,128]{3,2,1,0:T(8,128)S(1)} all-gather(f32[1,1,64,128]{3,2,1,0:T(8,128)S(1)} %slice.396), channel_id=1, replica_groups=mesh['strip'=16,'period'=16] {'period'}, dimensions={0}, use_global_device_ids=true | all-gather | bytes 557056 | tf_op jit(solution)/shard_map/all_gather | solution.py:26
  511.8 26.3 %psum.83 = f32[4]{0:T(128)S(1)} all-reduce(f32[4]{0:T(128)S(1)} %convolution_bitcast_fusion.2), channel_id=1, replica_groups=mesh['strip'=16,'period'=16] {'strip'}, use_global_device_ids=true, to_apply=%region_40.41 | all-reduce | flops 4 | bytes 32 | tf_op jit(solution)/shard_map/psum | solution.py:111
  546.6 32.1 %all_gather.44 = f32[16,1,64,128]{3,2,1,0:T(8,128)S(1)} all-gather(f32[1,1,64,128]{3,2,1,0:T(8,128)S(1)} %slice.397), channel_id=1, replica_groups=mesh['strip'=16,'period'=16] {'period'}, dimensions={0}, use_global_device_ids=true | all-gather | bytes 557056 | tf_op jit(solution)/shard_map/all_gather | solution.py:26
  580.2 22.7 %all_gather.45 = f32[16,1,64,128]{3,2,1,0:T(8,128)S(1)} all-gather(f32[1,1,64,128]{3,2,1,0:T(8,128)S(1)} %slice.398), channel_id=1, replica_groups=mesh['strip'=16,'period'=16] {'period'}, dimensions={0}, use_global_device_ids=true | all-gather | bytes 557056 | tf_op jit(solution)/shard_map/all_gather | solution.py:26
  611.1 26.9 %psum.84 = f32[4]{0:T(128)S(1)} all-reduce(f32[4]{0:T(128)S(1)} %convolution_bitcast_fusion.1), channel_id=1, replica_groups=mesh['strip'=16,'period'=16] {'strip'}, use_global_device_ids=true, to_apply=%region_47.48 | all-reduce | flops 4 | bytes 32 | tf_op jit(solution)/shard_map/psum | solution.py:111
  649.0 33.0 %all_gather.46 = f32[16,1,64,128]{3,2,1,0:T(8,128)} all-gather(f32[1,1,64,128]{3,2,1,0:T(8,128)S(1)} %slice.399), channel_id=1, replica_groups=mesh['strip'=16,'period'=16] {'period'}, dimensions={0}, use_global_device_ids=true | all-gather | bytes 557056 | tf_op jit(solution)/shard_map/all_gather | solution.py:26
  696.4 24.0 %all_gather.47 = f32[16,1,64,128]{3,2,1,0:T(8,128)} all-gather(f32[1,1,64,128]{3,2,1,0:T(8,128)S(1)} %slice.400), channel_id=1, replica_groups=mesh['strip'=16,'period'=16] {'period'}, dimensions={0}, use_global_device_ids=true | all-gather | bytes 557056 | tf_op jit(solution)/shard_map/all_gather | solution.py:26
  720.4 12.2 %while.191 = (s32[]{:T(128)}, f32[1,64,128]{2,1,0:T(8,128)S(1)}, s32[]{:T(128)}, f32[16,1,64,128]{3,2,1,0:T(8,128)}, s32[]{:T(128)}, /*index=5*/s32[]{:T(128)}) while((s32[]{:T(128)}, f32[1,64,128]{2,1,0:T(8,128)S(1)}, s32[]{:T(128)}, f32[16,1,64,128]{3,2,1,0:T(8,128)}, s32[]{:T(128)}, /*index=5*/s32[]{:T(128)}) %tuple.472), condition=%wide.region_50.51_spmd.clone, body=%wide.region_49.50_spmd.clone.sunk | while | flops 24580 | bytes 98397 | solution.py:35
  740.0 28.0 %psum.85 = f32[4]{0:T(128)S(1)} all-reduce(f32[4]{0:T(128)S(1)} %convolution_bitcast_fusion), channel_id=1, replica_groups=mesh['strip'=16,'period'=16] {'strip'}, use_global_device_ids=true, to_apply=%region_51.52 | all-reduce | flops 4 | bytes 32 | tf_op jit(solution)/shard_map/psum | solution.py:111
  774.7 81.7 %all-reduce.48 = (f32[]{:T(128)}, f32[]{:T(128)}) all-reduce(f32[]{:T(128)S(6)} %add.1387, f32[]{:T(128)} %get-tuple-element.1435), channel_id=1, replica_groups=mesh['strip'=16,'period'=16] {'strip','period'}, use_global_device_ids=true, to_apply=%region_55.56 | all-reduce | flops 2 | bytes 16 | tf_op jit(solution)/shard_map/psum | solution.py:219
  (406 shorter events, 218.3 us)
Async XLA Ops:
  3.1 8.4 collective-permute-start
  7.0 6.3 collective-permute-start.1
  65.7 37.6 %collective-permute-start.2 = (f32[1,4,64,128]{3,2,1,0:T(8,128)S(1)}, f32[1,4,64,128]{3,2,1,0:T(8,128)S(1)}, u32[]{:S(2)}, u32[]{:S(2)}) collective-permute-start(f32[1,4,64,128]{3,2,1,0:T(8,128)S(1)} %broadcast_add_fusion.5), channel_id=1, source_target_pairs={{16,0},{32,16},{48,32},{64,48},{80,64},{96,80},{112,96},{128,112},... | collective-permute-start | bytes 393224 | tf_op jit(solution)/shard_map/ppermute | solution.py:46
  67.0 36.4 %collective-permute-start.3 = (f32[1,4,64,128]{3,2,1,0:T(8,128)S(1)}, f32[1,4,64,128]{3,2,1,0:T(8,128)S(1)}, u32[]{:S(2)}, u32[]{:S(2)}) collective-permute-start(f32[1,4,64,128]{3,2,1,0:T(8,128)S(1)} %broadcast_add_fusion.5), channel_id=1, source_target_pairs={{0,16},{16,32},{32,48},{48,64},{64,80},{80,96},{96,112},{112,128},... | collective-permute-start | bytes 393224 | tf_op jit(solution)/shard_map/ppermute | solution.py:45
  103.5 6.9 collective-permute-start.5
  104.8 5.9 collective-permute-start.4
  194.5 34.0 %collective-permute-start.6 = (f32[1,4,64,128]{3,2,1,0:T(8,128)S(1)}, f32[1,4,64,128]{3,2,1,0:T(8,128)S(1)}, u32[]{:S(2)}, u32[]{:S(2)}) collective-permute-start(f32[1,4,64,128]{3,2,1,0:T(8,128)S(1)} %broadcast_add_fusion.4), channel_id=1, source_target_pairs={{16,0},{32,16},{48,32},{64,48},{80,64},{96,80},{112,96},{128,112},... | collective-permute-start | bytes 393224 | tf_op jit(solution)/shard_map/ppermute | solution.py:46
  196.5 32.8 %collective-permute-start.7 = (f32[1,4,64,128]{3,2,1,0:T(8,128)S(1)}, f32[1,4,64,128]{3,2,1,0:T(8,128)S(1)}, u32[]{:S(2)}, u32[]{:S(2)}) collective-permute-start(f32[1,4,64,128]{3,2,1,0:T(8,128)S(1)} %broadcast_add_fusion.4), channel_id=1, source_target_pairs={{0,16},{16,32},{32,48},{48,64},{64,80},{80,96},{96,112},{112,128},... | collective-permute-start | bytes 393224 | tf_op jit(solution)/shard_map/ppermute | solution.py:45
  230.9 6.1 collective-permute-start.9
  232.2 5.9 collective-permute-start.8
  322.1 36.6 %collective-permute-start.10 = (f32[1,4,64,128]{3,2,1,0:T(8,128)S(1)}, f32[1,4,64,128]{3,2,1,0:T(8,128)S(1)}, u32[]{:S(2)}, u32[]{:S(2)}) collective-permute-start(f32[1,4,64,128]{3,2,1,0:T(8,128)S(1)} %get-tuple-element.1476), channel_id=1, source_target_pairs={{16,0},{32,16},{48,32},{64,48},{80,64},{96,80},{112,96},{128,112},... | collective-permute-start | bytes 393224 | tf_op jit(solution)/shard_map/ppermute | solution.py:46
  324.0 34.8 %collective-permute-start.11 = (f32[1,4,64,128]{3,2,1,0:T(8,128)S(1)}, f32[1,4,64,128]{3,2,1,0:T(8,128)S(1)}, u32[]{:S(2)}, u32[]{:S(2)}) collective-permute-start(f32[1,4,64,128]{3,2,1,0:T(8,128)S(1)} %get-tuple-element.1476), channel_id=1, source_target_pairs={{0,16},{16,32},{32,48},{48,64},{64,80},{80,96},{96,112},{112,128},... | collective-permute-start | bytes 393224 | tf_op jit(solution)/shard_map/ppermute | solution.py:45
  446.5 3.8 collective-permute-start.12
  448.2 7.2 collective-permute-start.13
  504.6 34.1 %collective-permute-start.14 = (f32[1,4,64,128]{3,2,1,0:T(8,128)S(1)}, f32[1,4,64,128]{3,2,1,0:T(8,128)S(1)}, u32[]{:S(2)}, u32[]{:S(2)}) collective-permute-start(f32[1,4,64,128]{3,2,1,0:T(8,128)S(1)} %broadcast_add_fusion.2), channel_id=1, source_target_pairs={{16,0},{32,16},{48,32},{64,48},{80,64},{96,80},{112,96},{128,112},... | collective-permute-start | bytes 393224 | tf_op jit(solution)/shard_map/ppermute | solution.py:46
  505.9 33.0 %collective-permute-start.15 = (f32[1,4,64,128]{3,2,1,0:T(8,128)S(1)}, f32[1,4,64,128]{3,2,1,0:T(8,128)S(1)}, u32[]{:S(2)}, u32[]{:S(2)}) collective-permute-start(f32[1,4,64,128]{3,2,1,0:T(8,128)S(1)} %broadcast_add_fusion.2), channel_id=1, source_target_pairs={{0,16},{16,32},{32,48},{48,64},{64,80},{80,96},{96,112},{112,128},... | collective-permute-start | bytes 393224 | tf_op jit(solution)/shard_map/ppermute | solution.py:45
  539.1 6.0 collective-permute-start.17
  540.4 5.9 collective-permute-start.16
  603.7 34.9 %collective-permute-start.18 = (f32[1,4,64,128]{3,2,1,0:T(8,128)S(1)}, f32[1,4,64,128]{3,2,1,0:T(8,128)S(1)}, u32[]{:S(2)}, u32[]{:S(2)}) collective-permute-start(f32[1,4,64,128]{3,2,1,0:T(8,128)S(1)} %broadcast_add_fusion.1), channel_id=1, source_target_pairs={{16,0},{32,16},{48,32},{64,48},{80,64},{96,80},{112,96},{128,112},... | collective-permute-start | bytes 393224 | tf_op jit(solution)/shard_map/ppermute | solution.py:46
  605.7 34.6 %collective-permute-start.19 = (f32[1,4,64,128]{3,2,1,0:T(8,128)S(1)}, f32[1,4,64,128]{3,2,1,0:T(8,128)}, u32[]{:S(2)}, u32[]{:S(2)}) collective-permute-start(f32[1,4,64,128]{3,2,1,0:T(8,128)S(1)} %broadcast_add_fusion.1), channel_id=1, source_target_pairs={{0,16},{16,32},{32,48},{48,64},{64,80},{80,96},{96,112},{112,128},... | collective-permute-start | bytes 393224 | tf_op jit(solution)/shard_map/ppermute | solution.py:45
  641.4 5.7 collective-permute-start.21
  642.7 5.9 collective-permute-start.20
  734.0 36.5 %collective-permute-start.22 = (f32[1,4,64,128]{3,2,1,0:T(8,128)S(1)}, f32[1,4,64,128]{3,2,1,0:T(8,128)S(1)}, u32[]{:S(2)}, u32[]{:S(2)}) collective-permute-start(f32[1,4,64,128]{3,2,1,0:T(8,128)S(1)} %get-tuple-element.1442), channel_id=1, source_target_pairs={{16,0},{32,16},{48,32},{64,48},{80,64},{96,80},{112,96},{128,112},... | collective-permute-start | bytes 393224 | tf_op jit(solution)/shard_map/ppermute | solution.py:46
  735.3 35.3 %collective-permute-start.23 = (f32[1,4,64,128]{3,2,1,0:T(8,128)S(1)}, f32[1,4,64,128]{3,2,1,0:T(8,128)S(1)}, u32[]{:S(2)}, u32[]{:S(2)}) collective-permute-start(f32[1,4,64,128]{3,2,1,0:T(8,128)S(1)} %get-tuple-element.1442), channel_id=1, source_target_pairs={{0,16},{16,32},{32,48},{48,64},{64,80},{80,96},{96,112},{112,128},... | collective-permute-start | bytes 393224 | tf_op jit(solution)/shard_map/ppermute | solution.py:45
  (15 other events, 49.7 us)
where the time goes:
time: 867 us; the launch traced here: 859 us
  blocking collectives  656 us (76%)
  other arithmetic  102 us (12%)
  starting transfers between devices  64.7 us (7%)
  waiting for transfers between devices  12.8 us (1%)
  between operations  10.2 us (1%)
    all_gather x12, blocking collectives, carried_in(): everything = lax.all_gather(value, axis)  325 us
    psum x6, blocking collectives, capacity_sum(): return lax.psum(row_local, 'strip')  167 us
    psum x2, blocking collectives, per_device(): lax.psum((move_primal, move_dual + first_strip * move_cap), ('strip', 'pe...  165 us
    select_n x192, other arithmetic, lap(): return jnp.where(reached, new, before)  74.5 us
    ppermute x12, starting transfers between devices, from_behind(): return lax.ppermute(value, axis, pairs)  29.3 us
    ppermute x6, starting transfers between devices, padded_2(): before = lax.ppermute(last, axis, up)  27.7 us
  transfers between devices with their start and end apart: 24, of which 9 were waited for; matrix products, arithmetic and copies ran while one was open for 2% of the time, Pallas kernels for 0%

commit v1 on v0

v1 whole, which is shorter than its diff:
```python
import math

import jax
import jax.numpy as jnp
from jax import lax
from jax.experimental import pallas as pl
from jax.experimental.pallas import tpu as pltpu
from jax.sharding import PartitionSpec as P

OUTER = 2
INNER = 3
NX = 16
NY = 128
NZ = 64
NP = 64
RATE = math.log(1.1) / 12.0
EPS = 1e-06
SLOPE = 11.0
BLOCKS = float(NX * NY * NZ)
ROOT = math.sqrt(BLOCKS)
F32 = jnp.float32

TILES = 16
ROWS = NP // 2
DEVICES = 256
ARCS = 5
BOUND, SHARE, LEFT, RIGHT, EXTRA = 5, 6, 7, 8, 18
SLOTS = 19
LANE_PRIMAL, LANE_DUAL, LANE_TONS = 40, 41, 42
HALO1, HALO2, HALO3, HALO4, TONS, VALUE = 5, 6, 7, 8, 9, 10
PLANES = 11


def lanes(shape):
    return lax.broadcasted_iota(jnp.int32, shape, len(shape) - 1)


def subs(shape):
    return lax.broadcasted_iota(jnp.int32, shape, len(shape) - 2)


def later_half(shape):
    return lanes(shape) >= 64


def half_matrix():
    a = subs((128, 128)) >= 64
    b = lanes((128, 128)) >= 64
    return (a == b).astype(F32)


def half_sums(rows):
    return jnp.dot(
        rows, half_matrix(), precision=lax.Precision.HIGHEST, preferred_element_type=F32
    )


def period_table():
    shape = (ROWS, 128)
    return (2 * subs(shape) + later_half(shape).astype(jnp.int32)).astype(F32)


def down(v):
    return pltpu.roll(v, 1, v.ndim - 1)


def up(v):
    return pltpu.roll(v, 127, v.ndim - 1)


def swap(v):
    return pltpu.roll(v, 64, v.ndim - 1)


def pack_kernel(caps, limits, share, prec, bound, left, right, out):
    def put(field, source):
        for a in range(2):
            both = jnp.concatenate([source(2 * a), source(2 * a + 1)], axis=0)
            turned = both.T
            out[:, 2 * field + a] = turned.reshape(TILES, 8, 128)

    for k in range(ARCS):
        put(k, lambda t, k=k: prec[k, t])
    put(BOUND, lambda t: bound[t])
    put(SHARE, lambda t: share[t])
    put(LEFT, lambda t: left[t])
    put(RIGHT, lambda t: right[t])
    half = later_half((1, 128))
    for a in range(2):
        cap_row = jnp.where(half, caps[2 * a + 1], caps[2 * a])
        limit_row = jnp.where(half, limits[2 * a + 1], limits[2 * a])
        for j in range(TILES):
            if j > 0:
                out[j, EXTRA, a : a + 1] = out[j - 1, 2 * 3 + a, 7:8]
            else:
                out[j, EXTRA, a : a + 1] = jnp.zeros((1, 128), F32)
            if j < TILES - 1:
                out[j, EXTRA, 2 + a : 3 + a] = out[j + 1, 2 * 4 + a, 0:1]
            else:
                out[j, EXTRA, 2 + a : 3 + a] = jnp.zeros((1, 128), F32)
            out[j, EXTRA, 4 + a : 5 + a] = cap_row
            out[j, EXTRA, 6 + a : 7 + a] = limit_row


def planes_kernel(place, density, slope, ton_class, value, out, turned):
    x, tile = place[0], place[1]
    classes = ton_class[...]
    tons = jnp.zeros(classes.shape, F32)
    for c in range(8):
        tons = jnp.where(classes == c, (1.0 + c) * density[c], tons)
    turned[...] = jnp.concatenate([tons, value[...]], axis=0).T
    both = turned[pl.ds(pl.multiple_of(8 * tile, 8), 8), :]
    other = swap(both)
    shape = (8, 128)
    half = later_half(shape)
    out[TONS] = jnp.where(half, other, both)
    out[VALUE] = jnp.where(half, both, other)
    codes = jnp.broadcast_to(slope[...].astype(F32), shape)
    column = 8 * tile + subs(shape)

    def code_at(column):
        picked = jnp.sum(jnp.where(lanes(shape) == column, codes, 0.0), axis=1, keepdims=True)
        return jnp.broadcast_to(picked, shape).astype(jnp.int32)

    deep = (lanes(shape) & 63) >= 1
    code = code_at(column)

    def mask(code, bit, inside):
        return (deep & (((code >> bit) & 1) == 1) & inside).astype(F32)

    out[0] = deep.astype(F32)
    out[1] = mask(code, 0, jnp.full(shape, x) + 1 < NX)
    out[2] = mask(code, 1, jnp.full(shape, x) >= 1)
    out[3] = mask(code, 2, column + 1 < NY)
    out[4] = mask(code, 3, column >= 1)
    zero = jnp.zeros(shape, jnp.int32)
    out[HALO1] = jnp.zeros(shape, F32)
    out[HALO2] = jnp.zeros(shape, F32)
    out[HALO3] = mask(code_at(zero + 8 * tile - 1), 2, zero == 0)
    out[HALO4] = mask(code_at(zero + 8 * tile + 8), 3, zero == 0)


def adjoint_row(prices, bound, halo1, halo2, halo3, halo4, carry):
    shape = (8, 128)
    total = prices[0] + prices[1] + prices[2] + prices[3] + prices[4] + bound
    from_front = jnp.where(subs(shape) == 0, halo3, pltpu.roll(prices[3], 1, 0))
    from_back = jnp.where(subs(shape) == 7, halo4, pltpu.roll(prices[4], 7, 0))
    lower = prices[0] + halo1 + halo2 + from_front + from_back
    g = total - up(lower)
    pair = g + swap(g)
    return carry + jnp.where(later_half(shape), g, pair), carry + pair


def unpack_kernel(got, planes, prices, halos, edges, bound, share, caps, limits, tail, masks):
    masks[...] = planes[...]
    deep = planes[0]
    for n, field in ((HALO1, LEFT), (HALO2, RIGHT)):
        tile = got[0, 2 * field]
        masks[n] = jnp.broadcast_to(tile[:, 0:1], (8, 128)) * deep
    for s in range(TILES):
        edges[0, 2 * s : 2 * s + 2] = got[s, EXTRA, 0:2] * masks[HALO3][0:2]
        edges[1, 2 * s : 2 * s + 2] = got[s, EXTRA, 2:4] * masks[HALO4][0:2]
        caps[2 * s : 2 * s + 2] = got[s, EXTRA, 4:6]
        limits[2 * s : 2 * s + 2] = got[s, EXTRA, 6:8]
    carry = jnp.zeros((8, 128), F32)
    for r in reversed(range(ROWS)):
        s, a = divmod(r, 2)
        p = [got[s, 2 * k + a] * masks[k] for k in range(ARCS)]
        for k in range(ARCS):
            prices[k, r] = p[k]
        b = got[s, 2 * BOUND + a]
        bound[r] = b
        share[r] = got[s, 2 * SHARE + a]
        h1 = got[s, 2 * LEFT + a] * masks[HALO1]
        h2 = got[s, 2 * RIGHT + a] * masks[HALO2]
        halos[0, r] = h1
        halos[1, r] = h2
        tail[r], carry = adjoint_row(
            p, b, h1, h2, edges[0, r : r + 1], edges[1, r : r + 1], carry
        )


def summed_row(got):
    total = got[0:8]
    for n in range(1, DEVICES // 8):
        total = total + got[8 * n : 8 * n + 8]
    return jnp.sum(total, axis=0, keepdims=True)


def lane_value(row, lane):
    return jnp.sum(jnp.where(lanes((1, 128)) == lane, row, 0.0), axis=1, keepdims=True)


def caps_after(row, caps, limits, weight):
    shape = (ROWS, 128)
    spread = jnp.where((lanes(shape) & 63) == subs(shape), jnp.broadcast_to(row, shape), 0.0)
    totals = half_sums(spread)
    tons_all = lane_value(row, LANE_TONS)
    return jnp.maximum(caps + weight * (totals - BLOCKS * limits) / tons_all, 0.0)


def weight_after(row, weight, mean, first):
    move_cap = jnp.sum(
        jnp.sum((mean - first) ** 2, axis=0, keepdims=True), axis=1, keepdims=True
    ) * (1.0 / 64.0)
    primal_move = lane_value(row, LANE_PRIMAL)
    dual_move = lane_value(row, LANE_DUAL) + move_cap
    return jnp.sqrt(weight * jnp.sqrt((dual_move + EPS) / (primal_move + EPS)))


def primal_step(caps, tail, share, planes, weight, new, head, first, last, row, cap_rows, rate_rows):
    shape = (8, 128)
    tons = planes[TONS]
    value = planes[VALUE]
    lean = tons / ROOT
    cap_rows[...] = caps
    periods = period_table()
    rate_rows[0] = jnp.exp(-RATE * periods)
    rate_rows[1] = SLOPE * (NP - periods)
    half = later_half(shape)
    carry = jnp.zeros(shape, F32)
    mined = []
    for r in range(ROWS):
        one = slice(r, r + 1)
        gradient = tail[r] + tons * cap_rows[one] / ROOT
        tau = 1.0 / (weight * (rate_rows[1, one] + lean))
        old = share[r]
        now = jnp.maximum(old - tau * (gradient - value * rate_rows[0, one]), 0.0)
        new[r] = now
        ahead = 2.0 * now - old
        pair = ahead + swap(ahead)
        cumulative = carry + jnp.where(half, pair, ahead)
        carry = carry + pair
        head[r] = cumulative
        first[one] = cumulative[0:1]
        last[one] = cumulative[7:8]
        mined.append(tons * ahead)
    mined.append(tons)
    sums = half_sums(jnp.concatenate(mined, axis=0))
    lane = lanes(shape)
    total = jnp.where(lane == LANE_TONS, sums[8 * ROWS :], 0.0)
    for r in range(ROWS):
        total = total + jnp.where((lane & 63) == r, sums[8 * r : 8 * r + 8], 0.0)
    row[...] = jnp.broadcast_to(jnp.sum(total, axis=0, keepdims=True), row.shape)


def primal_first_kernel(caps, tail, share, planes, weight, *rest):
    primal_step(caps[...], tail, share, planes, weight[...], *rest)


def primal_kernel(got, caps, limits, tail, share, planes, weight, caps_new, *rest):
    row = summed_row(got)
    caps_now = caps_after(row, caps[...], limits[...], weight[...])
    caps_new[...] = caps_now
    primal_step(caps_now, tail, share, planes, weight[...], *rest)


def restart(got, caps0, caps1, caps2, limits, weight):
    row = summed_row(got)
    caps3 = caps_after(row, caps2[...], limits[...], weight[...])
    mean = (caps1[...] + caps2[...] + caps3) / INNER
    return mean, weight_after(row, weight[...], mean, caps0[...])


def primal_restart_kernel(
    got, caps0, caps1, caps2, limits, tail, share, planes, weight, caps_new, weight_new, *rest
):
    mean, new = restart(got, caps0, caps1, caps2, limits, weight)
    caps_new[...] = mean
    weight_new[...] = new
    primal_step(mean, tail, share, planes, new, *rest)


def finish_kernel(got, caps0, caps1, caps2, limits, weight, caps_new, weight_new):
    mean, new = restart(got, caps0, caps1, caps2, limits, weight)
    caps_new[...] = mean
    weight_new[...] = new


def dual_rows(
    weight, planes, head, right, left, front, back, first, last, prices, halos, edges, bound, steps
):
    periods = period_table()
    steps[0] = weight[...] / (2.0 * (periods + 1.0))
    steps[1] = weight[...] / (periods + 1.0)
    fronts, backs = front[...], back[...]
    steps[2] = down(fronts)
    steps[3] = down(backs)
    wide = (ROWS, 128)
    edge0 = jnp.broadcast_to(planes[HALO3][0:1], wide) * jnp.maximum(
        edges[0] + steps[0] * (fronts - down(first[...])), 0.0
    )
    edge1 = jnp.broadcast_to(planes[HALO4][0:1], wide) * jnp.maximum(
        edges[1] + steps[0] * (backs - down(last[...])), 0.0
    )
    return edge0, edge1


def dual_row(r, planes, head, right, left, prices, halos, bound, steps):
    shape = (8, 128)
    one = slice(r, r + 1)
    step = steps[0, one]
    here = head[r]
    under = down(here)
    sub = subs(shape)
    ahead = [
        under,
        down(right[r]),
        down(left[r]),
        jnp.where(sub == 7, steps[3, one], pltpu.roll(under, 7, 0)),
        jnp.where(sub == 0, steps[2, one], pltpu.roll(under, 1, 0)),
    ]
    p = [
        jnp.maximum(prices[k, r] + step * (here - ahead[k]), 0.0) * planes[k] for k in range(ARCS)
    ]
    b = jnp.maximum(bound[r] + steps[1, one] * (here - 1.0), 0.0)
    h1 = jnp.maximum(halos[0, r] + step * (left[r] - under), 0.0) * planes[HALO1]
    h2 = jnp.maximum(halos[1, r] + step * (right[r] - under), 0.0) * planes[HALO2]
    return p, b, h1, h2


def dual_kernel(
    weight, planes, head, right, left, front, back, first, last, prices, halos, edges, bound,
    prices_new, halos_new, edges_new, bound_new, tail, steps,
):
    edge0, edge1 = dual_rows(
        weight, planes, head, right, left, front, back, first, last, prices, halos, edges, bound, steps
    )
    edges_new[0] = edge0
    edges_new[1] = edge1
    carry = jnp.zeros((8, 128), F32)
    for r in reversed(range(ROWS)):
        p, b, h1, h2 = dual_row(r, planes, head, right, left, prices, halos, bound, steps)
        for k in range(ARCS):
            prices_new[k, r] = p[k]
        bound_new[r] = b
        halos_new[0, r] = h1
        halos_new[1, r] = h2
        tail[r], carry = adjoint_row(
            p, b, h1, h2, edges_new[0, r : r + 1], edges_new[1, r : r + 1], carry
        )


def mean_of(one, two, three):
    return (one + two + three) / INNER


def put_moves(row, primal_move, dual_move, row_new):
    lane = lanes((1, 128))

    def whole(v):
        return jnp.sum(jnp.sum(v, axis=0, keepdims=True), axis=1, keepdims=True)

    old = row[0:1]
    new = old + jnp.where(lane == LANE_PRIMAL, whole(primal_move), 0.0)
    new = new + jnp.where(lane == LANE_DUAL, whole(dual_move), 0.0)
    row_new[...] = jnp.broadcast_to(new, row_new.shape)


def dual_restart_kernel(
    weight, planes, head, right, left, front, back, first, last, prices, halos, edges, bound,
    prices0, prices1, halos1, edges1, bound0, bound1, share0, share1, share2, share3, row,
    prices_new, halos_new, edges_new, bound_new, tail, share_new, row_new, steps,
):
    edge0, edge1 = dual_rows(
        weight, planes, head, right, left, front, back, first, last, prices, halos, edges, bound, steps
    )
    edges_new[0] = mean_of(edges1[0], edges[0], edge0)
    edges_new[1] = mean_of(edges1[1], edges[1], edge1)
    shape = (8, 128)
    carry = jnp.zeros(shape, F32)
    primal_move = jnp.zeros(shape, F32)
    dual_move = jnp.zeros(shape, F32)
    for r in reversed(range(ROWS)):
        p, b, h1, h2 = dual_row(r, planes, head, right, left, prices, halos, bound, steps)
        p = [mean_of(prices1[k, r], prices[k, r], p[k]) for k in range(ARCS)]
        b = mean_of(bound1[r], bound[r], b)
        h1 = mean_of(halos1[0, r], halos[0, r], h1)
        h2 = mean_of(halos1[1, r], halos[1, r], h2)
        u = mean_of(share1[r], share2[r], share3[r])
        primal_move = primal_move + (u - share0[r]) ** 2
        dual_move = dual_move + (b - bound0[r]) ** 2
        for k in range(ARCS):
            dual_move = dual_move + (p[k] - prices0[k, r]) ** 2
            prices_new[k, r] = p[k]
        bound_new[r] = b
        halos_new[0, r] = h1
        halos_new[1, r] = h2
        share_new[r] = u
        tail[r], carry = adjoint_row(
            p, b, h1, h2, edges_new[0, r : r + 1], edges_new[1, r : r + 1], carry
        )
    put_moves(row, primal_move, dual_move, row_new)


def dual_final_kernel(
    weight, planes, head, right, left, front, back, first, last, prices, halos, edges, bound,
    prices0, prices1, bound0, bound1, share0, share1, share2, share3, row,
    send, row_new, steps,
):
    dual_rows(
        weight, planes, head, right, left, front, back, first, last, prices, halos, edges, bound, steps
    )
    shape = (8, 128)
    primal_move = jnp.zeros(shape, F32)
    dual_move = jnp.zeros(shape, F32)
    for r in reversed(range(ROWS)):
        s, a = divmod(r, 2)
        p, b, _, _ = dual_row(r, planes, head, right, left, prices, halos, bound, steps)
        p = [mean_of(prices1[k, r], prices[k, r], p[k]) for k in range(ARCS)]
        b = mean_of(bound1[r], bound[r], b)
        u = mean_of(share1[r], share2[r], share3[r])
        primal_move = primal_move + (u - share0[r]) ** 2
        dual_move = dual_move + (b - bound0[r]) ** 2
        for k in range(ARCS):
            dual_move = dual_move + (p[k] - prices0[k, r]) ** 2
            send[s, 2 * k + a] = p[k]
        send[s, 2 * BOUND + a] = b
        send[s, 2 * SHARE + a] = u
    put_moves(row, primal_move, dual_move, row_new)


def turn_back_kernel(got, share, prec, bound):
    def take(field, target):
        for a in range(2):
            turned = got[:, 2 * field + a].reshape(128, 128).T
            target(2 * a, turned[0:64])
            target(2 * a + 1, turned[64:128])

    for k in range(ARCS):

        def store(t, v, k=k):
            prec[k, t] = v

        take(k, store)

    def store_bound(t, v):
        bound[t] = v

    def store_share(t, v):
        share[t] = v

    take(BOUND, store_bound)
    take(SHARE, store_share)


def f32(*shape):
    return jax.ShapeDtypeStruct(shape, F32)


VMEM = pl.BlockSpec(memory_space=pltpu.VMEM)
SMEM = pl.BlockSpec(memory_space=pltpu.SMEM)
FIELD = (ROWS, 8, 128)


def call(kernel, outs, scratch=(), scalars=0):
    def run(*args):
        specs = [SMEM] * scalars + [VMEM] * (len(args) - scalars)
        return pl.pallas_call(
            kernel,
            out_shape=[f32(*shape) for shape in outs],
            in_specs=specs,
            out_specs=[VMEM] * len(outs),
            scratch_shapes=[pltpu.VMEM(shape, F32) for shape in scratch],
            compiler_params=pltpu.CompilerParams(vmem_limit_bytes=32 * 1024 * 1024),
        )(*args)

    return run


STEP_OUTS = [FIELD, FIELD, (ROWS, 128), (ROWS, 128), (DEVICES, 128)]
STEP_SCRATCH = [(ROWS, 128), (2, ROWS, 128)]
DUAL_OUTS = [(ARCS,) + FIELD, (2,) + FIELD, (2, ROWS, 128), FIELD, FIELD]


def chain(by):
    return [(i, i + by) for i in range(16) if 0 <= i + by < 16]


def share_row(row):
    return lax.all_to_all(row, ("strip", "period"), 0, 0, tiled=True)


def halo(head, first, last):
    right = lax.ppermute(head, "strip", chain(-1))
    left = lax.ppermute(head, "strip", chain(1))
    back = lax.ppermute(first, "period", chain(-1))
    front = lax.ppermute(last, "period", chain(1))
    return right, left, front, back


def per_device(
    u_start,
    dual_prec,
    dual_bound,
    dual_cap,
    capacity,
    block_value,
    ton_class,
    density,
    slope_code,
    omega_start,
):
    x, tile = lax.axis_index("strip"), lax.axis_index("period")
    prec = dual_prec[:, 0]
    top = (jnp.arange(NZ) == 0)[None, :, None]
    toward = ((slope_code & 1) * (x + 1 < NX)).astype(F32)[None]
    away = ((slope_code // 2 & 1) * (x >= 1)).astype(F32)[None]
    left0 = lax.ppermute(jnp.where(top, toward, prec[1]), "strip", chain(1))
    right0 = lax.ppermute(jnp.where(top, away, prec[2]), "strip", chain(-1))
    place = jnp.stack([x, tile]).astype(jnp.int32)
    (planes,) = call(planes_kernel, [(PLANES, 8, 128)], [(128, 128)], 2)(
        place, density, slope_code, ton_class[0], block_value[0]
    )
    (send,) = call(pack_kernel, [(TILES, SLOTS, 8, 128)], (), 2)(
        dual_cap, capacity, u_start[0], prec, dual_bound[0], left0, right0
    )
    got = lax.all_to_all(send, "period", 0, 0)
    prices, halos, edges, bound, share, caps, limits, tail, planes = call(
        unpack_kernel,
        [
            (ARCS,) + FIELD,
            (2,) + FIELD,
            (2, ROWS, 128),
            FIELD,
            FIELD,
            (ROWS, 128),
            (ROWS, 128),
            FIELD,
            (PLANES, 8, 128),
        ],
    )(got, planes)
    weight = jnp.reshape(omega_start, (1, 1))
    row_sums = None
    old_caps = None
    for outer in range(OUTER):
        shares, caps_list = [share], []
        price_list, halo_list, edge_list, bound_list = [prices], [halos], [edges], [bound]
        for inner in range(INNER):
            if inner == 0 and outer == 0:
                new, head, first, last, row = call(primal_first_kernel, STEP_OUTS, STEP_SCRATCH)(
                    caps, tail, share, planes, weight
                )
            elif inner == 0:
                caps, weight, new, head, first, last, row = call(
                    primal_restart_kernel, [(ROWS, 128), (1, 1)] + STEP_OUTS, STEP_SCRATCH
                )(row_sums, *old_caps, limits, tail, share, planes, weight)
            else:
                caps, new, head, first, last, row = call(
                    primal_kernel, [(ROWS, 128)] + STEP_OUTS, STEP_SCRATCH
                )(row_sums, caps, limits, tail, share, planes, weight)
            caps_list.append(caps)
            shares.append(new)
            share = new
            right, left, front, back = halo(head, first, last)
            common = (
                weight, planes, head, right, left, front, back, first, last,
                prices, halos, edges, bound,
            )
            steps = [(4, ROWS, 128)]
            if inner < INNER - 1:
                row_sums = share_row(row)
                prices, halos, edges, bound, tail = call(dual_kernel, DUAL_OUTS, steps)(*common)
                price_list.append(prices)
                halo_list.append(halos)
                edge_list.append(edges)
                bound_list.append(bound)
            elif outer < OUTER - 1:
                prices, halos, edges, bound, tail, share, row = call(
                    dual_restart_kernel, DUAL_OUTS + [FIELD, (DEVICES, 128)], steps
                )(
                    *common, price_list[0], price_list[1], halo_list[1], edge_list[1],
                    bound_list[0], bound_list[1], *shares, row,
                )
                row_sums = share_row(row)
                old_caps = caps_list
            else:
                send, row = call(
                    dual_final_kernel, [(TILES, 14, 8, 128), (DEVICES, 128)], steps
                )(
                    *common, price_list[0], price_list[1], bound_list[0], bound_list[1],
                    *shares, row,
                )
                got = lax.all_to_all(send, "period", 0, 0)
                row_sums = share_row(row)
                old_caps = caps_list
    mined, arcs, bounds = call(
        turn_back_kernel, [(4, NZ, NY), (ARCS, 4, NZ, NY), (4, NZ, NY)]
    )(got)
    caps, weight = call(finish_kernel, [(ROWS, 128), (1, 1)])(
        row_sums, *old_caps, limits, weight
    )
    own = lax.dynamic_slice(caps, (2 * tile, 0), (2, 128))[:, ::64]
    return (
        mined[None],
        arcs[:, None],
        bounds[None],
        jnp.reshape(own, (4,)),
        jnp.reshape(weight, (1,)),
    )


def solution(mesh):
    in_specs = (
        P("strip", "period", None, None),
        P(None, "strip", "period", None, None),
        P("strip", "period", None, None),
        P("period"),
        P("period"),
        P("strip", None, None),
        P("strip", None, None),
        P(),
        P("strip", None),
        P(),
    )
    out_specs = (
        P("strip", "period", None, None),
        P(None, "strip", "period", None, None),
        P("strip", "period", None, None),
        P("period"),
        P(),
    )
    return jax.shard_map(
        per_device, mesh=mesh, in_specs=in_specs, out_specs=out_specs, check_vma=False
    )
```

time: 867 us -> 305 us (0.35)
  blocking collectives: 656 us -> 63.5 us
  other arithmetic: 102 us -> 1.81 us
  starting transfers between devices: 64.7 us -> 133 us
  waiting for transfers between devices: 12.8 us -> 63.3 us
  Pallas kernels: 0 us -> 19.6 us
  local copies, waits for them, and re-layouts: 5.77 us -> 20.2 us
    psum x8 -> x0, blocking collectives: 331 us -> none  [the longest x6 167 us: capacity_sum(): return lax.psum(row_local, 'strip')]
    all_gather x12 -> x0, blocking collectives: 325 us -> none  [carried_in(): everything = lax.all_gather(value, axis)]
    select_n x192 -> x1, other arithmetic: 74.5 us -> 1.05 us  [per_device(): right0 = lax.ppermute(jnp.where(top, away, prec[2]), 'strip', chain(-1))]
    all_to_all x0 -> x2, blocking collectives: none -> 63.5 us  [share_row(): return lax.all_to_all(row, ('strip', 'period'), 0, 0, tiled=True)]
    all_to_all x0 -> x6, starting transfers between devices: none -> 62.4 us  [the longest x4 50 us: share_row(): return lax.all_to_all(row, ('strip', 'period'), 0, 0, tiled=True)]
    all_to_all x0 -> x6, waiting for transfers between devices: none -> 31.6 us  [the longest x2 31.6 us: per_device(): got = lax.all_to_all(send, 'period', 0, 0)]
    pallas_call x0 -> x17, Pallas kernels: none -> 19.6 us  [run(): pl.pallas_call(kernel, out_shape=[f32(*shape) for shape in outs], in_spec...]
    ppermute x24 -> x26, waiting for transfers between devices: 12.8 us -> 31.7 us  [the longest x6 28 us: halo(): back = lax.ppermute(first, 'period', chain(-1))]
  transfers between devices with their start and end apart: 24 -> 32, of which waited for: 9 -> 10; matrix products, arithmetic and copies ran while one was open for 2% -> 0% of each run, Pallas kernels for 0% -> 2%
where the time goes in v1:
time: 305 us; the launch traced here: 303 us
  starting transfers between devices  133 us (44%)
  blocking collectives  63.5 us (21%)
  waiting for transfers between devices  63.3 us (21%)
  local copies, waits for them, and re-layouts  20.2 us (7%)
  Pallas kernels  19.6 us (6%)
    all_to_all x2, blocking collectives, share_row(): return lax.all_to_all(row, ('strip', 'period'), 0, 0, tiled=True)  63.5 us
    all_to_all x4, starting transfers between devices, share_row(): return lax.all_to_all(row, ('strip', 'period'), 0, 0, tiled=True)  50 us
    all_to_all x2, waiting for transfers between devices, per_device(): got = lax.all_to_all(send, 'period', 0, 0)  31.6 us
    ppermute x6, waiting for transfers between devices, halo(): back = lax.ppermute(first, 'period', chain(-1))  28 us
    ppermute x6, starting transfers between devices, halo(): front = lax.ppermute(last, 'period', chain(1))  25 us
    ppermute x6, starting transfers between devices, halo(): left = lax.ppermute(head, 'strip', chain(1))  20.5 us
    pallas_call x17, Pallas kernels, run(): pl.pallas_call(kernel, out_shape=[f32(*shape) for shape in outs], in_spec...  19.6 us
    unnamed x82, local copies, waits for them, and re-layouts  19.5 us
  transfers between devices with their start and end apart: 32, of which 10 were waited for; matrix products, arithmetic and copies ran while one was open for 0% of the time, Pallas kernels for 2%

profile of v1, /device:TPU:1, one launch (start us, length us, event | category | flops | bytes accessed | tf_op | source)
XLA Modules:
  0.0 303.5 jit_solution(8195462503354553512)
XLA Ops:
  3.7 4.6 %collective-permute-start = (f32[4,64,128]{2,1,0:T(8,128)S(1)}, f32[4,64,128]{2,1,0:T(8,128)S(1)}, u32[]{:S(2)}, u32[]{:S(2)}) collective-permute-start(f32[4,64,128]{2,1,0:T(8,128)S(1)} %get-tuple-element.174), channel_id=1, source_target_pairs={{0,16},{16,32},{32,48},{48,64},{64,80},{80,96},{96,112},{112,128},... | collective-permute-start | bytes 393224 | tf_op jit(solution)/shard_map/ppermute | solution.py:509
  18.1 8.6 %all-to-all-start = ((f32[16,19,8,128]{3,2,1,0:T(8,128)}), f32[16,19,8,128]{3,2,1,0:T(8,128)S(1)}, u32[]{:S(2)}, u32[]{:S(2)}) async-start(f32[16,19,8,128]{3,2,1,0:T(8,128)} %shard_map.137), calls=%async_computation | async-start | bytes 2490368 | tf_op jit(solution)/shard_map/all_to_all | solution.py:518
  28.2 17.9 %all-to-all-done.got = f32[16,19,8,128]{3,2,1,0:T(8,128)S(1)} async-done(((f32[16,19,8,128]{3,2,1,0:T(8,128)}), f32[16,19,8,128]{3,2,1,0:T(8,128)S(1)}, u32[]{:S(2)}, u32[]{:S(2)}) %all-to-all-start) | async-done | bytes 1245216 | tf_op jit(solution)/shard_map/all_to_all | solution.py:518
  48.2 12.5 %all-to-all-start.1 = ((f32[256,1,128]{2,1,0:T(1,128)}), f32[256,1,128]{2,1,0:T(1,128)S(1)}, u32[]{:S(2)}, u32[]{:S(2)}) async-start(f32[256,1,128]{2,1,0:T(1,128)} %bitcast.13), calls=%async_computation.1 | async-start | bytes 262144 | tf_op jit(solution)/shard_map/all_to_all | solution.py:481
  65.2 4.8 %collective-permute-start.4 = (f32[32,128]{1,0:T(8,128)S(1)}, f32[32,128]{1,0:T(8,128)S(1)}, u32[]{:S(2)}, u32[]{:S(2)}) collective-permute-start(f32[32,128]{1,0:T(8,128)S(1)} %get-tuple-element.91.last), channel_id=1, source_target_pairs={{0,1},{1,2},{2,3},{3,4},{4,5},{5,6},{6,7},{7,8},{8,9},{9,10},{10,1... | collective-permute-start | bytes 49160 | tf_op jit(solution)/shard_map/ppermute | solution.py:488
  72.0 4.6 %collective-permute-done.5.back = f32[32,128]{1,0:T(8,128)S(1)} collective-permute-done((f32[32,128]{1,0:T(8,128)S(1)}, f32[32,128]{1,0:T(8,128)S(1)}, u32[]{:S(2)}, u32[]{:S(2)}) %collective-permute-start.5) | collective-permute-done | bytes 16416 | tf_op jit(solution)/shard_map/ppermute | solution.py:487
  78.6 16.0 %all-to-all-start.2 = ((f32[256,1,128]{2,1,0:T(1,128)}), f32[256,1,128]{2,1,0:T(1,128)S(1)}, u32[]{:S(2)}, u32[]{:S(2)}) async-start(f32[256,1,128]{2,1,0:T(1,128)} %bitcast.16), calls=%async_computation.2 | async-start | bytes 262144 | tf_op jit(solution)/shard_map/all_to_all | solution.py:481
  99.1 4.8 %collective-permute-start.8 = (f32[32,128]{1,0:T(8,128)S(1)}, f32[32,128]{1,0:T(8,128)S(1)}, u32[]{:S(2)}, u32[]{:S(2)}) collective-permute-start(f32[32,128]{1,0:T(8,128)S(1)} %get-tuple-element.102.last), channel_id=1, source_target_pairs={{0,1},{1,2},{2,3},{3,4},{4,5},{5,6},{6,7},{7,8},{8,9},{9,10},{10,1... | collective-permute-start | bytes 49160 | tf_op jit(solution)/shard_map/ppermute | solution.py:488
  105.9 4.6 %collective-permute-done.9.back = f32[32,128]{1,0:T(8,128)S(1)} collective-permute-done((f32[32,128]{1,0:T(8,128)S(1)}, f32[32,128]{1,0:T(8,128)S(1)}, u32[]{:S(2)}, u32[]{:S(2)}) %collective-permute-start.9) | collective-permute-done | bytes 16416 | tf_op jit(solution)/shard_map/ppermute | solution.py:487
  115.4 3.7 %collective-permute-start.11 = (f32[32,8,128]{2,1,0:T(8,128)S(1)}, f32[32,8,128]{2,1,0:T(8,128)S(1)}, u32[]{:S(2)}, u32[]{:S(2)}) collective-permute-start(f32[32,8,128]{2,1,0:T(8,128)S(1)} %get-tuple-element.110.head), channel_id=1, source_target_pairs={{0,16},{16,32},{32,48},{48,64},{64,80},{80,96},{96,112},{112,128},... | collective-permute-start | bytes 393224 | tf_op jit(solution)/shard_map/ppermute | solution.py:486
  125.1 4.8 %collective-permute-done.13.back = f32[32,128]{1,0:T(8,128)S(1)} collective-permute-done((f32[32,128]{1,0:T(8,128)S(1)}, f32[32,128]{1,0:T(8,128)S(1)}, u32[]{:S(2)}, u32[]{:S(2)}) %collective-permute-start.13) | collective-permute-done | bytes 16416 | tf_op jit(solution)/shard_map/ppermute | solution.py:487
  136.1 31.7 %all_to_all.76 = f32[256,1,128]{2,1,0:T(1,128)S(1)} all-to-all(f32[256,1,128]{2,1,0:T(1,128)S(1)} %bitcast.62), channel_id=1, replica_groups=mesh['strip'=16,'period'=16] {'strip','period'}, dimensions={0} | all-to-all | bytes 262144 | tf_op jit(solution)/shard_map/all_to_all | solution.py:481
  169.4 5.4 %all-to-all-start.4 = ((f32[256,1,128]{2,1,0:T(1,128)}), f32[256,1,128]{2,1,0:T(1,128)S(1)}, u32[]{:S(2)}, u32[]{:S(2)}) async-start(f32[256,1,128]{2,1,0:T(1,128)} %bitcast.22), calls=%async_computation.4 | async-start | bytes 262144 | tf_op jit(solution)/shard_map/all_to_all | solution.py:481
  174.9 3.3 %collective-permute-start.15 = (f32[32,8,128]{2,1,0:T(8,128)S(1)}, f32[32,8,128]{2,1,0:T(8,128)S(1)}, u32[]{:S(2)}, u32[]{:S(2)}) collective-permute-start(f32[32,8,128]{2,1,0:T(8,128)S(1)} %get-tuple-element.126.head), channel_id=1, source_target_pairs={{0,16},{16,32},{32,48},{48,64},{64,80},{80,96},{96,112},{112,128},... | collective-permute-start | bytes 393224 | tf_op jit(solution)/shard_map/ppermute | solution.py:486
  179.5 4.9 %collective-permute-start.16 = (f32[32,128]{1,0:T(8,128)S(1)}, f32[32,128]{1,0:T(8,128)S(1)}, u32[]{:S(2)}, u32[]{:S(2)}) collective-permute-start(f32[32,128]{1,0:T(8,128)S(1)} %get-tuple-element.127.last), channel_id=1, source_target_pairs={{0,1},{1,2},{2,3},{3,4},{4,5},{5,6},{6,7},{7,8},{8,9},{9,10},{10,1... | collective-permute-start | bytes 49160 | tf_op jit(solution)/shard_map/ppermute | solution.py:488
  186.5 4.4 %collective-permute-done.17.back = f32[32,128]{1,0:T(8,128)S(1)} collective-permute-done((f32[32,128]{1,0:T(8,128)S(1)}, f32[32,128]{1,0:T(8,128)S(1)}, u32[]{:S(2)}, u32[]{:S(2)}) %collective-permute-start.17) | collective-permute-done | bytes 16416 | tf_op jit(solution)/shard_map/ppermute | solution.py:487
  195.8 16.1 %all-to-all-start.5 = ((f32[256,1,128]{2,1,0:T(1,128)}), f32[256,1,128]{2,1,0:T(1,128)S(1)}, u32[]{:S(2)}, u32[]{:S(2)}) async-start(f32[256,1,128]{2,1,0:T(1,128)} %bitcast.25), calls=%async_computation.5 | async-start | bytes 262144 | tf_op jit(solution)/shard_map/all_to_all | solution.py:481
  216.4 4.8 %collective-permute-start.20 = (f32[32,128]{1,0:T(8,128)S(1)}, f32[32,128]{1,0:T(8,128)S(1)}, u32[]{:S(2)}, u32[]{:S(2)}) collective-permute-start(f32[32,128]{1,0:T(8,128)S(1)} %get-tuple-element.138.last), channel_id=1, source_target_pairs={{0,1},{1,2},{2,3},{3,4},{4,5},{5,6},{6,7},{7,8},{8,9},{9,10},{10,1... | collective-permute-start | bytes 49160 | tf_op jit(solution)/shard_map/ppermute | solution.py:488
  223.2 4.6 %collective-permute-done.21.back = f32[32,128]{1,0:T(8,128)S(1)} collective-permute-done((f32[32,128]{1,0:T(8,128)S(1)}, f32[32,128]{1,0:T(8,128)S(1)}, u32[]{:S(2)}, u32[]{:S(2)}) %collective-permute-start.21) | collective-permute-done | bytes 16416 | tf_op jit(solution)/shard_map/ppermute | solution.py:487
  234.3 3.7 %collective-permute-start.23 = (f32[32,8,128]{2,1,0:T(8,128)S(1)}, f32[32,8,128]{2,1,0:T(8,128)S(1)}, u32[]{:S(2)}, u32[]{:S(2)}) collective-permute-start(f32[32,8,128]{2,1,0:T(8,128)S(1)} %get-tuple-element.146.head), channel_id=1, source_target_pairs={{0,16},{16,32},{32,48},{48,64},{64,80},{80,96},{96,112},{112,128},... | collective-permute-start | bytes 393224 | tf_op jit(solution)/shard_map/ppermute | solution.py:486
  244.0 4.8 %collective-permute-done.25.back = f32[32,128]{1,0:T(8,128)S(1)} collective-permute-done((f32[32,128]{1,0:T(8,128)S(1)}, f32[32,128]{1,0:T(8,128)S(1)}, u32[]{:S(2)}, u32[]{:S(2)}) %collective-permute-start.25) | collective-permute-done | bytes 16416 | tf_op jit(solution)/shard_map/ppermute | solution.py:487
  250.8 31.7 %all_to_all.77 = f32[256,1,128]{2,1,0:T(1,128)S(1)} all-to-all(f32[256,1,128]{2,1,0:T(1,128)S(1)} %bitcast.63), channel_id=1, replica_groups=mesh['strip'=16,'period'=16] {'strip','period'}, dimensions={0} | all-to-all | bytes 262144 | tf_op jit(solution)/shard_map/all_to_all | solution.py:481
  282.6 3.8 %all-to-all-start.6 = ((f32[16,14,8,128]{3,2,1,0:T(8,128)}), f32[16,14,8,128]{3,2,1,0:T(8,128)S(1)}, u32[]{:S(2)}, u32[]{:S(2)}) async-start(f32[16,14,8,128]{3,2,1,0:T(8,128)} %get-tuple-element.155), calls=%async_computation.6 | async-start | bytes 1835008 | tf_op jit(solution)/shard_map/all_to_all | solution.py:584
  288.6 13.7 %all-to-all-done.6.got = f32[16,14,8,128]{3,2,1,0:T(8,128)S(1)} async-done(((f32[16,14,8,128]{3,2,1,0:T(8,128)}), f32[16,14,8,128]{3,2,1,0:T(8,128)S(1)}, u32[]{:S(2)}, u32[]{:S(2)}) %all-to-all-start.6) | async-done | bytes 917536 | tf_op jit(solution)/shard_map/all_to_all | solution.py:584
  (148 shorter events, 81.5 us)
Async XLA Ops:
  3.7 8.3 %collective-permute-start = (f32[4,64,128]{2,1,0:T(8,128)S(1)}, f32[4,64,128]{2,1,0:T(8,128)S(1)}, u32[]{:S(2)}, u32[]{:S(2)}) collective-permute-start(f32[4,64,128]{2,1,0:T(8,128)S(1)} %get-tuple-element.174), channel_id=1, source_target_pairs={{0,16},{16,32},{32,48},{48,64},{64,80},{80,96},{96,112},{112,128},... | collective-permute-start | bytes 393224 | tf_op jit(solution)/shard_map/ppermute | solution.py:509
  18.1 27.9 %all-to-all-start = ((f32[16,19,8,128]{3,2,1,0:T(8,128)}), f32[16,19,8,128]{3,2,1,0:T(8,128)S(1)}, u32[]{:S(2)}, u32[]{:S(2)}) async-start(f32[16,19,8,128]{3,2,1,0:T(8,128)} %shard_map.137), calls=%async_computation | async-start | bytes 2490368 | tf_op jit(solution)/shard_map/all_to_all | solution.py:518
  48.2 29.0 %all-to-all-start.1 = ((f32[256,1,128]{2,1,0:T(1,128)}), f32[256,1,128]{2,1,0:T(1,128)S(1)}, u32[]{:S(2)}, u32[]{:S(2)}) async-start(f32[256,1,128]{2,1,0:T(1,128)} %bitcast.13), calls=%async_computation.1 | async-start | bytes 262144 | tf_op jit(solution)/shard_map/all_to_all | solution.py:481
  60.6 16.0 %collective-permute-start.3 = (f32[32,8,128]{2,1,0:T(8,128)S(1)}, f32[32,8,128]{2,1,0:T(8,128)S(1)}, u32[]{:S(2)}, u32[]{:S(2)}) collective-permute-start(f32[32,8,128]{2,1,0:T(8,128)S(1)} %get-tuple-element.90.head), channel_id=1, source_target_pairs={{0,16},{16,32},{32,48},{48,64},{64,80},{80,96},{96,112},{112,128},... | collective-permute-start | bytes 393224 | tf_op jit(solution)/shard_map/ppermute | solution.py:486
  63.9 12.7 %collective-permute-start.2 = (f32[32,8,128]{2,1,0:T(8,128)S(1)}, f32[32,8,128]{2,1,0:T(8,128)S(1)}, u32[]{:S(2)}, u32[]{:S(2)}) collective-permute-start(f32[32,8,128]{2,1,0:T(8,128)S(1)} %get-tuple-element.90.head), channel_id=1, source_target_pairs={{16,0},{32,16},{48,32},{64,48},{80,64},{96,80},{112,96},{128,112},... | collective-permute-start | bytes 393224 | tf_op jit(solution)/shard_map/ppermute | solution.py:485
  65.2 6.8 %collective-permute-start.4 = (f32[32,128]{1,0:T(8,128)S(1)}, f32[32,128]{1,0:T(8,128)S(1)}, u32[]{:S(2)}, u32[]{:S(2)}) collective-permute-start(f32[32,128]{1,0:T(8,128)S(1)} %get-tuple-element.91.last), channel_id=1, source_target_pairs={{0,1},{1,2},{2,3},{3,4},{4,5},{5,6},{6,7},{7,8},{8,9},{9,10},{10,1... | collective-permute-start | bytes 49160 | tf_op jit(solution)/shard_map/ppermute | solution.py:488
  78.6 35.1 %all-to-all-start.2 = ((f32[256,1,128]{2,1,0:T(1,128)}), f32[256,1,128]{2,1,0:T(1,128)S(1)}, u32[]{:S(2)}, u32[]{:S(2)}) async-start(f32[256,1,128]{2,1,0:T(1,128)} %bitcast.16), calls=%async_computation.2 | async-start | bytes 262144 | tf_op jit(solution)/shard_map/all_to_all | solution.py:481
  94.5 16.0 %collective-permute-start.7 = (f32[32,8,128]{2,1,0:T(8,128)S(1)}, f32[32,8,128]{2,1,0:T(8,128)S(1)}, u32[]{:S(2)}, u32[]{:S(2)}) collective-permute-start(f32[32,8,128]{2,1,0:T(8,128)S(1)} %get-tuple-element.101.head), channel_id=1, source_target_pairs={{0,16},{16,32},{32,48},{48,64},{64,80},{80,96},{96,112},{112,128},... | collective-permute-start | bytes 393224 | tf_op jit(solution)/shard_map/ppermute | solution.py:486
  97.8 12.7 %collective-permute-start.6 = (f32[32,8,128]{2,1,0:T(8,128)S(1)}, f32[32,8,128]{2,1,0:T(8,128)S(1)}, u32[]{:S(2)}, u32[]{:S(2)}) collective-permute-start(f32[32,8,128]{2,1,0:T(8,128)S(1)} %get-tuple-element.101.head), channel_id=1, source_target_pairs={{16,0},{32,16},{48,32},{64,48},{80,64},{96,80},{112,96},{128,112},... | collective-permute-start | bytes 393224 | tf_op jit(solution)/shard_map/ppermute | solution.py:485
  99.1 6.8 %collective-permute-start.8 = (f32[32,128]{1,0:T(8,128)S(1)}, f32[32,128]{1,0:T(8,128)S(1)}, u32[]{:S(2)}, u32[]{:S(2)}) collective-permute-start(f32[32,128]{1,0:T(8,128)S(1)} %get-tuple-element.102.last), channel_id=1, source_target_pairs={{0,1},{1,2},{2,3},{3,4},{4,5},{5,6},{6,7},{7,8},{8,9},{9,10},{10,1... | collective-permute-start | bytes 49160 | tf_op jit(solution)/shard_map/ppermute | solution.py:488
  115.4 14.6 %collective-permute-start.11 = (f32[32,8,128]{2,1,0:T(8,128)S(1)}, f32[32,8,128]{2,1,0:T(8,128)S(1)}, u32[]{:S(2)}, u32[]{:S(2)}) collective-permute-start(f32[32,8,128]{2,1,0:T(8,128)S(1)} %get-tuple-element.110.head), channel_id=1, source_target_pairs={{0,16},{16,32},{32,48},{48,64},{64,80},{80,96},{96,112},{112,128},... | collective-permute-start | bytes 393224 | tf_op jit(solution)/shard_map/ppermute | solution.py:486
  119.1 10.9 %collective-permute-start.10 = (f32[32,8,128]{2,1,0:T(8,128)S(1)}, f32[32,8,128]{2,1,0:T(8,128)S(1)}, u32[]{:S(2)}, u32[]{:S(2)}) collective-permute-start(f32[32,8,128]{2,1,0:T(8,128)S(1)} %get-tuple-element.110.head), channel_id=1, source_target_pairs={{16,0},{32,16},{48,32},{64,48},{80,64},{96,80},{112,96},{128,112},... | collective-permute-start | bytes 393224 | tf_op jit(solution)/shard_map/ppermute | solution.py:485
  123.2 6.8 %collective-permute-start.13 = (f32[32,128]{1,0:T(8,128)S(1)}, f32[32,128]{1,0:T(8,128)S(1)}, u32[]{:S(2)}, u32[]{:S(2)}) collective-permute-start(f32[32,128]{1,0:T(8,128)S(1)} %get-tuple-element.112.first), channel_id=1, source_target_pairs={{1,0},{2,1},{3,2},{4,3},{5,4},{6,5},{7,6},{8,7},{9,8},{10,9},{11,1... | collective-permute-start | bytes 49160 | tf_op jit(solution)/shard_map/ppermute | solution.py:487
  169.4 24.3 %all-to-all-start.4 = ((f32[256,1,128]{2,1,0:T(1,128)}), f32[256,1,128]{2,1,0:T(1,128)S(1)}, u32[]{:S(2)}, u32[]{:S(2)}) async-start(f32[256,1,128]{2,1,0:T(1,128)} %bitcast.22), calls=%async_computation.4 | async-start | bytes 262144 | tf_op jit(solution)/shard_map/all_to_all | solution.py:481
  174.9 16.0 %collective-permute-start.15 = (f32[32,8,128]{2,1,0:T(8,128)S(1)}, f32[32,8,128]{2,1,0:T(8,128)S(1)}, u32[]{:S(2)}, u32[]{:S(2)}) collective-permute-start(f32[32,8,128]{2,1,0:T(8,128)S(1)} %get-tuple-element.126.head), channel_id=1, source_target_pairs={{0,16},{16,32},{32,48},{48,64},{64,80},{80,96},{96,112},{112,128},... | collective-permute-start | bytes 393224 | tf_op jit(solution)/shard_map/ppermute | solution.py:486
  178.2 12.7 %collective-permute-start.14 = (f32[32,8,128]{2,1,0:T(8,128)S(1)}, f32[32,8,128]{2,1,0:T(8,128)S(1)}, u32[]{:S(2)}, u32[]{:S(2)}) collective-permute-start(f32[32,8,128]{2,1,0:T(8,128)S(1)} %get-tuple-element.126.head), channel_id=1, source_target_pairs={{16,0},{32,16},{48,32},{64,48},{80,64},{96,80},{112,96},{128,112},... | collective-permute-start | bytes 393224 | tf_op jit(solution)/shard_map/ppermute | solution.py:485
  179.5 7.0 %collective-permute-start.16 = (f32[32,128]{1,0:T(8,128)S(1)}, f32[32,128]{1,0:T(8,128)S(1)}, u32[]{:S(2)}, u32[]{:S(2)}) collective-permute-start(f32[32,128]{1,0:T(8,128)S(1)} %get-tuple-element.127.last), channel_id=1, source_target_pairs={{0,1},{1,2},{2,3},{3,4},{4,5},{5,6},{6,7},{7,8},{8,9},{9,10},{10,1... | collective-permute-start | bytes 49160 | tf_op jit(solution)/shard_map/ppermute | solution.py:488
  195.8 36.3 %all-to-all-start.5 = ((f32[256,1,128]{2,1,0:T(1,128)}), f32[256,1,128]{2,1,0:T(1,128)S(1)}, u32[]{:S(2)}, u32[]{:S(2)}) async-start(f32[256,1,128]{2,1,0:T(1,128)} %bitcast.25), calls=%async_computation.5 | async-start | bytes 262144 | tf_op jit(solution)/shard_map/all_to_all | solution.py:481
  211.8 16.0 %collective-permute-start.19 = (f32[32,8,128]{2,1,0:T(8,128)S(1)}, f32[32,8,128]{2,1,0:T(8,128)S(1)}, u32[]{:S(2)}, u32[]{:S(2)}) collective-permute-start(f32[32,8,128]{2,1,0:T(8,128)S(1)} %get-tuple-element.137.head), channel_id=1, source_target_pairs={{0,16},{16,32},{32,48},{48,64},{64,80},{80,96},{96,112},{112,128},... | collective-permute-start | bytes 393224 | tf_op jit(solution)/shard_map/ppermute | solution.py:486
  215.1 12.7 %collective-permute-start.18 = (f32[32,8,128]{2,1,0:T(8,128)S(1)}, f32[32,8,128]{2,1,0:T(8,128)S(1)}, u32[]{:S(2)}, u32[]{:S(2)}) collective-permute-start(f32[32,8,128]{2,1,0:T(8,128)S(1)} %get-tuple-element.137.head), channel_id=1, source_target_pairs={{16,0},{32,16},{48,32},{64,48},{80,64},{96,80},{112,96},{128,112},... | collective-permute-start | bytes 393224 | tf_op jit(solution)/shard_map/ppermute | solution.py:485
  234.3 14.6 %collective-permute-start.23 = (f32[32,8,128]{2,1,0:T(8,128)S(1)}, f32[32,8,128]{2,1,0:T(8,128)S(1)}, u32[]{:S(2)}, u32[]{:S(2)}) collective-permute-start(f32[32,8,128]{2,1,0:T(8,128)S(1)} %get-tuple-element.146.head), channel_id=1, source_target_pairs={{0,16},{16,32},{32,48},{48,64},{64,80},{80,96},{96,112},{112,128},... | collective-permute-start | bytes 393224 | tf_op jit(solution)/shard_map/ppermute | solution.py:486
  237.9 10.9 %collective-permute-start.22 = (f32[32,8,128]{2,1,0:T(8,128)S(1)}, f32[32,8,128]{2,1,0:T(8,128)S(1)}, u32[]{:S(2)}, u32[]{:S(2)}) collective-permute-start(f32[32,8,128]{2,1,0:T(8,128)S(1)} %get-tuple-element.146.head), channel_id=1, source_target_pairs={{16,0},{32,16},{48,32},{64,48},{80,64},{96,80},{112,96},{128,112},... | collective-permute-start | bytes 393224 | tf_op jit(solution)/shard_map/ppermute | solution.py:485
  242.1 6.8 %collective-permute-start.25 = (f32[32,128]{1,0:T(8,128)S(1)}, f32[32,128]{1,0:T(8,128)S(1)}, u32[]{:S(2)}, u32[]{:S(2)}) collective-permute-start(f32[32,128]{1,0:T(8,128)S(1)} %get-tuple-element.148.first), channel_id=1, source_target_pairs={{1,0},{2,1},{3,2},{4,3},{5,4},{6,5},{7,6},{8,7},{9,8},{10,9},{11,1... | collective-permute-start | bytes 49160 | tf_op jit(solution)/shard_map/ppermute | solution.py:487
  282.6 19.7 %all-to-all-start.6 = ((f32[16,14,8,128]{3,2,1,0:T(8,128)}), f32[16,14,8,128]{3,2,1,0:T(8,128)S(1)}, u32[]{:S(2)}, u32[]{:S(2)}) async-start(f32[16,14,8,128]{3,2,1,0:T(8,128)} %get-tuple-element.155), calls=%async_computation.6 | async-start | bytes 1835008 | tf_op jit(solution)/shard_map/all_to_all | solution.py:584
  (49 other events, 574.1 us)

commit v2 on v1

v2 whole, which is shorter than its diff:
```python
import math

import jax
import jax.numpy as jnp
from jax import lax
from jax.experimental import pallas as pl
from jax.experimental.pallas import tpu as pltpu
from jax.sharding import PartitionSpec as P

OUTER = 2
INNER = 3
NX = 16
NY = 128
NZ = 64
NP = 64
RATE = math.log(1.1) / 12.0
EPS = 1e-06
SLOPE = 11.0
BLOCKS = float(NX * NY * NZ)
ROOT = math.sqrt(BLOCKS)
F32 = jnp.float32

PLANE = 32
TILES = 32
ROWS = NP // 2
DEVICES = 256
ARCS = 5
BOUND, SHARE, RIM, EXTRA, BLOCK = 5, 6, 7, 8, 9
SLOTS = 10
LANE_PRIMAL, LANE_DUAL, LANE_TONS = 40, 41, 42
HALO, EDGES, TONS, VALUE = 5, 6, 7, 8
PLANES = 9


def member(tile):
    chip, core = divmod(tile, 2)
    row, at = divmod(chip, 4)
    at = at if row % 2 == 0 else 3 - at
    return row % 2 * 16 + at * 4 + row // 2 * 2 + core


def lanes(shape):
    return lax.broadcasted_iota(jnp.int32, shape, len(shape) - 1)


def subs(shape):
    return lax.broadcasted_iota(jnp.int32, shape, len(shape) - 2)


def later_half(shape):
    return lanes(shape) >= 64


def half_matrix():
    a = subs((128, 128)) >= 64
    b = lanes((128, 128)) >= 64
    return (a == b).astype(F32)


def half_sums(rows):
    return jnp.dot(
        rows, half_matrix(), precision=lax.Precision.HIGHEST, preferred_element_type=F32
    )


def period_table():
    shape = (ROWS, 128)
    return (2 * subs(shape) + later_half(shape).astype(jnp.int32)).astype(F32)


def down(v):
    return pltpu.roll(v, 1, v.ndim - 1)


def up(v):
    return pltpu.roll(v, 127, v.ndim - 1)


def swap(v):
    return pltpu.roll(v, 64, v.ndim - 1)


def low(shape=(8, 128)):
    return subs(shape) < 4


def turn(v):
    return pltpu.roll(v, 4, v.ndim - 2)


def mix(one, two):
    return jnp.where(low(), one, turn(two)), jnp.where(low(), turn(one), two)


def pack_kernel(place, caps, limits, density, slope, ton_class, value, share, prec, bound, rim, out):
    x = place[0]
    row = (1, 128)
    code = slope[...]
    column = lanes(row)
    mask = [
        jnp.ones(row, F32),
        ((code & 1 == 1) & (jnp.full(row, x) + 1 < NX)).astype(F32),
        ((code >> 1 & 1 == 1) & (jnp.full(row, x) >= 1)).astype(F32),
        ((code >> 2 & 1 == 1) & (column + 1 < NY)).astype(F32),
        ((code >> 3 & 1 == 1) & (column >= 1)).astype(F32),
    ]
    top = subs((NZ, NY)) == 0

    def put(field, source):
        one = jnp.concatenate([source(0), source(1)], axis=0).T
        two = jnp.concatenate([source(2), source(3)], axis=0).T
        for m in range(TILES // 2):
            here = slice(8 * m, 8 * m + 8)
            even, odd = mix(one[here], two[here])
            out[member(2 * m), field] = even
            out[member(2 * m + 1), field] = odd

    for k in range(ARCS):
        put(k, lambda t, k=k: jnp.where(top, mask[k], prec[k, t]))
    put(BOUND, lambda t: bound[t])
    put(SHARE, lambda t: share[t])
    put(RIM, lambda t: rim[t])
    classes = ton_class[...]
    tons = jnp.zeros(classes.shape, F32)
    for c in range(8):
        tons = jnp.where(classes == c, (1.0 + c) * density[c], tons)
    blocks = jnp.concatenate([tons, value[...]], axis=0).T
    half = later_half(row)
    zero = jnp.zeros(row, F32)
    cap_rows = [jnp.where(half, caps[2 * a + 1], caps[2 * a]) for a in range(2)]
    limit_rows = [jnp.where(half, limits[2 * a + 1], limits[2 * a]) for a in range(2)]
    for j in range(TILES):
        i = member(j)
        two = blocks[8 * (j // 2) : 8 * (j // 2) + 8]
        out[i, BLOCK] = two if j % 2 == 0 else turn(two)
        for a in range(2):
            if j > 0:
                out[i, EXTRA, a : a + 1] = out[member(j - 1), 3, 4 * a + 3 : 4 * a + 4]
            else:
                out[i, EXTRA, a : a + 1] = zero
            if j < TILES - 1:
                out[i, EXTRA, 2 + a : 3 + a] = out[member(j + 1), 4, 4 * a : 4 * a + 1]
            else:
                out[i, EXTRA, 2 + a : 3 + a] = zero
            out[i, EXTRA, 4 + a : 5 + a] = cap_rows[a]
            out[i, EXTRA, 6 + a : 7 + a] = limit_rows[a]


def adjoint_row(prices, bound, halo, edges, r, carry):
    shape = (8, 128)
    sub = subs(shape)
    one = slice(r, r + 1)
    total = prices[0] + prices[1] + prices[2] + prices[3] + prices[4] + bound
    across = turn(jnp.where(low(), prices[1], prices[2]))
    before = pltpu.roll(prices[3], 1, 0)
    before = jnp.where(sub == 0, edges[0, 0, one], jnp.where(sub == 4, edges[0, 1, one], before))
    after = pltpu.roll(prices[4], 7, 0)
    after = jnp.where(sub == 3, edges[1, 0, one], jnp.where(sub == 7, edges[1, 1, one], after))
    lower = prices[0] + halo + across + before + after
    g = total - up(lower)
    pair = g + swap(g)
    return carry + jnp.where(later_half(shape), g, pair), carry + pair


def unpack_kernel(got, prices, halos, edges, bound, share, caps, limits, tail, masks):
    shape = (8, 128)
    lane = lanes(shape)
    deep = ((lane & 63) >= 1).astype(F32)
    half = later_half(shape)

    def pair(s, field):
        return mix(got[s, field], got[16 + s, field])

    for k in range(ARCS):
        masks[k] = jnp.broadcast_to(pair(0, k)[0][:, 0:1], shape) * deep
    masks[HALO] = jnp.broadcast_to(pair(0, RIM)[0][:, 0:1], shape) * deep
    for n in range(2):
        for x in range(2):
            at = 2 * n + x
            edge = got[16 * x, EXTRA, 2 * n : 2 * n + 1]
            masks[EDGES, at : at + 1] = jnp.broadcast_to(edge[:, 0:1], (1, 128)) * deep[0:1]
            masks[EDGES, 4 + at : 5 + at] = jnp.zeros((1, 128), F32)
    blocks = pair(0, BLOCK)[0]
    other = swap(blocks)
    masks[TONS] = jnp.where(half, other, blocks)
    masks[VALUE] = jnp.where(half, blocks, other)
    for s in range(ROWS // 2):
        two = slice(2 * s, 2 * s + 2)
        for n in range(2):
            for x in range(2):
                at = 2 * n + x
                edges[n, x, two] = got[16 * x + s, EXTRA, 2 * n : 2 * n + 2] * masks[EDGES, at : at + 1]
        caps[two] = got[s, EXTRA, 4:6]
        limits[two] = got[s, EXTRA, 6:8]
    carry = jnp.zeros(shape, F32)
    for s in reversed(range(ROWS // 2)):
        p = [pair(s, k) for k in range(ARCS)]
        b, u, h = pair(s, BOUND), pair(s, SHARE), pair(s, RIM)
        for a in (1, 0):
            r = 2 * s + a
            here = [p[k][a] * masks[k] for k in range(ARCS)]
            for k in range(ARCS):
                prices[k, r] = here[k]
            bound[r] = b[a]
            share[r] = u[a]
            halo = h[a] * masks[HALO]
            halos[r] = halo
            tail[r], carry = adjoint_row(here, b[a], halo, edges, r, carry)


def summed_row(got):
    total = got[0:8]
    for n in range(1, DEVICES // 8):
        total = total + got[8 * n : 8 * n + 8]
    return jnp.sum(total, axis=0, keepdims=True)


def lane_value(row, lane):
    return jnp.sum(jnp.where(lanes((1, 128)) == lane, row, 0.0), axis=1, keepdims=True)


def caps_after(row, caps, limits, weight):
    shape = (ROWS, 128)
    spread = jnp.where((lanes(shape) & 63) == subs(shape), jnp.broadcast_to(row, shape), 0.0)
    totals = half_sums(spread)
    tons_all = lane_value(row, LANE_TONS)
    return jnp.maximum(caps + weight * (totals - BLOCKS * limits) / tons_all, 0.0)


def weight_after(row, weight, mean, first):
    move_cap = jnp.sum(
        jnp.sum((mean - first) ** 2, axis=0, keepdims=True), axis=1, keepdims=True
    ) * (1.0 / 64.0)
    primal_move = lane_value(row, LANE_PRIMAL)
    dual_move = lane_value(row, LANE_DUAL) + move_cap
    return jnp.sqrt(weight * jnp.sqrt((dual_move + EPS) / (primal_move + EPS)))


def primal_step(
    caps, tail, share, planes, weight, new, head, low_rows, high_rows,
    first, last, row, cap_rows, rate_rows,
):
    shape = (8, 128)
    tons = planes[TONS]
    value = planes[VALUE]
    lean = tons / ROOT
    cap_rows[...] = caps
    periods = period_table()
    rate_rows[0] = jnp.exp(-RATE * periods)
    rate_rows[1] = SLOPE * (NP - periods)
    half = later_half(shape)
    carry = jnp.zeros(shape, F32)
    mined = []
    for r in range(ROWS):
        one = slice(r, r + 1)
        gradient = tail[r] + tons * cap_rows[one] / ROOT
        tau = 1.0 / (weight * (rate_rows[1, one] + lean))
        old = share[r]
        now = jnp.maximum(old - tau * (gradient - value * rate_rows[0, one]), 0.0)
        new[r] = now
        ahead = 2.0 * now - old
        pair = ahead + swap(ahead)
        cumulative = carry + jnp.where(half, pair, ahead)
        carry = carry + pair
        head[r] = cumulative
        for x in range(2):
            first[x, one] = cumulative[4 * x : 4 * x + 1]
            last[x, one] = cumulative[4 * x + 3 : 4 * x + 4]
        if r % 2 == 0:
            even = cumulative
        else:
            low_rows[r // 2], high_rows[r // 2] = mix(even, cumulative)
        mined.append(tons * ahead)
    mined.append(tons)
    sums = half_sums(jnp.concatenate(mined, axis=0))
    lane = lanes(shape)
    total = jnp.where(lane == LANE_TONS, sums[8 * ROWS :], 0.0)
    for r in range(ROWS):
        total = total + jnp.where((lane & 63) == r, sums[8 * r : 8 * r + 8], 0.0)
    row[...] = jnp.broadcast_to(jnp.sum(total, axis=0, keepdims=True), row.shape)


def primal_first_kernel(caps, tail, share, planes, weight, *rest):
    primal_step(caps[...], tail, share, planes, weight[...], *rest)


def primal_kernel(got, caps, limits, tail, share, planes, weight, caps_new, *rest):
    row = summed_row(got)
    caps_now = caps_after(row, caps[...], limits[...], weight[...])
    caps_new[...] = caps_now
    primal_step(caps_now, tail, share, planes, weight[...], *rest)


def restart(got, caps0, caps1, caps2, limits, weight):
    row = summed_row(got)
    caps3 = caps_after(row, caps2[...], limits[...], weight[...])
    mean = (caps1[...] + caps2[...] + caps3) / INNER
    return mean, weight_after(row, weight[...], mean, caps0[...])


def primal_restart_kernel(
    got, caps0, caps1, caps2, limits, tail, share, planes, weight, caps_new, weight_new, *rest
):
    mean, new = restart(got, caps0, caps1, caps2, limits, weight)
    caps_new[...] = mean
    weight_new[...] = new
    primal_step(mean, tail, share, planes, new, *rest)


def finish_kernel(got, caps0, caps1, caps2, limits, weight, caps_new, weight_new):
    mean, new = restart(got, caps0, caps1, caps2, limits, weight)
    caps_new[...] = mean
    weight_new[...] = new


def dual_rows(weight, planes, front, back, first, last, edges, steps, ahead):
    periods = period_table()
    steps[0] = weight[...] / (2.0 * (periods + 1.0))
    steps[1] = weight[...] / (periods + 1.0)
    new = []
    for n, outside, inside in ((0, front, first), (1, back, last)):
        new.append([])
        for x in range(2):
            at = 2 * n + x
            there = outside[x]
            ahead[n, x] = down(there)
            price = edges[n, x] + steps[0] * (there - down(inside[x]))
            new[n].append(jnp.maximum(price, 0.0) * planes[EDGES, at : at + 1])
    return new


def dual_pair(s, planes, head, lower, upper, prices, halos, bound, steps, ahead_rows):
    outside = mix(lower[s], upper[s])
    return [
        dual_row(2 * s + a, outside[a], planes, head, prices, halos, bound, steps, ahead_rows)
        for a in range(2)
    ]


def dual_row(r, outside, planes, head, prices, halos, bound, steps, ahead_rows):
    one = slice(r, r + 1)
    step = steps[0, one]
    here = head[r]
    under = down(here)
    away = down(outside)
    other = turn(under)
    sub = subs((8, 128))
    after = pltpu.roll(under, 7, 0)
    before = pltpu.roll(under, 1, 0)
    ahead = [
        under,
        jnp.where(low(), other, away),
        jnp.where(low(), away, other),
        jnp.where(
            sub == 3, ahead_rows[1, 0, one], jnp.where(sub == 7, ahead_rows[1, 1, one], after)
        ),
        jnp.where(
            sub == 0, ahead_rows[0, 0, one], jnp.where(sub == 4, ahead_rows[0, 1, one], before)
        ),
    ]
    p = [
        jnp.maximum(prices[k, r] + step * (here - ahead[k]), 0.0) * planes[k] for k in range(ARCS)
    ]
    b = jnp.maximum(bound[r] + steps[1, one] * (here - 1.0), 0.0)
    h = jnp.maximum(halos[r] + step * (outside - under), 0.0) * planes[HALO]
    return p, b, h


def dual_kernel(
    weight, planes, head, lower, upper, front, back, first, last, prices, halos, edges, bound,
    prices_new, halos_new, edges_new, bound_new, tail, steps, ahead,
):
    new = dual_rows(weight, planes, front, back, first, last, edges, steps, ahead)
    for n in range(2):
        for x in range(2):
            edges_new[n, x] = new[n][x]
    carry = jnp.zeros((8, 128), F32)
    for s in reversed(range(ROWS // 2)):
        both = dual_pair(s, planes, head, lower, upper, prices, halos, bound, steps, ahead)
        for a in (1, 0):
            r = 2 * s + a
            p, b, h = both[a]
            for k in range(ARCS):
                prices_new[k, r] = p[k]
            bound_new[r] = b
            halos_new[r] = h
            tail[r], carry = adjoint_row(p, b, h, edges_new, r, carry)


def mean_of(one, two, three):
    return (one + two + three) / INNER


def moves_kernel(moves, row, row_new):
    lane = lanes((1, 128))

    def whole(v):
        return jnp.sum(jnp.sum(v, axis=0, keepdims=True), axis=1, keepdims=True)

    new = row[0:1] + jnp.where(lane == LANE_PRIMAL, whole(moves[0]), 0.0)
    new = new + jnp.where(lane == LANE_DUAL, whole(moves[1]), 0.0)
    row_new[...] = jnp.broadcast_to(new, row_new.shape)


def dual_restart_kernel(
    weight, planes, head, lower, upper, front, back, first, last, prices, halos, edges, bound,
    prices0, prices1, halos1, edges1, bound0, bound1, share0, share1, share2, share3, row,
    prices_new, halos_new, edges_new, bound_new, tail, share_new, row_new, steps, ahead, moves,
):
    new = dual_rows(weight, planes, front, back, first, last, edges, steps, ahead)
    for n in range(2):
        for x in range(2):
            edges_new[n, x] = mean_of(edges1[n, x], edges[n, x], new[n][x])
    shape = (8, 128)
    carry = jnp.zeros(shape, F32)
    primal_move = jnp.zeros(shape, F32)
    dual_move = jnp.zeros(shape, F32)
    for s in reversed(range(ROWS // 2)):
        both = dual_pair(s, planes, head, lower, upper, prices, halos, bound, steps, ahead)
        for a in (1, 0):
            r = 2 * s + a
            p, b, h = both[a]
            p = [mean_of(prices1[k, r], prices[k, r], p[k]) for k in range(ARCS)]
            b = mean_of(bound1[r], bound[r], b)
            h = mean_of(halos1[r], halos[r], h)
            u = mean_of(share1[r], share2[r], share3[r])
            primal_move = primal_move + (u - share0[r]) ** 2
            dual_move = dual_move + (b - bound0[r]) ** 2
            for k in range(ARCS):
                dual_move = dual_move + (p[k] - prices0[k, r]) ** 2
                prices_new[k, r] = p[k]
            bound_new[r] = b
            halos_new[r] = h
            share_new[r] = u
            tail[r], carry = adjoint_row(p, b, h, edges_new, r, carry)
    moves[0] = primal_move
    moves[1] = dual_move
    moves_kernel(moves, row, row_new)


def dual_final_kernel(
    weight, planes, head, lower, upper, front, back, first, last, prices, halos, edges, bound,
    prices0, prices1, bound0, bound1, share0, share1, share2, share3, send, moves, steps, ahead,
):
    dual_rows(weight, planes, front, back, first, last, edges, steps, ahead)
    shape = (8, 128)
    primal_move = jnp.zeros(shape, F32)
    dual_move = jnp.zeros(shape, F32)
    for s in range(ROWS // 2):
        both = dual_pair(s, planes, head, lower, upper, prices, halos, bound, steps, ahead)
        means = []
        for a in range(2):
            r = 2 * s + a
            p, b, _ = both[a]
            p = [mean_of(prices1[k, r], prices[k, r], p[k]) for k in range(ARCS)]
            b = mean_of(bound1[r], bound[r], b)
            u = mean_of(share1[r], share2[r], share3[r])
            primal_move = primal_move + (u - share0[r]) ** 2
            dual_move = dual_move + (b - bound0[r]) ** 2
            for k in range(ARCS):
                dual_move = dual_move + (p[k] - prices0[k, r]) ** 2
            means.append(p + [b, u])
        for field in range(7):
            send[s, field], send[16 + s, field] = mix(means[0][field], means[1][field])
    moves[0] = primal_move
    moves[1] = dual_move


def turn_back_kernel(got, share, prec, bound):
    def take(field, target):
        rows = [
            mix(got[member(2 * m), field], got[member(2 * m + 1), field]) for m in range(TILES // 2)
        ]
        for a in range(2):
            turned = jnp.concatenate([pair[a] for pair in rows], axis=0).T
            target(2 * a, turned[0:64])
            target(2 * a + 1, turned[64:128])

    for k in range(ARCS):

        def store(t, v, k=k):
            prec[k, t] = v

        take(k, store)

    def store_bound(t, v):
        bound[t] = v

    def store_share(t, v):
        share[t] = v

    take(BOUND, store_bound)
    take(SHARE, store_share)


def f32(*shape):
    return jax.ShapeDtypeStruct(shape, F32)


VMEM = pl.BlockSpec(memory_space=pltpu.VMEM)
SMEM = pl.BlockSpec(memory_space=pltpu.SMEM)
FIELD = (ROWS, 8, 128)


def call(kernel, outs, scratch=(), scalars=0):
    def run(*args):
        specs = [SMEM] * scalars + [VMEM] * (len(args) - scalars)
        return pl.pallas_call(
            kernel,
            out_shape=[f32(*shape) for shape in outs],
            in_specs=specs,
            out_specs=[VMEM] * len(outs),
            scratch_shapes=[pltpu.VMEM(shape, F32) for shape in scratch],
            compiler_params=pltpu.CompilerParams(vmem_limit_bytes=12 * 1024 * 1024),
        )(*args)

    return run


STEP_OUTS = [
    FIELD, FIELD, (ROWS // 2, 8, 128), (ROWS // 2, 8, 128), (2, ROWS, 128), (2, ROWS, 128),
    (DEVICES, 128),
]
STEP_SCRATCH = [(ROWS, 128), (2, ROWS, 128)]
DUAL_OUTS = [(ARCS,) + FIELD, FIELD, (2, 2, ROWS, 128), FIELD, FIELD]
DUAL_SCRATCH = [(2, ROWS, 128), (2, 2, ROWS, 128)]
EVERY = ("strip", "period")


def share_row(row):
    return lax.all_to_all(row, EVERY, 0, 0, tiled=True)


def exchange(slots):
    groups = [[PLANE * z + i for i in range(PLANE)] for z in range(DEVICES // PLANE)]
    return lax.all_to_all(slots, EVERY, 0, 0, axis_index_groups=groups)


def along_x(value, by):
    planes = DEVICES // PLANE
    pairs = [
        (PLANE * z + i, PLANE * (z + by) + i)
        for z in range(planes)
        if 0 <= z + by < planes
        for i in range(PLANE)
    ]
    return lax.ppermute(value, EVERY, pairs)


def along_y(value, by):
    pairs = [
        (PLANE * z + member(j), PLANE * z + member(j + by))
        for z in range(DEVICES // PLANE)
        for j in range(TILES)
        if 0 <= j + by < TILES
    ]
    return lax.ppermute(value, EVERY, pairs)


def halo(low_rows, high_rows, first, last):
    back = along_y(first, -1)
    front = along_y(last, 1)
    lower = along_x(high_rows, 1)
    upper = along_x(low_rows, -1)
    return lower, upper, front, back


def per_device(
    u_start,
    dual_prec,
    dual_bound,
    dual_cap,
    capacity,
    block_value,
    ton_class,
    density,
    slope_code,
    omega_start,
):
    x, tile = lax.axis_index("strip"), lax.axis_index("period")
    prec = dual_prec[:, 0]
    top = (jnp.arange(NZ) == 0)[None, :, None]
    toward = ((slope_code & 1) * (x + 1 < NX)).astype(F32)[None]
    away = ((slope_code // 2 & 1) * (x >= 1)).astype(F32)[None]
    odd = x % 2 == 1
    rim = jnp.where(top, jnp.where(odd, toward, away), jnp.where(odd, prec[1], prec[2]))
    swaps = [(i, i + 1 if i % 2 else i - 1) for i in range(1, NX - 1)]
    rim = lax.ppermute(rim, "strip", swaps)
    place = jnp.reshape(x, (1,)).astype(jnp.int32)
    (send,) = call(pack_kernel, [(TILES, SLOTS, 8, 128)], (), 4)(
        place, dual_cap, capacity, density, slope_code, ton_class[0], block_value[0],
        u_start[0], prec, dual_bound[0], rim,
    )
    got = exchange(send)
    prices, halos, edges, bound, share, caps, limits, tail, planes = call(
        unpack_kernel,
        [
            (ARCS,) + FIELD, FIELD, (2, 2, ROWS, 128), FIELD, FIELD, (ROWS, 128), (ROWS, 128),
            FIELD, (PLANES, 8, 128),
        ],
    )(got)
    weight = jnp.reshape(omega_start, (1, 1))
    row_sums = None
    old_caps = None
    for outer in range(OUTER):
        shares, caps_list = [share], []
        price_list, halo_list, edge_list, bound_list = [prices], [halos], [edges], [bound]
        for inner in range(INNER):
            if inner == 0 and outer == 0:
                new, head, low_rows, high_rows, first, last, row = call(
                    primal_first_kernel, STEP_OUTS, STEP_SCRATCH
                )(caps, tail, share, planes, weight)
            elif inner == 0:
                caps, weight, new, head, low_rows, high_rows, first, last, row = call(
                    primal_restart_kernel, [(ROWS, 128), (1, 1)] + STEP_OUTS, STEP_SCRATCH
                )(row_sums, *old_caps, limits, tail, share, planes, weight)
            else:
                caps, new, head, low_rows, high_rows, first, last, row = call(
                    primal_kernel, [(ROWS, 128)] + STEP_OUTS, STEP_SCRATCH
                )(row_sums, caps, limits, tail, share, planes, weight)
            caps_list.append(caps)
            shares.append(new)
            share = new
            lower, upper, front, back = halo(low_rows, high_rows, first, last)
            common = (
                weight, planes, head, lower, upper, front, back, first, last,
                prices, halos, edges, bound,
            )
            if inner < INNER - 1:
                row_sums = share_row(row)
                prices, halos, edges, bound, tail = call(
                    dual_kernel, DUAL_OUTS, DUAL_SCRATCH
                )(*common)
                price_list.append(prices)
                halo_list.append(halos)
                edge_list.append(edges)
                bound_list.append(bound)
            elif outer < OUTER - 1:
                prices, halos, edges, bound, tail, share, row = call(
                    dual_restart_kernel, DUAL_OUTS + [FIELD, (DEVICES, 128)],
                    DUAL_SCRATCH + [(2, 8, 128)],
                )(
                    *common, price_list[0], price_list[1], halo_list[1], edge_list[1],
                    bound_list[0], bound_list[1], *shares, row,
                )
                row_sums = share_row(row)
                old_caps = caps_list
            else:
                send, moves = call(
                    dual_final_kernel, [(TILES, 7, 8, 128), (2, 8, 128)], DUAL_SCRATCH
                )(
                    *common, price_list[0], price_list[1], bound_list[0], bound_list[1], *shares,
                )
                got = exchange(send)
                (row,) = call(moves_kernel, [(DEVICES, 128)])(moves, row)
                row_sums = share_row(row)
                old_caps = caps_list
    mined, arcs, bounds = call(
        turn_back_kernel, [(4, NZ, NY), (ARCS, 4, NZ, NY), (4, NZ, NY)]
    )(got)
    caps, weight = call(finish_kernel, [(ROWS, 128), (1, 1)])(
        row_sums, *old_caps, limits, weight
    )
    own = lax.dynamic_slice(caps, (2 * tile, 0), (2, 128))[:, ::64]
    return (
        mined[None],
        arcs[:, None],
        bounds[None],
        jnp.reshape(own, (4,)),
        jnp.reshape(weight, (1,)),
    )


def solution(mesh):
    in_specs = (
        P("strip", "period", None, None),
        P(None, "strip", "period", None, None),
        P("strip", "period", None, None),
        P("period"),
        P("period"),
        P("strip", None, None),
        P("strip", None, None),
        P(),
        P("strip", None),
        P(),
    )
    out_specs = (
        P("strip", "period", None, None),
        P(None, "strip", "period", None, None),
        P("strip", "period", None, None),
        P("period"),
        P(),
    )
    return jax.shard_map(
        per_device, mesh=mesh, in_specs=in_specs, out_specs=out_specs, check_vma=False
    )
```

time: 305 us -> 285 us (0.934)
  waiting for transfers between devices: 63.3 us -> 52.1 us
  blocking collectives: 63.5 us -> 58.8 us
    ppermute x26 -> x25, waiting for transfers between devices: 31.7 us -> 19.2 us  [the longest x12 19.2 us: along_y(): return lax.ppermute(value, EVERY, pairs)]
    ppermute x26 -> x25, starting transfers between devices: 70.9 us -> 62 us  [the longest x12 31.2 us: along_y(): return lax.ppermute(value, EVERY, pairs)]
    all_to_all x6, starting transfers between devices: 62.4 us -> 68 us  [the longest x4 48.3 us: share_row(): return lax.all_to_all(row, EVERY, 0, 0, tiled=True)]
    all_to_all x2, blocking collectives: 63.5 us -> 58.8 us  [share_row(): return lax.all_to_all(row, EVERY, 0, 0, tiled=True)]
    unnamed x82 -> x76, local copies, waits for them, and re-layouts: 19.5 us -> 19.1 us
  transfers between devices with their start and end apart: 32 -> 31, of which waited for: 10 -> 8; matrix products, arithmetic and copies ran while one was open for 0% -> 0% of each run, Pallas kernels for 2% -> 2%
where the time goes in v2:
time: 285 us; the launch traced here: 283 us
  starting transfers between devices  130 us (46%)
  blocking collectives  58.8 us (21%)
  waiting for transfers between devices  52.1 us (18%)
  local copies, waits for them, and re-layouts  19.8 us (7%)
  Pallas kernels  18.9 us (7%)
    all_to_all x2, blocking collectives, share_row(): return lax.all_to_all(row, EVERY, 0, 0, tiled=True)  58.8 us
    all_to_all x4, starting transfers between devices, share_row(): return lax.all_to_all(row, EVERY, 0, 0, tiled=True)  48.3 us
    all_to_all x2, waiting for transfers between devices, exchange(): return lax.all_to_all(slots, EVERY, 0, 0, axis_index_groups=groups)  32.9 us
    ppermute x12, starting transfers between devices, along_y(): return lax.ppermute(value, EVERY, pairs)  31.2 us
    ppermute x12, starting transfers between devices, along_x(): return lax.ppermute(value, EVERY, pairs)  30.1 us
    all_to_all x2, starting transfers between devices, exchange(): return lax.all_to_all(slots, EVERY, 0, 0, axis_index_groups=groups)  19.7 us
    ppermute x12, waiting for transfers between devices, along_y(): return lax.ppermute(value, EVERY, pairs)  19.2 us
    unnamed x76, local copies, waits for them, and re-layouts  19.1 us
  transfers between devices with their start and end apart: 31, of which 8 were waited for; matrix products, arithmetic and copies ran while one was open for 0% of the time, Pallas kernels for 2%

profile of v2, /device:TPU:1, one launch (start us, length us, event | category | flops | bytes accessed | tf_op | source)
XLA Modules:
  0.0 283.4 jit_solution(13052727418555520326)
XLA Ops:
  12.1 15.7 %all-to-all-start = ((f32[32,10,8,128]{3,2,1,0:T(8,128)}), f32[32,10,8,128]{3,2,1,0:T(8,128)S(1)}, u32[]{:S(2)}, u32[]{:S(2)}) async-start(f32[32,10,8,128]{3,2,1,0:T(8,128)} %shard_map.137), calls=%async_computation | async-start | bytes 2621440 | tf_op jit(solution)/shard_map/all_to_all | solution.py:536
  28.5 19.2 %all-to-all-done.got = f32[32,10,8,128]{3,2,1,0:T(8,128)S(1)} async-done(((f32[32,10,8,128]{3,2,1,0:T(8,128)}), f32[32,10,8,128]{3,2,1,0:T(8,128)S(1)}, u32[]{:S(2)}, u32[]{:S(2)}) %all-to-all-start) | async-done | bytes 1310752 | tf_op jit(solution)/shard_map/all_to_all | solution.py:536
  49.2 12.4 %all-to-all-start.1 = ((f32[256,1,128]{2,1,0:T(1,128)}), f32[256,1,128]{2,1,0:T(1,128)S(1)}, u32[]{:S(2)}, u32[]{:S(2)}) async-start(f32[256,1,128]{2,1,0:T(1,128)} %bitcast.10), calls=%async_computation.1 | async-start | bytes 262144 | tf_op jit(solution)/shard_map/all_to_all | solution.py:531
  61.6 3.4 %collective-permute-start.1 = (f32[16,8,128]{2,1,0:T(8,128)S(1)}, f32[16,8,128]{2,1,0:T(8,128)S(1)}, u32[]{:S(2)}, u32[]{:S(2)}) collective-permute-start(f32[16,8,128]{2,1,0:T(8,128)S(1)} %get-tuple-element.103), channel_id=1, source_target_pairs={{0,32},{1,33},{2,34},{3,35},{4,36},{5,37},{6,38},{7,39},{8,40},{9,... | collective-permute-start | bytes 196616 | tf_op jit(solution)/shard_map/ppermute | solution.py:547
  66.3 3.7 %collective-permute-start.3 = (f32[2,32,128]{2,1,0:T(8,128)S(1)}, f32[2,32,128]{2,1,0:T(8,128)S(1)}, u32[]{:S(2)}, u32[]{:S(2)}) collective-permute-start(f32[2,32,128]{2,1,0:T(8,128)S(1)} %get-tuple-element.105.last), channel_id=1, source_target_pairs={{0,1},{1,4},{4,5},{5,8},{8,9},{9,12},{12,13},{13,28},{28,29},{29,2... | collective-permute-start | bytes 98312 | tf_op jit(solution)/shard_map/ppermute | solution.py:557
  71.9 3.3 %collective-permute-done.4.back = f32[2,32,128]{2,1,0:T(8,128)S(1)} collective-permute-done((f32[2,32,128]{2,1,0:T(8,128)S(1)}, f32[2,32,128]{2,1,0:T(8,128)S(1)}, u32[]{:S(2)}, u32[]{:S(2)}) %collective-permute-start.4) | collective-permute-done | bytes 32800 | tf_op jit(solution)/shard_map/ppermute | solution.py:557
  77.2 15.2 %all-to-all-start.2 = ((f32[256,1,128]{2,1,0:T(1,128)}), f32[256,1,128]{2,1,0:T(1,128)S(1)}, u32[]{:S(2)}, u32[]{:S(2)}) async-start(f32[256,1,128]{2,1,0:T(1,128)} %bitcast.13), calls=%async_computation.2 | async-start | bytes 262144 | tf_op jit(solution)/shard_map/all_to_all | solution.py:531
  92.4 3.4 %collective-permute-start.5 = (f32[16,8,128]{2,1,0:T(8,128)S(1)}, f32[16,8,128]{2,1,0:T(8,128)S(1)}, u32[]{:S(2)}, u32[]{:S(2)}) collective-permute-start(f32[16,8,128]{2,1,0:T(8,128)S(1)} %get-tuple-element.116), channel_id=1, source_target_pairs={{0,32},{1,33},{2,34},{3,35},{4,36},{5,37},{6,38},{7,39},{8,40},{9,... | collective-permute-start | bytes 196616 | tf_op jit(solution)/shard_map/ppermute | solution.py:547
  97.1 3.7 %collective-permute-start.7 = (f32[2,32,128]{2,1,0:T(8,128)S(1)}, f32[2,32,128]{2,1,0:T(8,128)S(1)}, u32[]{:S(2)}, u32[]{:S(2)}) collective-permute-start(f32[2,32,128]{2,1,0:T(8,128)S(1)} %get-tuple-element.118.last), channel_id=1, source_target_pairs={{0,1},{1,4},{4,5},{5,8},{8,9},{9,12},{12,13},{13,28},{28,29},{29,2... | collective-permute-start | bytes 98312 | tf_op jit(solution)/shard_map/ppermute | solution.py:557
  102.8 3.3 %collective-permute-done.8.back = f32[2,32,128]{2,1,0:T(8,128)S(1)} collective-permute-done((f32[2,32,128]{2,1,0:T(8,128)S(1)}, f32[2,32,128]{2,1,0:T(8,128)S(1)}, u32[]{:S(2)}, u32[]{:S(2)}) %collective-permute-start.8) | collective-permute-done | bytes 32800 | tf_op jit(solution)/shard_map/ppermute | solution.py:557
  110.3 4.3 %collective-permute-start.9 = (f32[16,8,128]{2,1,0:T(8,128)S(1)}, f32[16,8,128]{2,1,0:T(8,128)S(1)}, u32[]{:S(2)}, u32[]{:S(2)}) collective-permute-start(f32[16,8,128]{2,1,0:T(8,128)S(1)} %get-tuple-element.127), channel_id=1, source_target_pairs={{0,32},{1,33},{2,34},{3,35},{4,36},{5,37},{6,38},{7,39},{8,40},{9,... | collective-permute-start | bytes 196616 | tf_op jit(solution)/shard_map/ppermute | solution.py:547
  128.6 29.4 %all_to_all.76 = f32[256,1,128]{2,1,0:T(1,128)S(1)} all-to-all(f32[256,1,128]{2,1,0:T(1,128)S(1)} %bitcast.58), channel_id=1, replica_groups=mesh['strip'=16,'period'=16] {'strip','period'}, dimensions={0} | all-to-all | bytes 262144 | tf_op jit(solution)/shard_map/all_to_all | solution.py:531
  159.6 5.4 %all-to-all-start.4 = ((f32[256,1,128]{2,1,0:T(1,128)}), f32[256,1,128]{2,1,0:T(1,128)S(1)}, u32[]{:S(2)}, u32[]{:S(2)}) async-start(f32[256,1,128]{2,1,0:T(1,128)} %bitcast.19), calls=%async_computation.4 | async-start | bytes 262144 | tf_op jit(solution)/shard_map/all_to_all | solution.py:531
  165.0 3.6 %collective-permute-start.13 = (f32[16,8,128]{2,1,0:T(8,128)S(1)}, f32[16,8,128]{2,1,0:T(8,128)S(1)}, u32[]{:S(2)}, u32[]{:S(2)}) collective-permute-start(f32[16,8,128]{2,1,0:T(8,128)S(1)} %get-tuple-element.145), channel_id=1, source_target_pairs={{0,32},{1,33},{2,34},{3,35},{4,36},{5,37},{6,38},{7,39},{8,40},{9,... | collective-permute-start | bytes 196616 | tf_op jit(solution)/shard_map/ppermute | solution.py:547
  169.9 3.7 %collective-permute-start.15 = (f32[2,32,128]{2,1,0:T(8,128)S(1)}, f32[2,32,128]{2,1,0:T(8,128)S(1)}, u32[]{:S(2)}, u32[]{:S(2)}) collective-permute-start(f32[2,32,128]{2,1,0:T(8,128)S(1)} %get-tuple-element.147.last), channel_id=1, source_target_pairs={{0,1},{1,4},{4,5},{5,8},{8,9},{9,12},{12,13},{13,28},{28,29},{29,2... | collective-permute-start | bytes 98312 | tf_op jit(solution)/shard_map/ppermute | solution.py:557
  175.7 3.1 %collective-permute-done.16.back = f32[2,32,128]{2,1,0:T(8,128)S(1)} collective-permute-done((f32[2,32,128]{2,1,0:T(8,128)S(1)}, f32[2,32,128]{2,1,0:T(8,128)S(1)}, u32[]{:S(2)}, u32[]{:S(2)}) %collective-permute-start.16) | collective-permute-done | bytes 32800 | tf_op jit(solution)/shard_map/ppermute | solution.py:557
  183.6 15.2 %all-to-all-start.5 = ((f32[256,1,128]{2,1,0:T(1,128)}), f32[256,1,128]{2,1,0:T(1,128)S(1)}, u32[]{:S(2)}, u32[]{:S(2)}) async-start(f32[256,1,128]{2,1,0:T(1,128)} %bitcast.22), calls=%async_computation.5 | async-start | bytes 262144 | tf_op jit(solution)/shard_map/all_to_all | solution.py:531
  198.8 3.4 %collective-permute-start.17 = (f32[16,8,128]{2,1,0:T(8,128)S(1)}, f32[16,8,128]{2,1,0:T(8,128)S(1)}, u32[]{:S(2)}, u32[]{:S(2)}) collective-permute-start(f32[16,8,128]{2,1,0:T(8,128)S(1)} %get-tuple-element.158), channel_id=1, source_target_pairs={{0,32},{1,33},{2,34},{3,35},{4,36},{5,37},{6,38},{7,39},{8,40},{9,... | collective-permute-start | bytes 196616 | tf_op jit(solution)/shard_map/ppermute | solution.py:547
  203.6 3.7 %collective-permute-start.19 = (f32[2,32,128]{2,1,0:T(8,128)S(1)}, f32[2,32,128]{2,1,0:T(8,128)S(1)}, u32[]{:S(2)}, u32[]{:S(2)}) collective-permute-start(f32[2,32,128]{2,1,0:T(8,128)S(1)} %get-tuple-element.160.last), channel_id=1, source_target_pairs={{0,1},{1,4},{4,5},{5,8},{8,9},{9,12},{12,13},{13,28},{28,29},{29,2... | collective-permute-start | bytes 98312 | tf_op jit(solution)/shard_map/ppermute | solution.py:557
  209.2 3.3 %collective-permute-done.20.back = f32[2,32,128]{2,1,0:T(8,128)S(1)} collective-permute-done((f32[2,32,128]{2,1,0:T(8,128)S(1)}, f32[2,32,128]{2,1,0:T(8,128)S(1)}, u32[]{:S(2)}, u32[]{:S(2)}) %collective-permute-start.20) | collective-permute-done | bytes 32800 | tf_op jit(solution)/shard_map/ppermute | solution.py:557
  217.0 4.3 %collective-permute-start.21 = (f32[16,8,128]{2,1,0:T(8,128)S(1)}, f32[16,8,128]{2,1,0:T(8,128)S(1)}, u32[]{:S(2)}, u32[]{:S(2)}) collective-permute-start(f32[16,8,128]{2,1,0:T(8,128)S(1)} %get-tuple-element.169), channel_id=1, source_target_pairs={{0,32},{1,33},{2,34},{3,35},{4,36},{5,37},{6,38},{7,39},{8,40},{9,... | collective-permute-start | bytes 196616 | tf_op jit(solution)/shard_map/ppermute | solution.py:547
  233.0 29.4 %all_to_all.77 = f32[256,1,128]{2,1,0:T(1,128)S(1)} all-to-all(f32[256,1,128]{2,1,0:T(1,128)S(1)} %bitcast.55), channel_id=1, replica_groups=mesh['strip'=16,'period'=16] {'strip','period'}, dimensions={0} | all-to-all | bytes 262144 | tf_op jit(solution)/shard_map/all_to_all | solution.py:531
  262.4 4.0 %all-to-all-start.6 = ((f32[32,7,8,128]{3,2,1,0:T(8,128)}), f32[32,7,8,128]{3,2,1,0:T(8,128)S(1)}, u32[]{:S(2)}, u32[]{:S(2)}) async-start(f32[32,7,8,128]{3,2,1,0:T(8,128)} %get-tuple-element.178), calls=%async_computation.6 | async-start | bytes 1835008 | tf_op jit(solution)/shard_map/all_to_all | solution.py:536
  268.5 13.7 %all-to-all-done.6.got = f32[32,7,8,128]{3,2,1,0:T(8,128)S(1)} async-done(((f32[32,7,8,128]{3,2,1,0:T(8,128)}), f32[32,7,8,128]{3,2,1,0:T(8,128)S(1)}, u32[]{:S(2)}, u32[]{:S(2)}) %all-to-all-start.6) | async-done | bytes 917536 | tf_op jit(solution)/shard_map/all_to_all | solution.py:536
  (139 shorter events, 71.7 us)
Async XLA Ops:
  12.1 35.6 %all-to-all-start = ((f32[32,10,8,128]{3,2,1,0:T(8,128)}), f32[32,10,8,128]{3,2,1,0:T(8,128)S(1)}, u32[]{:S(2)}, u32[]{:S(2)}) async-start(f32[32,10,8,128]{3,2,1,0:T(8,128)} %shard_map.137), calls=%async_computation | async-start | bytes 2621440 | tf_op jit(solution)/shard_map/all_to_all | solution.py:536
  49.2 26.6 %all-to-all-start.1 = ((f32[256,1,128]{2,1,0:T(1,128)}), f32[256,1,128]{2,1,0:T(1,128)S(1)}, u32[]{:S(2)}, u32[]{:S(2)}) async-start(f32[256,1,128]{2,1,0:T(1,128)} %bitcast.10), calls=%async_computation.1 | async-start | bytes 262144 | tf_op jit(solution)/shard_map/all_to_all | solution.py:531
  61.6 13.7 %collective-permute-start.1 = (f32[16,8,128]{2,1,0:T(8,128)S(1)}, f32[16,8,128]{2,1,0:T(8,128)S(1)}, u32[]{:S(2)}, u32[]{:S(2)}) collective-permute-start(f32[16,8,128]{2,1,0:T(8,128)S(1)} %get-tuple-element.103), channel_id=1, source_target_pairs={{0,32},{1,33},{2,34},{3,35},{4,36},{5,37},{6,38},{7,39},{8,40},{9,... | collective-permute-start | bytes 196616 | tf_op jit(solution)/shard_map/ppermute | solution.py:547
  65.0 10.2 %collective-permute-start.2 = (f32[16,8,128]{2,1,0:T(8,128)S(1)}, f32[16,8,128]{2,1,0:T(8,128)S(1)}, u32[]{:S(2)}, u32[]{:S(2)}) collective-permute-start(f32[16,8,128]{2,1,0:T(8,128)S(1)} %get-tuple-element.104), channel_id=1, source_target_pairs={{32,0},{33,1},{34,2},{35,3},{36,4},{37,5},{38,6},{39,7},{40,8},{41... | collective-permute-start | bytes 196616 | tf_op jit(solution)/shard_map/ppermute | solution.py:547
  66.3 5.6 %collective-permute-start.3 = (f32[2,32,128]{2,1,0:T(8,128)S(1)}, f32[2,32,128]{2,1,0:T(8,128)S(1)}, u32[]{:S(2)}, u32[]{:S(2)}) collective-permute-start(f32[2,32,128]{2,1,0:T(8,128)S(1)} %get-tuple-element.105.last), channel_id=1, source_target_pairs={{0,1},{1,4},{4,5},{5,8},{8,9},{9,12},{12,13},{13,28},{28,29},{29,2... | collective-permute-start | bytes 98312 | tf_op jit(solution)/shard_map/ppermute | solution.py:557
  70.0 5.2 %collective-permute-start.4 = (f32[2,32,128]{2,1,0:T(8,128)S(1)}, f32[2,32,128]{2,1,0:T(8,128)S(1)}, u32[]{:S(2)}, u32[]{:S(2)}) collective-permute-start(f32[2,32,128]{2,1,0:T(8,128)S(1)} %get-tuple-element.106.first), channel_id=1, source_target_pairs={{1,0},{4,1},{5,4},{8,5},{9,8},{12,9},{13,12},{28,13},{29,28},{24,2... | collective-permute-start | bytes 98312 | tf_op jit(solution)/shard_map/ppermute | solution.py:557
  77.2 31.6 %all-to-all-start.2 = ((f32[256,1,128]{2,1,0:T(1,128)}), f32[256,1,128]{2,1,0:T(1,128)S(1)}, u32[]{:S(2)}, u32[]{:S(2)}) async-start(f32[256,1,128]{2,1,0:T(1,128)} %bitcast.13), calls=%async_computation.2 | async-start | bytes 262144 | tf_op jit(solution)/shard_map/all_to_all | solution.py:531
  92.4 13.7 %collective-permute-start.5 = (f32[16,8,128]{2,1,0:T(8,128)S(1)}, f32[16,8,128]{2,1,0:T(8,128)S(1)}, u32[]{:S(2)}, u32[]{:S(2)}) collective-permute-start(f32[16,8,128]{2,1,0:T(8,128)S(1)} %get-tuple-element.116), channel_id=1, source_target_pairs={{0,32},{1,33},{2,34},{3,35},{4,36},{5,37},{6,38},{7,39},{8,40},{9,... | collective-permute-start | bytes 196616 | tf_op jit(solution)/shard_map/ppermute | solution.py:547
  95.8 10.2 %collective-permute-start.6 = (f32[16,8,128]{2,1,0:T(8,128)S(1)}, f32[16,8,128]{2,1,0:T(8,128)S(1)}, u32[]{:S(2)}, u32[]{:S(2)}) collective-permute-start(f32[16,8,128]{2,1,0:T(8,128)S(1)} %get-tuple-element.117), channel_id=1, source_target_pairs={{32,0},{33,1},{34,2},{35,3},{36,4},{37,5},{38,6},{39,7},{40,8},{41... | collective-permute-start | bytes 196616 | tf_op jit(solution)/shard_map/ppermute | solution.py:547
  97.1 5.6 %collective-permute-start.7 = (f32[2,32,128]{2,1,0:T(8,128)S(1)}, f32[2,32,128]{2,1,0:T(8,128)S(1)}, u32[]{:S(2)}, u32[]{:S(2)}) collective-permute-start(f32[2,32,128]{2,1,0:T(8,128)S(1)} %get-tuple-element.118.last), channel_id=1, source_target_pairs={{0,1},{1,4},{4,5},{5,8},{8,9},{9,12},{12,13},{13,28},{28,29},{29,2... | collective-permute-start | bytes 98312 | tf_op jit(solution)/shard_map/ppermute | solution.py:557
  100.8 5.2 %collective-permute-start.8 = (f32[2,32,128]{2,1,0:T(8,128)S(1)}, f32[2,32,128]{2,1,0:T(8,128)S(1)}, u32[]{:S(2)}, u32[]{:S(2)}) collective-permute-start(f32[2,32,128]{2,1,0:T(8,128)S(1)} %get-tuple-element.119.first), channel_id=1, source_target_pairs={{1,0},{4,1},{5,4},{8,5},{9,8},{12,9},{13,12},{28,13},{29,28},{24,2... | collective-permute-start | bytes 98312 | tf_op jit(solution)/shard_map/ppermute | solution.py:557
  110.3 13.0 %collective-permute-start.9 = (f32[16,8,128]{2,1,0:T(8,128)S(1)}, f32[16,8,128]{2,1,0:T(8,128)S(1)}, u32[]{:S(2)}, u32[]{:S(2)}) collective-permute-start(f32[16,8,128]{2,1,0:T(8,128)S(1)} %get-tuple-element.127), channel_id=1, source_target_pairs={{0,32},{1,33},{2,34},{3,35},{4,36},{5,37},{6,38},{7,39},{8,40},{9,... | collective-permute-start | bytes 196616 | tf_op jit(solution)/shard_map/ppermute | solution.py:547
  114.5 8.7 %collective-permute-start.10 = (f32[16,8,128]{2,1,0:T(8,128)S(1)}, f32[16,8,128]{2,1,0:T(8,128)S(1)}, u32[]{:S(2)}, u32[]{:S(2)}) collective-permute-start(f32[16,8,128]{2,1,0:T(8,128)S(1)} %get-tuple-element.128), channel_id=1, source_target_pairs={{32,0},{33,1},{34,2},{35,3},{36,4},{37,5},{38,6},{39,7},{40,8},{41... | collective-permute-start | bytes 196616 | tf_op jit(solution)/shard_map/ppermute | solution.py:547
  159.6 22.1 %all-to-all-start.4 = ((f32[256,1,128]{2,1,0:T(1,128)}), f32[256,1,128]{2,1,0:T(1,128)S(1)}, u32[]{:S(2)}, u32[]{:S(2)}) async-start(f32[256,1,128]{2,1,0:T(1,128)} %bitcast.19), calls=%async_computation.4 | async-start | bytes 262144 | tf_op jit(solution)/shard_map/all_to_all | solution.py:531
  165.0 13.8 %collective-permute-start.13 = (f32[16,8,128]{2,1,0:T(8,128)S(1)}, f32[16,8,128]{2,1,0:T(8,128)S(1)}, u32[]{:S(2)}, u32[]{:S(2)}) collective-permute-start(f32[16,8,128]{2,1,0:T(8,128)S(1)} %get-tuple-element.145), channel_id=1, source_target_pairs={{0,32},{1,33},{2,34},{3,35},{4,36},{5,37},{6,38},{7,39},{8,40},{9,... | collective-permute-start | bytes 196616 | tf_op jit(solution)/shard_map/ppermute | solution.py:547
  168.6 10.2 %collective-permute-start.14 = (f32[16,8,128]{2,1,0:T(8,128)S(1)}, f32[16,8,128]{2,1,0:T(8,128)S(1)}, u32[]{:S(2)}, u32[]{:S(2)}) collective-permute-start(f32[16,8,128]{2,1,0:T(8,128)S(1)} %get-tuple-element.146), channel_id=1, source_target_pairs={{32,0},{33,1},{34,2},{35,3},{36,4},{37,5},{38,6},{39,7},{40,8},{41... | collective-permute-start | bytes 196616 | tf_op jit(solution)/shard_map/ppermute | solution.py:547
  169.9 5.8 %collective-permute-start.15 = (f32[2,32,128]{2,1,0:T(8,128)S(1)}, f32[2,32,128]{2,1,0:T(8,128)S(1)}, u32[]{:S(2)}, u32[]{:S(2)}) collective-permute-start(f32[2,32,128]{2,1,0:T(8,128)S(1)} %get-tuple-element.147.last), channel_id=1, source_target_pairs={{0,1},{1,4},{4,5},{5,8},{8,9},{9,12},{12,13},{13,28},{28,29},{29,2... | collective-permute-start | bytes 98312 | tf_op jit(solution)/shard_map/ppermute | solution.py:557
  183.6 32.2 %all-to-all-start.5 = ((f32[256,1,128]{2,1,0:T(1,128)}), f32[256,1,128]{2,1,0:T(1,128)S(1)}, u32[]{:S(2)}, u32[]{:S(2)}) async-start(f32[256,1,128]{2,1,0:T(1,128)} %bitcast.22), calls=%async_computation.5 | async-start | bytes 262144 | tf_op jit(solution)/shard_map/all_to_all | solution.py:531
  198.8 13.7 %collective-permute-start.17 = (f32[16,8,128]{2,1,0:T(8,128)S(1)}, f32[16,8,128]{2,1,0:T(8,128)S(1)}, u32[]{:S(2)}, u32[]{:S(2)}) collective-permute-start(f32[16,8,128]{2,1,0:T(8,128)S(1)} %get-tuple-element.158), channel_id=1, source_target_pairs={{0,32},{1,33},{2,34},{3,35},{4,36},{5,37},{6,38},{7,39},{8,40},{9,... | collective-permute-start | bytes 196616 | tf_op jit(solution)/shard_map/ppermute | solution.py:547
  202.3 10.2 %collective-permute-start.18 = (f32[16,8,128]{2,1,0:T(8,128)S(1)}, f32[16,8,128]{2,1,0:T(8,128)S(1)}, u32[]{:S(2)}, u32[]{:S(2)}) collective-permute-start(f32[16,8,128]{2,1,0:T(8,128)S(1)} %get-tuple-element.159), channel_id=1, source_target_pairs={{32,0},{33,1},{34,2},{35,3},{36,4},{37,5},{38,6},{39,7},{40,8},{41... | collective-permute-start | bytes 196616 | tf_op jit(solution)/shard_map/ppermute | solution.py:547
  203.6 5.6 %collective-permute-start.19 = (f32[2,32,128]{2,1,0:T(8,128)S(1)}, f32[2,32,128]{2,1,0:T(8,128)S(1)}, u32[]{:S(2)}, u32[]{:S(2)}) collective-permute-start(f32[2,32,128]{2,1,0:T(8,128)S(1)} %get-tuple-element.160.last), channel_id=1, source_target_pairs={{0,1},{1,4},{4,5},{5,8},{8,9},{9,12},{12,13},{13,28},{28,29},{29,2... | collective-permute-start | bytes 98312 | tf_op jit(solution)/shard_map/ppermute | solution.py:557
  217.0 13.0 %collective-permute-start.21 = (f32[16,8,128]{2,1,0:T(8,128)S(1)}, f32[16,8,128]{2,1,0:T(8,128)S(1)}, u32[]{:S(2)}, u32[]{:S(2)}) collective-permute-start(f32[16,8,128]{2,1,0:T(8,128)S(1)} %get-tuple-element.169), channel_id=1, source_target_pairs={{0,32},{1,33},{2,34},{3,35},{4,36},{5,37},{6,38},{7,39},{8,40},{9,... | collective-permute-start | bytes 196616 | tf_op jit(solution)/shard_map/ppermute | solution.py:547
  221.3 8.7 %collective-permute-start.22 = (f32[16,8,128]{2,1,0:T(8,128)S(1)}, f32[16,8,128]{2,1,0:T(8,128)S(1)}, u32[]{:S(2)}, u32[]{:S(2)}) collective-permute-start(f32[16,8,128]{2,1,0:T(8,128)S(1)} %get-tuple-element.170), channel_id=1, source_target_pairs={{32,0},{33,1},{34,2},{35,3},{36,4},{37,5},{38,6},{39,7},{40,8},{41... | collective-permute-start | bytes 196616 | tf_op jit(solution)/shard_map/ppermute | solution.py:547
  262.4 19.8 %all-to-all-start.6 = ((f32[32,7,8,128]{3,2,1,0:T(8,128)}), f32[32,7,8,128]{3,2,1,0:T(8,128)S(1)}, u32[]{:S(2)}, u32[]{:S(2)}) async-start(f32[32,7,8,128]{3,2,1,0:T(8,128)} %get-tuple-element.178), calls=%async_computation.6 | async-start | bytes 1835008 | tf_op jit(solution)/shard_map/all_to_all | solution.py:536
  (45 other events, 482.4 us)

commit v3 on v2

--- a/solution.py
+++ b/solution.py
@@ -28,8 +28,9 @@
 BOUND, SHARE, RIM, EXTRA, BLOCK = 5, 6, 7, 8, 9
 SLOTS = 10
 LANE_PRIMAL, LANE_DUAL, LANE_TONS = 40, 41, 42
-HALO, EDGES, TONS, VALUE = 5, 6, 7, 8
-PLANES = 9
+HALO, EDGES, TONS, VALUE, ODD_X, ODD_Y = 5, 6, 7, 8, 9, 10
+PLANES = 11
+ROW = 7
 
 
 def member(tile):
@@ -92,7 +93,41 @@
     return jnp.where(low(), one, turn(two)), jnp.where(low(), turn(one), two)
 
 
-def pack_kernel(place, caps, limits, density, slope, ton_class, value, share, prec, bound, rim, out):
+def fetch(pairs, sems):
+    copies = [
+        pltpu.make_async_copy(source, target, sems.at[n]) for n, (source, target) in enumerate(pairs)
+    ]
+    for copy in copies:
+        copy.start()
+    return copies
+
+
+def put_tiles(source, target):
+    one = jnp.concatenate([source(0), source(1)], axis=0).T
+    two = jnp.concatenate([source(2), source(3)], axis=0).T
+    for m in range(TILES // 2):
+        here = slice(8 * m, 8 * m + 8)
+        even, odd = mix(one[here], two[here])
+        target(member(2 * m), even)
+        target(member(2 * m + 1), odd)
+
+
+def pack_kernel(
+    small, place, slope_at, ton_class_at, value_at, share_at, prec_at, bound_at,
+    out, slope, ton_class, value, share, prec, bound, sems,
+):
+    copies = fetch(
+        [
+            (slope_at, slope), (ton_class_at, ton_class), (value_at, value), (prec_at, prec),
+            (bound_at, bound), (share_at, share),
+        ],
+        sems,
+    )
+    caps = [small[t] for t in range(4)]
+    limits = [small[4 + t] for t in range(4)]
+    density = [small[8 + c] for c in range(8)]
+    for copy in copies:
+        copy.wait()
     x = place[0]
     row = (1, 128)
     code = slope[...]
@@ -107,19 +142,15 @@
     top = subs((NZ, NY)) == 0
 
     def put(field, source):
-        one = jnp.concatenate([source(0), source(1)], axis=0).T
-        two = jnp.concatenate([source(2), source(3)], axis=0).T
-        for m in range(TILES // 2):
-            here = slice(8 * m, 8 * m + 8)
-            even, odd = mix(one[here], two[here])
-            out[member(2 * m), field] = even
-            out[member(2 * m + 1), field] = odd
+        def target(slot, tile):
+            out[slot, field] = tile
+
+        put_tiles(source, target)
 
     for k in range(ARCS):
         put(k, lambda t, k=k: jnp.where(top, mask[k], prec[k, t]))
     put(BOUND, lambda t: bound[t])
     put(SHARE, lambda t: share[t])
-    put(RIM, lambda t: rim[t])
     classes = ton_class[...]
     tons = jnp.zeros(classes.shape, F32)
     for c in range(8):
@@ -146,6 +177,16 @@
             out[i, EXTRA, 6 + a : 7 + a] = limit_rows[a]
 
 
+def rim_kernel(rim, send, out, tiles, sem):
+    def target(slot, tile):
+        tiles[slot] = tile
+
+    put_tiles(lambda t: rim[t], target)
+    copy = pltpu.make_async_copy(tiles, out.at[:, RIM], sem)
+    copy.start()
+    copy.wait()
+
+
 def adjoint_row(prices, bound, halo, edges, r, carry):
     shape = (8, 128)
     sub = subs(shape)
@@ -162,8 +203,13 @@
     return carry + jnp.where(later_half(shape), g, pair), carry + pair
 
 
-def unpack_kernel(got, prices, halos, edges, bound, share, caps, limits, tail, masks):
+def unpack_kernel(
+    small, place, got, prices, halos, edges, bound, share, caps, limits, tail, masks, weight
+):
     shape = (8, 128)
+    weight[...] = jnp.full(shape, small[16])
+    masks[ODD_X] = jnp.full(shape, place[0] // 2 % 2).astype(F32)
+    masks[ODD_Y] = jnp.full(shape, place[1] % 2).astype(F32)
     lane = lanes(shape)
     deep = ((lane & 63) >= 1).astype(F32)
     half = later_half(shape)
@@ -237,7 +283,7 @@
 
 
 def primal_step(
-    caps, tail, share, planes, weight, new, head, low_rows, high_rows,
+    caps, tail, share, planes, weight, new, head, x_one, x_two, y_one, y_two,
     first, last, row, cap_rows, rate_rows,
 ):
     shape = (8, 128)
@@ -249,6 +295,8 @@
     rate_rows[0] = jnp.exp(-RATE * periods)
     rate_rows[1] = SLOPE * (NP - periods)
     half = later_half(shape)
+    odd_x = planes[ODD_X] > 0.5
+    odd_y = planes[ODD_Y, 0:1] > 0.5
     carry = jnp.zeros(shape, F32)
     mined = []
     for r in range(ROWS):
@@ -269,8 +317,13 @@
         if r % 2 == 0:
             even = cumulative
         else:
-            low_rows[r // 2], high_rows[r // 2] = mix(even, cumulative)
+            lows, highs = mix(even, cumulative)
+            x_one[r // 2] = jnp.where(odd_x, lows, highs)
+            x_two[r // 2] = jnp.where(odd_x, highs, lows)
         mined.append(tons * ahead)
+    for x in range(2):
+        y_one[x] = jnp.where(odd_y, first[x], last[x])
+        y_two[x] = jnp.where(odd_y, last[x], first[x])
     mined.append(tons)
     sums = half_sums(jnp.concatenate(mined, axis=0))
     lane = lanes(shape)
@@ -281,56 +334,62 @@
 
 
 def primal_first_kernel(caps, tail, share, planes, weight, *rest):
-    primal_step(caps[...], tail, share, planes, weight[...], *rest)
+    primal_step(caps[...], tail, share, planes, weight[0:1], *rest)
 
 
 def primal_kernel(got, caps, limits, tail, share, planes, weight, caps_new, *rest):
     row = summed_row(got)
-    caps_now = caps_after(row, caps[...], limits[...], weight[...])
+    caps_now = caps_after(row, caps[...], limits[...], weight[0:1])
     caps_new[...] = caps_now
-    primal_step(caps_now, tail, share, planes, weight[...], *rest)
-
-
-def restart(got, caps0, caps1, caps2, limits, weight):
-    row = summed_row(got)
-    caps3 = caps_after(row, caps2[...], limits[...], weight[...])
+    primal_step(caps_now, tail, share, planes, weight[0:1], *rest)
+
+
+def restart(row, caps0, caps1, caps2, limits, weight):
+    caps3 = caps_after(row, caps2[...], limits[...], weight[0:1])
     mean = (caps1[...] + caps2[...] + caps3) / INNER
-    return mean, weight_after(row, weight[...], mean, caps0[...])
+    return mean, weight_after(row, weight[0:1], mean, caps0[...])
 
 
 def primal_restart_kernel(
     got, caps0, caps1, caps2, limits, tail, share, planes, weight, caps_new, weight_new, *rest
 ):
-    mean, new = restart(got, caps0, caps1, caps2, limits, weight)
+    mean, new = restart(summed_row(got), caps0, caps1, caps2, limits, weight)
     caps_new[...] = mean
-    weight_new[...] = new
+    weight_new[...] = jnp.broadcast_to(new, weight_new.shape)
     primal_step(mean, tail, share, planes, new, *rest)
 
 
 def finish_kernel(got, caps0, caps1, caps2, limits, weight, caps_new, weight_new):
-    mean, new = restart(got, caps0, caps1, caps2, limits, weight)
+    row = jnp.sum(got[...], axis=0, keepdims=True)
+    mean, new = restart(row, caps0, caps1, caps2, limits, weight)
     caps_new[...] = mean
-    weight_new[...] = new
-
-
-def dual_rows(weight, planes, front, back, first, last, edges, steps, ahead):
+    weight_new[...] = jnp.broadcast_to(new, weight_new.shape)
+
+
+def dual_rows(weight, planes, y_one, y_two, first, last, edges, steps, ahead):
+    odd_y = planes[ODD_Y, 0:1] > 0.5
     periods = period_table()
-    steps[0] = weight[...] / (2.0 * (periods + 1.0))
-    steps[1] = weight[...] / (periods + 1.0)
+    steps[0] = weight[0:1] / (2.0 * (periods + 1.0))
+    steps[1] = weight[0:1] / (periods + 1.0)
     new = []
-    for n, outside, inside in ((0, front, first), (1, back, last)):
+    for n, inside in ((0, first), (1, last)):
         new.append([])
         for x in range(2):
             at = 2 * n + x
-            there = outside[x]
+            before = jnp.where(odd_y, y_one[x], y_two[x])
+            after = jnp.where(odd_y, y_two[x], y_one[x])
+            there = after if n else before
             ahead[n, x] = down(there)
             price = edges[n, x] + steps[0] * (there - down(inside[x]))
             new[n].append(jnp.maximum(price, 0.0) * planes[EDGES, at : at + 1])
     return new
 
 
-def dual_pair(s, planes, head, lower, upper, prices, halos, bound, steps, ahead_rows):
-    outside = mix(lower[s], upper[s])
+def dual_pair(s, planes, head, x_one, x_two, prices, halos, bound, steps, ahead_rows):
+    odd = planes[ODD_X] > 0.5
+    lower = jnp.where(odd, x_one[s], x_two[s])
+    upper = jnp.where(odd, x_two[s], x_one[s])
+    outside = mix(lower, upper)
     return [
         dual_row(2 * s + a, outside[a], planes, head, prices, halos, bound, steps, ahead_rows)
         for a in range(2)
@@ -367,16 +426,16 @@
 
 
 def dual_kernel(
-    weight, planes, head, lower, upper, front, back, first, last, prices, halos, edges, bound,
+    weight, planes, head, x_one, x_two, y_one, y_two, first, last, prices, halos, edges, bound,
     prices_new, halos_new, edges_new, bound_new, tail, steps, ahead,
 ):
-    new = dual_rows(weight, planes, front, back, first, last, edges, steps, ahead)
+    new = dual_rows(weight, planes, y_one, y_two, first, last, edges, steps, ahead)
     for n in range(2):
         for x in range(2):
             edges_new[n, x] = new[n][x]
     carry = jnp.zeros((8, 128), F32)
     for s in reversed(range(ROWS // 2)):
-        both = dual_pair(s, planes, head, lower, upper, prices, halos, bound, steps, ahead)
+        both = dual_pair(s, planes, head, x_one, x_two, prices, halos, bound, steps, ahead)
         for a in (1, 0):
             r = 2 * s + a
             p, b, h = both[a]
@@ -391,23 +450,28 @@
     return (one + two + three) / INNER
 
 
-def moves_kernel(moves, row, row_new):
+def with_moves(row, primal_move, dual_move):
     lane = lanes((1, 128))
 
     def whole(v):
         return jnp.sum(jnp.sum(v, axis=0, keepdims=True), axis=1, keepdims=True)
 
-    new = row[0:1] + jnp.where(lane == LANE_PRIMAL, whole(moves[0]), 0.0)
-    new = new + jnp.where(lane == LANE_DUAL, whole(moves[1]), 0.0)
-    row_new[...] = jnp.broadcast_to(new, row_new.shape)
+    new = row[0:1] + jnp.where(lane == LANE_PRIMAL, whole(primal_move), 0.0)
+    return new + jnp.where(lane == LANE_DUAL, whole(dual_move), 0.0)
 
 
 def dual_restart_kernel(
-    weight, planes, head, lower, upper, front, back, first, last, prices, halos, edges, bound,
-    prices0, prices1, halos1, edges1, bound0, bound1, share0, share1, share2, share3, row,
-    prices_new, halos_new, edges_new, bound_new, tail, share_new, row_new, steps, ahead, moves,
+    weight, planes, head, x_one, x_two, y_one, y_two, first, last, prices, halos, edges, bound,
+    row, share3, *rest,
 ):
-    new = dual_rows(weight, planes, front, back, first, last, edges, steps, ahead)
+    olds, rest = rest[:9], rest[9:]
+    prices_new, halos_new, edges_new, bound_new, tail, share_new, row_new, steps, ahead = rest[:9]
+    sems, fetched = rest[9], rest[10:]
+    copies = fetch(zip(olds, fetched), sems)
+    prices0, prices1, bound0, bound1, share0, share1, share2, halos1, edges1 = fetched
+    new = dual_rows(weight, planes, y_one, y_two, first, last, edges, steps, ahead)
+    for copy in copies:
+        copy.wait()
     for n in range(2):
         for x in range(2):
             edges_new[n, x] = mean_of(edges1[n, x], edges[n, x], new[n][x])
@@ -416,7 +480,7 @@
     primal_move = jnp.zeros(shape, F32)
     dual_move = jnp.zeros(shape, F32)
     for s in reversed(range(ROWS // 2)):
-        both = dual_pair(s, planes, head, lower, upper, prices, halos, bound, steps, ahead)
+        both = dual_pair(s, planes, head, x_one, x_two, prices, halos, bound, steps, ahead)
         for a in (1, 0):
             r = 2 * s + a
             p, b, h = both[a]
@@ -433,21 +497,26 @@
             halos_new[r] = h
             share_new[r] = u
             tail[r], carry = adjoint_row(p, b, h, edges_new, r, carry)
-    moves[0] = primal_move
-    moves[1] = dual_move
-    moves_kernel(moves, row, row_new)
+    row_new[...] = jnp.broadcast_to(with_moves(row, primal_move, dual_move), row_new.shape)
 
 
 def dual_final_kernel(
-    weight, planes, head, lower, upper, front, back, first, last, prices, halos, edges, bound,
-    prices0, prices1, bound0, bound1, share0, share1, share2, share3, send, moves, steps, ahead,
+    weight, planes, head, x_one, x_two, y_one, y_two, first, last, prices, halos, edges, bound,
+    row, share3, *rest,
 ):
-    dual_rows(weight, planes, front, back, first, last, edges, steps, ahead)
+    olds, rest = rest[:7], rest[7:]
+    send, steps, ahead, sems = rest[:4]
+    fetched = rest[4:]
+    copies = fetch(zip(olds, fetched), sems)
+    prices0, prices1, bound0, bound1, share0, share1, share2 = fetched
+    dual_rows(weight, planes, y_one, y_two, first, last, edges, steps, ahead)
+    for copy in copies:
+        copy.wait()
     shape = (8, 128)
     primal_move = jnp.zeros(shape, F32)
     dual_move = jnp.zeros(shape, F32)
     for s in range(ROWS // 2):
-        both = dual_pair(s, planes, head, lower, upper, prices, halos, bound, steps, ahead)
+        both = dual_pair(s, planes, head, x_one, x_two, prices, halos, bound, steps, ahead)
         means = []
         for a in range(2):
             r = 2 * s + a
@@ -462,8 +531,16 @@
             means.append(p + [b, u])
         for field in range(7):
             send[s, field], send[16 + s, field] = mix(means[0][field], means[1][field])
-    moves[0] = primal_move
-    moves[1] = dual_move
+    tile = jnp.broadcast_to(with_moves(row, primal_move, dual_move), shape)
+    for i in range(TILES):
+        send[i, ROW] = tile
+
+
+def plane_sum_kernel(got, out):
+    total = got[0, ROW]
+    for i in range(1, TILES):
+        total = total + got[i, ROW]
+    out[...] = total
 
 
 def turn_back_kernel(got, share, prec, bound):
@@ -499,27 +576,38 @@
 
 VMEM = pl.BlockSpec(memory_space=pltpu.VMEM)
 SMEM = pl.BlockSpec(memory_space=pltpu.SMEM)
+ANY = pl.BlockSpec(memory_space=pl.ANY)
 FIELD = (ROWS, 8, 128)
 
 
-def call(kernel, outs, scratch=(), scalars=0):
+def call(kernel, outs, scratch=(), scalars=0, far=0, out_space=VMEM, aliases=None):
     def run(*args):
-        specs = [SMEM] * scalars + [VMEM] * (len(args) - scalars)
+        near = len(args) - scalars - far
         return pl.pallas_call(
             kernel,
             out_shape=[f32(*shape) for shape in outs],
-            in_specs=specs,
-            out_specs=[VMEM] * len(outs),
-            scratch_shapes=[pltpu.VMEM(shape, F32) for shape in scratch],
+            in_specs=[SMEM] * scalars + [VMEM] * near + [ANY] * far,
+            out_specs=[out_space] * len(outs),
+            scratch_shapes=[
+                pltpu.VMEM(shape, F32) if isinstance(shape, tuple) else shape for shape in scratch
+            ],
+            input_output_aliases=aliases or {},
             compiler_params=pltpu.CompilerParams(vmem_limit_bytes=12 * 1024 * 1024),
+            cost_estimate=pl.CostEstimate(
+                flops=10**6, bytes_accessed=4 * 10**6, transcendentals=0
+            ),
         )(*args)
 
     return run
+
+
+def semaphores(n):
+    return pltpu.SemaphoreType.DMA((n,))
 
 
 STEP_OUTS = [
     FIELD, FIELD, (ROWS // 2, 8, 128), (ROWS // 2, 8, 128), (2, ROWS, 128), (2, ROWS, 128),
-    (DEVICES, 128),
+    (2, ROWS, 128), (2, ROWS, 128), (DEVICES, 128),
 ]
 STEP_SCRATCH = [(ROWS, 128), (2, ROWS, 128)]
 DUAL_OUTS = [(ARCS,) + FIELD, FIELD, (2, 2, ROWS, 128), FIELD, FIELD]
@@ -531,38 +619,40 @@
     return lax.all_to_all(row, EVERY, 0, 0, tiled=True)
 
 
+def share_planes(row):
+    planes = DEVICES // PLANE
+    groups = [[PLANE * z + i for z in range(planes)] for i in range(PLANE)]
+    return lax.all_to_all(row, EVERY, 0, 0, axis_index_groups=groups, tiled=True)
+
+
 def exchange(slots):
     groups = [[PLANE * z + i for i in range(PLANE)] for z in range(DEVICES // PLANE)]
     return lax.all_to_all(slots, EVERY, 0, 0, axis_index_groups=groups)
 
 
-def along_x(value, by):
+def swap_x(value, odd):
     planes = DEVICES // PLANE
-    pairs = [
-        (PLANE * z + i, PLANE * (z + by) + i)
-        for z in range(planes)
-        if 0 <= z + by < planes
-        for i in range(PLANE)
-    ]
+    pairs = []
+    for z in range(planes):
+        other = z + 1 if z % 2 == odd else z - 1
+        if 0 <= other < planes:
+            pairs += [(PLANE * z + i, PLANE * other + i) for i in range(PLANE)]
     return lax.ppermute(value, EVERY, pairs)
 
 
-def along_y(value, by):
-    pairs = [
-        (PLANE * z + member(j), PLANE * z + member(j + by))
-        for z in range(DEVICES // PLANE)
-        for j in range(TILES)
-        if 0 <= j + by < TILES
-    ]
+def swap_y(value, odd):
+    pairs = []
+    for j in range(TILES):
+        other = j + 1 if j % 2 == odd else j - 1
+        if 0 <= other < TILES:
+            pairs += [
+                (PLANE * z + member(j), PLANE * z + member(other)) for z in range(DEVICES // PLANE)
+            ]
     return lax.ppermute(value, EVERY, pairs)
 
 
-def halo(low_rows, high_rows, first, last):
-    back = along_y(first, -1)
-    front = along_y(last, 1)
-    lower = along_x(high_rows, 1)
-    upper = along_x(low_rows, -1)
-    return lower, upper, front, back
+def halo(x_one, x_two, y_one, y_two):
+    return swap_x(x_one, 0), swap_x(x_two, 1), swap_y(y_one, 0), swap_y(y_two, 1)
 
 
 def per_device(
@@ -578,28 +668,47 @@
     omega_start,
 ):
     x, tile = lax.axis_index("strip"), lax.axis_index("period")
-    prec = dual_prec[:, 0]
-    top = (jnp.arange(NZ) == 0)[None, :, None]
-    toward = ((slope_code & 1) * (x + 1 < NX)).astype(F32)[None]
-    away = ((slope_code // 2 & 1) * (x >= 1)).astype(F32)[None]
-    odd = x % 2 == 1
-    rim = jnp.where(top, jnp.where(odd, toward, away), jnp.where(odd, prec[1], prec[2]))
+    arc = 2 - x % 2
+    inside = jnp.where(x % 2 == 1, x + 1 < NX, x >= 1)
+    toward = jnp.where(inside, slope_code >> (arc - 1) & 1, 0).astype(F32)[None]
+    top = lax.broadcasted_iota(jnp.int32, (4, NZ, NY), 1) == 0
+    rim = jnp.where(top, toward, lax.dynamic_index_in_dim(dual_prec[:, 0], arc, 0, False))
     swaps = [(i, i + 1 if i % 2 else i - 1) for i in range(1, NX - 1)]
     rim = lax.ppermute(rim, "strip", swaps)
-    place = jnp.reshape(x, (1,)).astype(jnp.int32)
-    (send,) = call(pack_kernel, [(TILES, SLOTS, 8, 128)], (), 4)(
-        place, dual_cap, capacity, density, slope_code, ton_class[0], block_value[0],
-        u_start[0], prec, dual_bound[0], rim,
+    place = jnp.stack([x, tile]).astype(jnp.int32)
+    small = jnp.concatenate([dual_cap, capacity, density, omega_start])
+    plane = (NZ, NY)
+    slots = (TILES, SLOTS, 8, 128)
+    (send,) = call(
+        pack_kernel,
+        [slots],
+        [
+            pltpu.VMEM((1, NY), jnp.int32), pltpu.VMEM(plane, jnp.int32), plane, (4,) + plane,
+            (ARCS, 4) + plane, (4,) + plane, semaphores(6),
+        ],
+        scalars=2,
+        far=6,
+    )(
+        small, place, slope_code, ton_class[0], block_value[0], u_start[0], dual_prec[:, 0],
+        dual_bound[0],
     )
+    (send,) = call(
+        rim_kernel,
+        [slots],
+        [(TILES, 8, 128), pltpu.SemaphoreType.DMA],
+        far=1,
+        out_space=ANY,
+        aliases={1: 0},
+    )(rim, send)
     got = exchange(send)
-    prices, halos, edges, bound, share, caps, limits, tail, planes = call(
+    prices, halos, edges, bound, share, caps, limits, tail, planes, weight = call(
         unpack_kernel,
         [
             (ARCS,) + FIELD, FIELD, (2, 2, ROWS, 128), FIELD, FIELD, (ROWS, 128), (ROWS, 128),
-            FIELD, (PLANES, 8, 128),
+            FIELD, (PLANES, 8, 128), (8, 128),
         ],
-    )(got)
-    weight = jnp.reshape(omega_start, (1, 1))
+        scalars=2,
+    )(small, place, got)
     row_sums = None
     old_caps = None
     for outer in range(OUTER):
@@ -607,23 +716,23 @@
         price_list, halo_list, edge_list, bound_list = [prices], [halos], [edges], [bound]
         for inner in range(INNER):
             if inner == 0 and outer == 0:
-                new, head, low_rows, high_rows, first, last, row = call(
+                new, head, *sides, first, last, row = call(
                     primal_first_kernel, STEP_OUTS, STEP_SCRATCH
                 )(caps, tail, share, planes, weight)
             elif inner == 0:
-                caps, weight, new, head, low_rows, high_rows, first, last, row = call(
-                    primal_restart_kernel, [(ROWS, 128), (1, 1)] + STEP_OUTS, STEP_SCRATCH
+                caps, weight, new, head, *sides, first, last, row = call(
+                    primal_restart_kernel, [(ROWS, 128), (8, 128)] + STEP_OUTS, STEP_SCRATCH
                 )(row_sums, *old_caps, limits, tail, share, planes, weight)
             else:
-                caps, new, head, low_rows, high_rows, first, last, row = call(
+                caps, new, head, *sides, first, last, row = call(
                     primal_kernel, [(ROWS, 128)] + STEP_OUTS, STEP_SCRATCH
                 )(row_sums, caps, limits, tail, share, planes, weight)
             caps_list.append(caps)
             shares.append(new)
             share = new
-            lower, upper, front, back = halo(low_rows, high_rows, first, last)
+            sides = halo(*sides)
             common = (
-                weight, planes, head, lower, upper, front, back, first, last,
+                weight, planes, head, *sides, first, last,
                 prices, halos, edges, bound,
             )
             if inner < INNER - 1:
@@ -636,29 +745,34 @@
                 edge_list.append(edges)
                 bound_list.append(bound)
             elif outer < OUTER - 1:
+                olds = [
+                    price_list[0], price_list[1], bound_list[0], bound_list[1], *shares[:3],
+                    halo_list[1], edge_list[1],
+                ]
                 prices, halos, edges, bound, tail, share, row = call(
-                    dual_restart_kernel, DUAL_OUTS + [FIELD, (DEVICES, 128)],
-                    DUAL_SCRATCH + [(2, 8, 128)],
-                )(
-                    *common, price_list[0], price_list[1], halo_list[1], edge_list[1],
-                    bound_list[0], bound_list[1], *shares, row,
-                )
+                    dual_restart_kernel,
+                    DUAL_OUTS + [FIELD, (DEVICES, 128)],
+                    DUAL_SCRATCH + [semaphores(9)] + [old.shape for old in olds],
+                    far=9,
+                )(*common, row, new, *olds)
                 row_sums = share_row(row)
                 old_caps = caps_list
             else:
-                send, moves = call(
-                    dual_final_kernel, [(TILES, 7, 8, 128), (2, 8, 128)], DUAL_SCRATCH
-                )(
-                    *common, price_list[0], price_list[1], bound_list[0], bound_list[1], *shares,
-                )
+                olds = [price_list[0], price_list[1], bound_list[0], bound_list[1], *shares[:3]]
+                (send,) = call(
+                    dual_final_kernel,
+                    [(TILES, ROW + 1, 8, 128)],
+                    DUAL_SCRATCH + [semaphores(7)] + [old.shape for old in olds],
+                    far=7,
+                )(*common, row, new, *olds)
                 got = exchange(send)
-                (row,) = call(moves_kernel, [(DEVICES, 128)])(moves, row)
-                row_sums = share_row(row)
+                (row,) = call(plane_sum_kernel, [(8, 128)])(got)
+                row_sums = share_planes(row)
                 old_caps = caps_list
     mined, arcs, bounds = call(
         turn_back_kernel, [(4, NZ, NY), (ARCS, 4, NZ, NY), (4, NZ, NY)]
     )(got)
-    caps, weight = call(finish_kernel, [(ROWS, 128), (1, 1)])(
+    caps, weight = call(finish_kernel, [(ROWS, 128), (8, 128)])(
         row_sums, *old_caps, limits, weight
     )
     own = lax.dynamic_slice(caps, (2 * tile, 0), (2, 128))[:, ::64]
@@ -667,7 +781,7 @@
         arcs[:, None],
         bounds[None],
         jnp.reshape(own, (4,)),
-        jnp.reshape(weight, (1,)),
+        weight[0, 0:1],
     )
 
 

time: 285 us -> 239 us (0.84)
  starting transfers between devices: 130 us -> 82.8 us
  blocking collectives: 58.8 us -> 82.2 us
  waiting for transfers between devices: 52.1 us -> 29.7 us
    all_to_all x0 -> x2, blocking collectives: none -> 55.6 us  [exchange(): return lax.all_to_all(slots, EVERY, 0, 0, axis_index_groups=groups)]
    all_to_all x2 -> x1, blocking collectives: 58.8 us -> 26.6 us  [share_row(): return lax.all_to_all(row, EVERY, 0, 0, tiled=True)]
    all_to_all x2 -> x1, waiting for transfers between devices: 32.9 us -> 5.38 us  [share_planes(): lax.all_to_all(row, EVERY, 0, 0, axis_index_groups=groups, tiled=True)]
    ppermute x24, starting transfers between devices: 61.3 us -> 37.6 us  [the longest x12 22 us: swap_y(): return lax.ppermute(value, EVERY, pairs)]
    all_to_all x2 -> x1, starting transfers between devices: 19.7 us -> 7.59 us  [share_planes(): lax.all_to_all(row, EVERY, 0, 0, axis_index_groups=groups, tiled=True)]
    all_to_all x4, starting transfers between devices: 48.3 us -> 36.9 us  [share_row(): return lax.all_to_all(row, EVERY, 0, 0, tiled=True)]
    all_to_all x4, waiting for transfers between devices: 0.01 us -> 10.4 us  [share_row(): return lax.all_to_all(row, EVERY, 0, 0, tiled=True)]
    ppermute x24, waiting for transfers between devices: 19.2 us -> 13.9 us  [the longest x12 13.9 us: swap_y(): return lax.ppermute(value, EVERY, pairs)]
  transfers between devices with their start and end apart: 31 -> 30, of which waited for: 8 -> 11; matrix products, arithmetic and copies ran while one was open for 0% -> 0% of each run, Pallas kernels for 2% -> 2%
where the time goes in v3:
time: 239 us; the launch traced here: 238 us
  starting transfers between devices  82.8 us (35%)
  blocking collectives  82.2 us (34%)
  waiting for transfers between devices  29.7 us (12%)
  local copies, waits for them, and re-layouts  20.9 us (9%)
  Pallas kernels  17.9 us (7%)
  other arithmetic  2.49 us (1%)
    all_to_all x2, blocking collectives, exchange(): return lax.all_to_all(slots, EVERY, 0, 0, axis_index_groups=groups)  55.6 us
    all_to_all x4, starting transfers between devices, share_row(): return lax.all_to_all(row, EVERY, 0, 0, tiled=True)  36.9 us
    all_to_all x1, blocking collectives, share_row(): return lax.all_to_all(row, EVERY, 0, 0, tiled=True)  26.6 us
    ppermute x12, starting transfers between devices, swap_y(): return lax.ppermute(value, EVERY, pairs)  22 us
    unnamed x66, local copies, waits for them, and re-layouts  19.6 us
    pallas_call x18, Pallas kernels, run(): pl.pallas_call(kernel, out_shape=[f32(*shape) for shape in outs], in_spec...  17.9 us
    ppermute x12, starting transfers between devices, swap_x(): return lax.ppermute(value, EVERY, pairs)  15.6 us
    ppermute x12, waiting for transfers between devices, swap_y(): return lax.ppermute(value, EVERY, pairs)  13.9 us
  transfers between devices with their start and end apart: 30, of which 11 were waited for; matrix products, arithmetic and copies ran while one was open for 0% of the time, Pallas kernels for 2%

profile of v3, /device:TPU:1, one launch (start us, length us, event | category | flops | bytes accessed | tf_op | source)
XLA Modules:
  0.0 237.6 jit_solution(9361149499317306915)
XLA Ops:
  11.3 31.6 %all_to_all.76.got = f32[32,10,8,128]{3,2,1,0:T(8,128)S(1)} all-to-all(f32[32,10,8,128]{3,2,1,0:T(8,128)S(1)} %shard_map.138), channel_id=1, replica_groups={{0,1,2,3,4,5,6,7,8,9,10,11,12,13,14,15,16,17,18,19,20,21,22,23,24,25,26..., dimensions={0} | all-to-all | bytes 2621440 | tf_op jit(solution)/shard_map/all_to_all | solution.py:630
  44.9 10.2 %all-to-all-start.1 = ((f32[256,1,128]{2,1,0:T(1,128)}), f32[256,1,128]{2,1,0:T(1,128)S(1)}, u32[]{:S(2)}, u32[]{:S(2)}) async-start(f32[256,1,128]{2,1,0:T(1,128)} %bitcast.10), calls=%async_computation.1 | async-start | bytes 262144 | tf_op jit(solution)/shard_map/all_to_all | solution.py:619
  58.1 3.0 %collective-permute-start.4 = (f32[2,32,128]{2,1,0:T(8,128)S(1)}, f32[2,32,128]{2,1,0:T(8,128)S(1)}, u32[]{:S(2)}, u32[]{:S(2)}) collective-permute-start(f32[2,32,128]{2,1,0:T(8,128)S(1)} %get-tuple-element.118), channel_id=1, source_target_pairs={{1,4},{33,36},{65,68},{97,100},{129,132},{161,164},{193,196},{225,... | collective-permute-start | bytes 98312 | tf_op jit(solution)/shard_map/ppermute | solution.py:651
  61.1 2.5 %collective-permute-done.4.y_two = f32[2,32,128]{2,1,0:T(8,128)S(1)} collective-permute-done((f32[2,32,128]{2,1,0:T(8,128)S(1)}, f32[2,32,128]{2,1,0:T(8,128)S(1)}, u32[]{:S(2)}, u32[]{:S(2)}) %collective-permute-start.4) | collective-permute-done | bytes 32800 | tf_op jit(solution)/shard_map/ppermute | solution.py:651
  64.2 4.2 %all-to-all-done.1 = f32[256,1,128]{2,1,0:T(1,128)S(1)} async-done(((f32[256,1,128]{2,1,0:T(1,128)}), f32[256,1,128]{2,1,0:T(1,128)S(1)}, u32[]{:S(2)}, u32[]{:S(2)}) %all-to-all-start.1) | async-done | bytes 131104 | tf_op jit(solution)/shard_map/all_to_all | solution.py:619
  71.0 9.8 %all-to-all-start.2 = ((f32[256,1,128]{2,1,0:T(1,128)}), f32[256,1,128]{2,1,0:T(1,128)S(1)}, u32[]{:S(2)}, u32[]{:S(2)}) async-start(f32[256,1,128]{2,1,0:T(1,128)} %bitcast.13), calls=%async_computation.2 | async-start | bytes 262144 | tf_op jit(solution)/shard_map/all_to_all | solution.py:619
  83.8 3.0 %collective-permute-start.8 = (f32[2,32,128]{2,1,0:T(8,128)S(1)}, f32[2,32,128]{2,1,0:T(8,128)S(1)}, u32[]{:S(2)}, u32[]{:S(2)}) collective-permute-start(f32[2,32,128]{2,1,0:T(8,128)S(1)} %get-tuple-element.133), channel_id=1, source_target_pairs={{1,4},{33,36},{65,68},{97,100},{129,132},{161,164},{193,196},{225,... | collective-permute-start | bytes 98312 | tf_op jit(solution)/shard_map/ppermute | solution.py:651
  86.8 2.5 %collective-permute-done.8.y_two = f32[2,32,128]{2,1,0:T(8,128)S(1)} collective-permute-done((f32[2,32,128]{2,1,0:T(8,128)S(1)}, f32[2,32,128]{2,1,0:T(8,128)S(1)}, u32[]{:S(2)}, u32[]{:S(2)}) %collective-permute-start.8) | collective-permute-done | bytes 32800 | tf_op jit(solution)/shard_map/ppermute | solution.py:651
  95.5 2.4 %collective-permute-start.9 = (f32[16,8,128]{2,1,0:T(8,128)S(1)}, f32[16,8,128]{2,1,0:T(8,128)S(1)}, u32[]{:S(2)}, u32[]{:S(2)}) collective-permute-start(f32[16,8,128]{2,1,0:T(8,128)S(1)} %get-tuple-element.143), channel_id=1, source_target_pairs={{0,32},{1,33},{2,34},{3,35},{4,36},{5,37},{6,38},{7,39},{8,40},{9,... | collective-permute-start | bytes 196616 | tf_op jit(solution)/shard_map/ppermute | solution.py:640
  98.7 3.4 %collective-permute-start.12 = (f32[2,32,128]{2,1,0:T(8,128)S(1)}, f32[2,32,128]{2,1,0:T(8,128)S(1)}, u32[]{:S(2)}, u32[]{:S(2)}) collective-permute-start(f32[2,32,128]{2,1,0:T(8,128)S(1)} %get-tuple-element.146), channel_id=1, source_target_pairs={{1,4},{33,36},{65,68},{97,100},{129,132},{161,164},{193,196},{225,... | collective-permute-start | bytes 98312 | tf_op jit(solution)/shard_map/ppermute | solution.py:651
  108.4 2.5 %shard_map.145 = (f32[5,32,8,128]{3,2,1,0:T(8,128)S(1)}, f32[32,8,128]{2,1,0:T(8,128)S(1)}, f32[2,2,32,128]{3,2,1,0:T(8,128)S(1)}, f32[32,8,128]{2,1,0:T(8,128)S...) custom-call(f32[8,128]{1,0:T(8,128)S(1)} %get-tuple-element.107.weight, ...), custom_call_target="tpu_custom_call" | custom-call | flops 1000000 | bytes 4000000 | tf_op jit(solution)/shard_map/pallas_call | solution.py:586
  110.9 26.6 %all_to_all.77 = f32[256,1,128]{2,1,0:T(1,128)S(1)} all-to-all(f32[256,1,128]{2,1,0:T(1,128)S(1)} %bitcast.49), channel_id=1, replica_groups=mesh['strip'=16,'period'=16] {'strip','period'}, dimensions={0} | all-to-all | bytes 262144 | tf_op jit(solution)/shard_map/all_to_all | solution.py:619
  139.0 5.4 %all-to-all-start.4 = ((f32[256,1,128]{2,1,0:T(1,128)}), f32[256,1,128]{2,1,0:T(1,128)S(1)}, u32[]{:S(2)}, u32[]{:S(2)}) async-start(f32[256,1,128]{2,1,0:T(1,128)} %bitcast.19), calls=%async_computation.4 | async-start | bytes 262144 | tf_op jit(solution)/shard_map/all_to_all | solution.py:619
  147.6 3.0 %collective-permute-start.16 = (f32[2,32,128]{2,1,0:T(8,128)S(1)}, f32[2,32,128]{2,1,0:T(8,128)S(1)}, u32[]{:S(2)}, u32[]{:S(2)}) collective-permute-start(f32[2,32,128]{2,1,0:T(8,128)S(1)} %get-tuple-element.166), channel_id=1, source_target_pairs={{1,4},{33,36},{65,68},{97,100},{129,132},{161,164},{193,196},{225,... | collective-permute-start | bytes 98312 | tf_op jit(solution)/shard_map/ppermute | solution.py:651
  150.6 2.5 %collective-permute-done.16.y_two = f32[2,32,128]{2,1,0:T(8,128)S(1)} collective-permute-done((f32[2,32,128]{2,1,0:T(8,128)S(1)}, f32[2,32,128]{2,1,0:T(8,128)S(1)}, u32[]{:S(2)}, u32[]{:S(2)}) %collective-permute-start.16) | collective-permute-done | bytes 32800 | tf_op jit(solution)/shard_map/ppermute | solution.py:651
  155.4 2.4 %all-to-all-done.4 = f32[256,1,128]{2,1,0:T(1,128)S(1)} async-done(((f32[256,1,128]{2,1,0:T(1,128)}), f32[256,1,128]{2,1,0:T(1,128)S(1)}, u32[]{:S(2)}, u32[]{:S(2)}) %all-to-all-start.4) | async-done | bytes 131104 | tf_op jit(solution)/shard_map/all_to_all | solution.py:619
  161.1 11.5 %all-to-all-start.5 = ((f32[256,1,128]{2,1,0:T(1,128)}), f32[256,1,128]{2,1,0:T(1,128)S(1)}, u32[]{:S(2)}, u32[]{:S(2)}) async-start(f32[256,1,128]{2,1,0:T(1,128)} %bitcast.22), calls=%async_computation.5 | async-start | bytes 262144 | tf_op jit(solution)/shard_map/all_to_all | solution.py:619
  175.7 3.0 %collective-permute-start.20 = (f32[2,32,128]{2,1,0:T(8,128)S(1)}, f32[2,32,128]{2,1,0:T(8,128)S(1)}, u32[]{:S(2)}, u32[]{:S(2)}) collective-permute-start(f32[2,32,128]{2,1,0:T(8,128)S(1)} %get-tuple-element.181), channel_id=1, source_target_pairs={{1,4},{33,36},{65,68},{97,100},{129,132},{161,164},{193,196},{225,... | collective-permute-start | bytes 98312 | tf_op jit(solution)/shard_map/ppermute | solution.py:651
  178.7 2.5 %collective-permute-done.20.y_two = f32[2,32,128]{2,1,0:T(8,128)S(1)} collective-permute-done((f32[2,32,128]{2,1,0:T(8,128)S(1)}, f32[2,32,128]{2,1,0:T(8,128)S(1)}, u32[]{:S(2)}, u32[]{:S(2)}) %collective-permute-start.20) | collective-permute-done | bytes 32800 | tf_op jit(solution)/shard_map/ppermute | solution.py:651
  186.7 2.7 %collective-permute-start.21 = (f32[16,8,128]{2,1,0:T(8,128)S(1)}, f32[16,8,128]{2,1,0:T(8,128)S(1)}, u32[]{:S(2)}, u32[]{:S(2)}) collective-permute-start(f32[16,8,128]{2,1,0:T(8,128)S(1)} %get-tuple-element.191), channel_id=1, source_target_pairs={{0,32},{1,33},{2,34},{3,35},{4,36},{5,37},{6,38},{7,39},{8,40},{9,... | collective-permute-start | bytes 196616 | tf_op jit(solution)/shard_map/ppermute | solution.py:640
  190.1 3.4 %collective-permute-start.24 = (f32[2,32,128]{2,1,0:T(8,128)S(1)}, f32[2,32,128]{2,1,0:T(8,128)S(1)}, u32[]{:S(2)}, u32[]{:S(2)}) collective-permute-start(f32[2,32,128]{2,1,0:T(8,128)S(1)} %get-tuple-element.194), channel_id=1, source_target_pairs={{1,4},{33,36},{65,68},{97,100},{129,132},{161,164},{193,196},{225,... | collective-permute-start | bytes 98312 | tf_op jit(solution)/shard_map/ppermute | solution.py:651
  197.4 24.0 %all_to_all.78.got = f32[32,8,8,128]{3,2,1,0:T(8,128)S(1)} all-to-all(f32[32,8,8,128]{3,2,1,0:T(8,128)S(1)} %shard_map.151), channel_id=1, replica_groups={{0,1,2,3,4,5,6,7,8,9,10,11,12,13,14,15,16,17,18,19,20,21,22,23,24,25,26..., dimensions={0} | all-to-all | bytes 2097152 | tf_op jit(solution)/shard_map/all_to_all | solution.py:630
  222.0 7.6 %all-to-all-start.7 = ((f32[8,1,128]{2,1,0:T(1,128)}), f32[8,1,128]{2,1,0:T(1,128)S(1)}, u32[]{:S(2)}, u32[]{:S(2)}) async-start(f32[8,1,128]{2,1,0:T(1,128)} %bitcast.29), calls=%async_computation.7 | async-start | bytes 8192 | tf_op jit(solution)/shard_map/all_to_all | solution.py:625
  230.7 5.4 %all-to-all-done.7 = f32[8,1,128]{2,1,0:T(1,128)S(1)} async-done(((f32[8,1,128]{2,1,0:T(1,128)}), f32[8,1,128]{2,1,0:T(1,128)S(1)}, u32[]{:S(2)}, u32[]{:S(2)}) %all-to-all-start.7) | async-done | bytes 4128 | tf_op jit(solution)/shard_map/all_to_all | solution.py:625
  (132 shorter events, 60.7 us)
Async XLA Ops:
  2.3 8.9 %collective-permute-start = (f32[4,64,128]{2,1,0:T(8,128)S(1)}, f32[4,64,128]{2,1,0:T(8,128)S(1)}, u32[]{:S(2)}, u32[]{:S(2)}) collective-permute-start(f32[4,64,128]{2,1,0:T(8,128)S(1)} %bitcast_select_fusion), channel_id=1, source_target_pairs={{16,32},{32,16},{48,64},{64,48},{80,96},{96,80},{112,128},{128,112... | collective-permute-start | bytes 393224 | tf_op jit(solution)/shard_map/ppermute | solution.py:677
  44.9 23.5 %all-to-all-start.1 = ((f32[256,1,128]{2,1,0:T(1,128)}), f32[256,1,128]{2,1,0:T(1,128)S(1)}, u32[]{:S(2)}, u32[]{:S(2)}) async-start(f32[256,1,128]{2,1,0:T(1,128)} %bitcast.10), calls=%async_computation.1 | async-start | bytes 262144 | tf_op jit(solution)/shard_map/all_to_all | solution.py:619
  55.1 8.6 %collective-permute-start.1 = (f32[16,8,128]{2,1,0:T(8,128)S(1)}, f32[16,8,128]{2,1,0:T(8,128)S(1)}, u32[]{:S(2)}, u32[]{:S(2)}) collective-permute-start(f32[16,8,128]{2,1,0:T(8,128)S(1)} %get-tuple-element.115), channel_id=1, source_target_pairs={{0,32},{1,33},{2,34},{3,35},{4,36},{5,37},{6,38},{7,39},{8,40},{9,... | collective-permute-start | bytes 196616 | tf_op jit(solution)/shard_map/ppermute | solution.py:640
  56.7 7.0 %collective-permute-start.2 = (f32[16,8,128]{2,1,0:T(8,128)S(1)}, f32[16,8,128]{2,1,0:T(8,128)S(1)}, u32[]{:S(2)}, u32[]{:S(2)}) collective-permute-start(f32[16,8,128]{2,1,0:T(8,128)S(1)} %get-tuple-element.116), channel_id=1, source_target_pairs={{32,64},{33,65},{34,66},{35,67},{36,68},{37,69},{38,70},{39,71},{4... | collective-permute-start | bytes 196616 | tf_op jit(solution)/shard_map/ppermute | solution.py:640
  58.1 5.6 %collective-permute-start.4 = (f32[2,32,128]{2,1,0:T(8,128)S(1)}, f32[2,32,128]{2,1,0:T(8,128)S(1)}, u32[]{:S(2)}, u32[]{:S(2)}) collective-permute-start(f32[2,32,128]{2,1,0:T(8,128)S(1)} %get-tuple-element.118), channel_id=1, source_target_pairs={{1,4},{33,36},{65,68},{97,100},{129,132},{161,164},{193,196},{225,... | collective-permute-start | bytes 98312 | tf_op jit(solution)/shard_map/ppermute | solution.py:651
  71.0 23.1 %all-to-all-start.2 = ((f32[256,1,128]{2,1,0:T(1,128)}), f32[256,1,128]{2,1,0:T(1,128)S(1)}, u32[]{:S(2)}, u32[]{:S(2)}) async-start(f32[256,1,128]{2,1,0:T(1,128)} %bitcast.13), calls=%async_computation.2 | async-start | bytes 262144 | tf_op jit(solution)/shard_map/all_to_all | solution.py:619
  80.8 8.6 %collective-permute-start.5 = (f32[16,8,128]{2,1,0:T(8,128)S(1)}, f32[16,8,128]{2,1,0:T(8,128)S(1)}, u32[]{:S(2)}, u32[]{:S(2)}) collective-permute-start(f32[16,8,128]{2,1,0:T(8,128)S(1)} %get-tuple-element.130), channel_id=1, source_target_pairs={{0,32},{1,33},{2,34},{3,35},{4,36},{5,37},{6,38},{7,39},{8,40},{9,... | collective-permute-start | bytes 196616 | tf_op jit(solution)/shard_map/ppermute | solution.py:640
  82.4 7.0 %collective-permute-start.6 = (f32[16,8,128]{2,1,0:T(8,128)S(1)}, f32[16,8,128]{2,1,0:T(8,128)S(1)}, u32[]{:S(2)}, u32[]{:S(2)}) collective-permute-start(f32[16,8,128]{2,1,0:T(8,128)S(1)} %get-tuple-element.131), channel_id=1, source_target_pairs={{32,64},{33,65},{34,66},{35,67},{36,68},{37,69},{38,70},{39,71},{4... | collective-permute-start | bytes 196616 | tf_op jit(solution)/shard_map/ppermute | solution.py:640
  83.8 5.6 %collective-permute-start.8 = (f32[2,32,128]{2,1,0:T(8,128)S(1)}, f32[2,32,128]{2,1,0:T(8,128)S(1)}, u32[]{:S(2)}, u32[]{:S(2)}) collective-permute-start(f32[2,32,128]{2,1,0:T(8,128)S(1)} %get-tuple-element.133), channel_id=1, source_target_pairs={{1,4},{33,36},{65,68},{97,100},{129,132},{161,164},{193,196},{225,... | collective-permute-start | bytes 98312 | tf_op jit(solution)/shard_map/ppermute | solution.py:651
  95.5 8.4 %collective-permute-start.9 = (f32[16,8,128]{2,1,0:T(8,128)S(1)}, f32[16,8,128]{2,1,0:T(8,128)S(1)}, u32[]{:S(2)}, u32[]{:S(2)}) collective-permute-start(f32[16,8,128]{2,1,0:T(8,128)S(1)} %get-tuple-element.143), channel_id=1, source_target_pairs={{0,32},{1,33},{2,34},{3,35},{4,36},{5,37},{6,38},{7,39},{8,40},{9,... | collective-permute-start | bytes 196616 | tf_op jit(solution)/shard_map/ppermute | solution.py:640
  97.9 6.0 %collective-permute-start.10 = (f32[16,8,128]{2,1,0:T(8,128)S(1)}, f32[16,8,128]{2,1,0:T(8,128)S(1)}, u32[]{:S(2)}, u32[]{:S(2)}) collective-permute-start(f32[16,8,128]{2,1,0:T(8,128)S(1)} %get-tuple-element.144), channel_id=1, source_target_pairs={{32,64},{33,65},{34,66},{35,67},{36,68},{37,69},{38,70},{39,71},{4... | collective-permute-start | bytes 196616 | tf_op jit(solution)/shard_map/ppermute | solution.py:640
  98.7 5.2 %collective-permute-start.12 = (f32[2,32,128]{2,1,0:T(8,128)S(1)}, f32[2,32,128]{2,1,0:T(8,128)S(1)}, u32[]{:S(2)}, u32[]{:S(2)}) collective-permute-start(f32[2,32,128]{2,1,0:T(8,128)S(1)} %get-tuple-element.146), channel_id=1, source_target_pairs={{1,4},{33,36},{65,68},{97,100},{129,132},{161,164},{193,196},{225,... | collective-permute-start | bytes 98312 | tf_op jit(solution)/shard_map/ppermute | solution.py:651
  139.0 18.9 %all-to-all-start.4 = ((f32[256,1,128]{2,1,0:T(1,128)}), f32[256,1,128]{2,1,0:T(1,128)S(1)}, u32[]{:S(2)}, u32[]{:S(2)}) async-start(f32[256,1,128]{2,1,0:T(1,128)} %bitcast.19), calls=%async_computation.4 | async-start | bytes 262144 | tf_op jit(solution)/shard_map/all_to_all | solution.py:619
  144.5 8.7 %collective-permute-start.13 = (f32[16,8,128]{2,1,0:T(8,128)S(1)}, f32[16,8,128]{2,1,0:T(8,128)S(1)}, u32[]{:S(2)}, u32[]{:S(2)}) collective-permute-start(f32[16,8,128]{2,1,0:T(8,128)S(1)} %get-tuple-element.163), channel_id=1, source_target_pairs={{0,32},{1,33},{2,34},{3,35},{4,36},{5,37},{6,38},{7,39},{8,40},{9,... | collective-permute-start | bytes 196616 | tf_op jit(solution)/shard_map/ppermute | solution.py:640
  146.2 7.0 %collective-permute-start.14 = (f32[16,8,128]{2,1,0:T(8,128)S(1)}, f32[16,8,128]{2,1,0:T(8,128)S(1)}, u32[]{:S(2)}, u32[]{:S(2)}) collective-permute-start(f32[16,8,128]{2,1,0:T(8,128)S(1)} %get-tuple-element.164), channel_id=1, source_target_pairs={{32,64},{33,65},{34,66},{35,67},{36,68},{37,69},{38,70},{39,71},{4... | collective-permute-start | bytes 196616 | tf_op jit(solution)/shard_map/ppermute | solution.py:640
  147.6 5.6 %collective-permute-start.16 = (f32[2,32,128]{2,1,0:T(8,128)S(1)}, f32[2,32,128]{2,1,0:T(8,128)S(1)}, u32[]{:S(2)}, u32[]{:S(2)}) collective-permute-start(f32[2,32,128]{2,1,0:T(8,128)S(1)} %get-tuple-element.166), channel_id=1, source_target_pairs={{1,4},{33,36},{65,68},{97,100},{129,132},{161,164},{193,196},{225,... | collective-permute-start | bytes 98312 | tf_op jit(solution)/shard_map/ppermute | solution.py:651
  161.1 24.8 %all-to-all-start.5 = ((f32[256,1,128]{2,1,0:T(1,128)}), f32[256,1,128]{2,1,0:T(1,128)S(1)}, u32[]{:S(2)}, u32[]{:S(2)}) async-start(f32[256,1,128]{2,1,0:T(1,128)} %bitcast.22), calls=%async_computation.5 | async-start | bytes 262144 | tf_op jit(solution)/shard_map/all_to_all | solution.py:619
  172.6 8.6 %collective-permute-start.17 = (f32[16,8,128]{2,1,0:T(8,128)S(1)}, f32[16,8,128]{2,1,0:T(8,128)S(1)}, u32[]{:S(2)}, u32[]{:S(2)}) collective-permute-start(f32[16,8,128]{2,1,0:T(8,128)S(1)} %get-tuple-element.178), channel_id=1, source_target_pairs={{0,32},{1,33},{2,34},{3,35},{4,36},{5,37},{6,38},{7,39},{8,40},{9,... | collective-permute-start | bytes 196616 | tf_op jit(solution)/shard_map/ppermute | solution.py:640
  174.2 7.0 %collective-permute-start.18 = (f32[16,8,128]{2,1,0:T(8,128)S(1)}, f32[16,8,128]{2,1,0:T(8,128)S(1)}, u32[]{:S(2)}, u32[]{:S(2)}) collective-permute-start(f32[16,8,128]{2,1,0:T(8,128)S(1)} %get-tuple-element.179), channel_id=1, source_target_pairs={{32,64},{33,65},{34,66},{35,67},{36,68},{37,69},{38,70},{39,71},{4... | collective-permute-start | bytes 196616 | tf_op jit(solution)/shard_map/ppermute | solution.py:640
  175.7 5.6 %collective-permute-start.20 = (f32[2,32,128]{2,1,0:T(8,128)S(1)}, f32[2,32,128]{2,1,0:T(8,128)S(1)}, u32[]{:S(2)}, u32[]{:S(2)}) collective-permute-start(f32[2,32,128]{2,1,0:T(8,128)S(1)} %get-tuple-element.181), channel_id=1, source_target_pairs={{1,4},{33,36},{65,68},{97,100},{129,132},{161,164},{193,196},{225,... | collective-permute-start | bytes 98312 | tf_op jit(solution)/shard_map/ppermute | solution.py:651
  186.7 8.7 %collective-permute-start.21 = (f32[16,8,128]{2,1,0:T(8,128)S(1)}, f32[16,8,128]{2,1,0:T(8,128)S(1)}, u32[]{:S(2)}, u32[]{:S(2)}) collective-permute-start(f32[16,8,128]{2,1,0:T(8,128)S(1)} %get-tuple-element.191), channel_id=1, source_target_pairs={{0,32},{1,33},{2,34},{3,35},{4,36},{5,37},{6,38},{7,39},{8,40},{9,... | collective-permute-start | bytes 196616 | tf_op jit(solution)/shard_map/ppermute | solution.py:640
  189.4 6.0 %collective-permute-start.22 = (f32[16,8,128]{2,1,0:T(8,128)S(1)}, f32[16,8,128]{2,1,0:T(8,128)S(1)}, u32[]{:S(2)}, u32[]{:S(2)}) collective-permute-start(f32[16,8,128]{2,1,0:T(8,128)S(1)} %get-tuple-element.192), channel_id=1, source_target_pairs={{32,64},{33,65},{34,66},{35,67},{36,68},{37,69},{38,70},{39,71},{4... | collective-permute-start | bytes 196616 | tf_op jit(solution)/shard_map/ppermute | solution.py:640
  190.1 5.2 %collective-permute-start.24 = (f32[2,32,128]{2,1,0:T(8,128)S(1)}, f32[2,32,128]{2,1,0:T(8,128)S(1)}, u32[]{:S(2)}, u32[]{:S(2)}) collective-permute-start(f32[2,32,128]{2,1,0:T(8,128)S(1)} %get-tuple-element.194), channel_id=1, source_target_pairs={{1,4},{33,36},{65,68},{97,100},{129,132},{161,164},{193,196},{225,... | collective-permute-start | bytes 98312 | tf_op jit(solution)/shard_map/ppermute | solution.py:651
  222.0 14.1 %all-to-all-start.7 = ((f32[8,1,128]{2,1,0:T(1,128)}), f32[8,1,128]{2,1,0:T(1,128)S(1)}, u32[]{:S(2)}, u32[]{:S(2)}) async-start(f32[8,1,128]{2,1,0:T(1,128)} %bitcast.29), calls=%async_computation.7 | async-start | bytes 8192 | tf_op jit(solution)/shard_map/all_to_all | solution.py:625
  (39 other events, 232.0 us)

commit v4 on v3

v4 whole, which is shorter than its diff:
```python
import functools
import math

import jax
import jax.numpy as jnp
from jax import lax
from jax.experimental import pallas as pl
from jax.experimental.pallas import tpu as pltpu
from jax.sharding import PartitionSpec as P

OUTER = 2
INNER = 3
NX = 16
NY = 128
NZ = 64
NP = 64
RATE = math.log(1.1) / 12.0
EPS = 1e-06
SLOPE = 11.0
BLOCKS = float(NX * NY * NZ)
ROOT = math.sqrt(BLOCKS)
F32 = jnp.float32

PLANE = 32
TILES = 32
ROWS = NP // 2
DEVICES = 256
ARCS = 5
BOUND, SHARE, RIM, EXTRA = 5, 6, 7, 8
SLOTS = 9
LANE_PRIMAL, LANE_DUAL, LANE_TONS = 40, 41, 42
HALO, EDGES, TONS, VALUE, ODD_X, ODD_Y, LIMITS = 5, 6, 7, 8, 9, 10, 11
CONSTANTS = 15
TABLE = ROWS // 8
SHARES, SHARE_SUM, SHARE_FIRST, HEAD = 0, ROWS, 2 * ROWS, 3 * ROWS
CAPS = 4 * ROWS
CAP_SUM, CAP_FIRST, WEIGHT = CAPS + TABLE, CAPS + 2 * TABLE, CAPS + 3 * TABLE
FIRST = WEIGHT + 1
LAST = FIRST + 2 * TABLE
PRIMAL = LAST + 2 * TABLE
PRICES, BOUNDS, HALOS = 0, ARCS * ROWS, (ARCS + 1) * ROWS
EDGE_ROWS = (ARCS + 2) * ROWS
TAIL = EDGE_ROWS + 4 * TABLE
DUAL = TAIL + ROWS
ROW = 7


def member(tile):
    chip, core = divmod(tile, 2)
    row, at = divmod(chip, 4)
    at = at if row % 2 == 0 else 3 - at
    return row % 2 * 16 + at * 4 + row // 2 * 2 + core


def table(ref, at):
    return ref[at : at + TABLE].reshape(ROWS, 128)


def put_table(ref, at, value):
    ref[at : at + TABLE] = value.reshape(TABLE, 8, 128)


def line(ref, at, r):
    return ref[at + r // 8, r % 8 : r % 8 + 1]


def edge_at(n, x):
    return EDGE_ROWS + (2 * n + x) * TABLE


def lanes(shape):
    return lax.broadcasted_iota(jnp.int32, shape, len(shape) - 1)


def subs(shape):
    return lax.broadcasted_iota(jnp.int32, shape, len(shape) - 2)


def later_half(shape):
    return lanes(shape) >= 64


def half_matrix():
    a = subs((128, 128)) >= 64
    b = lanes((128, 128)) >= 64
    return (a == b).astype(F32)


def half_sums(rows):
    return jnp.dot(
        rows, half_matrix(), precision=lax.Precision.HIGHEST, preferred_element_type=F32
    )


def period_table():
    shape = (ROWS, 128)
    return (2 * subs(shape) + later_half(shape).astype(jnp.int32)).astype(F32)


def down(v):
    return pltpu.roll(v, 1, v.ndim - 1)


def up(v):
    return pltpu.roll(v, 127, v.ndim - 1)


def swap(v):
    return pltpu.roll(v, 64, v.ndim - 1)


def low(shape=(8, 128)):
    return subs(shape) < 4


def turn(v):
    return pltpu.roll(v, 4, v.ndim - 2)


def mix(one, two):
    return jnp.where(low(), one, turn(two)), jnp.where(low(), turn(one), two)


def fetch(pairs, sems):
    copies = [
        pltpu.make_async_copy(source, target, sems.at[n]) for n, (source, target) in enumerate(pairs)
    ]
    for copy in copies:
        copy.start()
    return copies


def put_tiles(source, target):
    one = jnp.concatenate([source(0), source(1)], axis=0).T
    two = jnp.concatenate([source(2), source(3)], axis=0).T
    for m in range(TILES // 2):
        here = slice(8 * m, 8 * m + 8)
        even, odd = mix(one[here], two[here])
        target(member(2 * m), even)
        target(member(2 * m + 1), odd)


def pack_kernel(
    small, place, slope_at, ton_class_at, value_at, share_at, prec_at, bound_at,
    out, slope, ton_class, value, share, prec, bound, sems,
):
    copies = fetch(
        [
            (slope_at, slope), (ton_class_at, ton_class), (value_at, value), (prec_at, prec),
            (bound_at, bound), (share_at, share),
        ],
        sems,
    )
    caps = [small[t] for t in range(4)]
    limits = [small[4 + t] for t in range(4)]
    density = [small[8 + c] for c in range(8)]
    for copy in copies:
        copy.wait()
    x = place[0]
    row = (1, 128)
    code = slope[...]
    column = lanes(row)
    mask = [
        None,
        ((code & 1 == 1) & (jnp.full(row, x) + 1 < NX)).astype(F32),
        ((code >> 1 & 1 == 1) & (jnp.full(row, x) >= 1)).astype(F32),
        ((code >> 2 & 1 == 1) & (column + 1 < NY)).astype(F32),
        ((code >> 3 & 1 == 1) & (column >= 1)).astype(F32),
    ]
    top = subs((NZ, NY)) == 0

    def put(field, source):
        def target(slot, tile):
            out[slot, field] = tile

        put_tiles(source, target)

    for k in range(ARCS):
        def source(t, k=k):
            spare = jnp.where(column % 2 == 0, caps[t], limits[t]) if k == 0 else mask[k]
            return jnp.where(top, spare, prec[k, t])

        put(k, source)
    put(BOUND, lambda t: bound[t])
    put(SHARE, lambda t: share[t])
    classes = ton_class[...]
    tons = jnp.zeros(classes.shape, F32)
    for c in range(8):
        tons = jnp.where(classes == c, (1.0 + c) * density[c], tons)
    blocks = jnp.concatenate([tons, value[...]], axis=0).T
    zero = jnp.zeros(row, F32)
    for j in range(TILES):
        i = member(j)
        out[i, EXTRA, 4:8] = blocks[4 * j : 4 * j + 4]
        for a in range(2):
            if j > 0:
                out[i, EXTRA, a : a + 1] = out[member(j - 1), 3, 4 * a + 3 : 4 * a + 4]
            else:
                out[i, EXTRA, a : a + 1] = zero
            if j < TILES - 1:
                out[i, EXTRA, 2 + a : 3 + a] = out[member(j + 1), 4, 4 * a : 4 * a + 1]
            else:
                out[i, EXTRA, 2 + a : 3 + a] = zero


def rim_kernel(rim, send, out, tiles, sem):
    def target(slot, tile):
        tiles[slot] = tile

    put_tiles(lambda t: rim[t], target)
    copy = pltpu.make_async_copy(tiles, out.at[:, RIM], sem)
    copy.start()
    copy.wait()


def adjoint_row(prices, bound, halo, dual, r, carry):
    shape = (8, 128)
    sub = subs(shape)
    edge = [[line(dual, edge_at(n, x), r) for x in range(2)] for n in range(2)]
    total = prices[0] + prices[1] + prices[2] + prices[3] + prices[4] + bound
    across = turn(jnp.where(low(), prices[1], prices[2]))
    before = pltpu.roll(prices[3], 1, 0)
    before = jnp.where(sub == 0, edge[0][0], jnp.where(sub == 4, edge[0][1], before))
    after = pltpu.roll(prices[4], 7, 0)
    after = jnp.where(sub == 3, edge[1][0], jnp.where(sub == 7, edge[1][1], after))
    lower = prices[0] + halo + across + before + after
    g = total - up(lower)
    pair = g + swap(g)
    return carry + jnp.where(later_half(shape), g, pair), carry + pair


def put_dual(dual, r, prices, bound, halo, carry):
    for k in range(ARCS):
        dual[PRICES + k * ROWS + r] = prices[k]
    dual[BOUNDS + r] = bound
    dual[HALOS + r] = halo
    dual[TAIL + r], carry = adjoint_row(prices, bound, halo, dual, r, carry)
    return carry


def unpack_kernel(small, place, got, primal, dual, const):
    shape = (8, 128)
    primal[WEIGHT] = jnp.full(shape, small[0])
    const[ODD_X] = jnp.full(shape, place[0] // 2 % 2).astype(F32)
    const[ODD_Y] = jnp.full(shape, place[1] % 2).astype(F32)
    lane = lanes(shape)
    deep = ((lane & 63) >= 1).astype(F32)
    half = later_half(shape)

    def pair(s, field):
        return mix(got[s, field], got[16 + s, field])

    const[0] = deep
    for k in range(1, ARCS):
        const[k] = jnp.broadcast_to(pair(0, k)[0][:, 0:1], shape) * deep
    const[HALO] = jnp.broadcast_to(pair(0, RIM)[0][:, 0:1], shape) * deep
    for n in range(2):
        for x in range(2):
            at = 2 * n + x
            edge = got[16 * x, EXTRA, 2 * n : 2 * n + 1]
            const[EDGES, at : at + 1] = jnp.broadcast_to(edge[:, 0:1], (1, 128)) * deep[0:1]
            const[EDGES, 4 + at : 5 + at] = jnp.zeros((1, 128), F32)
    blocks = jnp.where(low(), turn(got[0, EXTRA]), got[16, EXTRA])
    other = swap(blocks)
    const[TONS] = jnp.where(half, other, blocks)
    const[VALUE] = jnp.where(half, blocks, other)
    for s in range(ROWS // 2):
        tile, within = s // 4, slice(2 * s % 8, 2 * s % 8 + 2)
        for n in range(2):
            for x in range(2):
                at = 2 * n + x
                edge = got[16 * x + s, EXTRA, 2 * n : 2 * n + 2]
                dual[edge_at(n, x) + tile, within] = edge * const[EDGES, at : at + 1]
    carry = jnp.zeros(shape, F32)
    for s in reversed(range(ROWS // 2)):
        p = [pair(s, k) for k in range(ARCS)]
        b, u, h = pair(s, BOUND), pair(s, SHARE), pair(s, RIM)
        for a in (1, 0):
            r = 2 * s + a
            spare = jnp.where(
                half,
                jnp.broadcast_to(p[0][a][:, 64:65], shape),
                jnp.broadcast_to(p[0][a][:, 0:1], shape),
            )
            at = slice(r % 8, r % 8 + 1)
            primal[CAPS + r // 8, at] = spare[0:1]
            const[LIMITS + r // 8, at] = spare[1:2]
            primal[SHARES + r] = u[a]
            here = [p[k][a] * const[k] for k in range(ARCS)]
            carry = put_dual(dual, r, here, b[a], h[a] * const[HALO], carry)


def summed_row(got):
    total = got[0:8]
    for n in range(1, DEVICES // 8):
        total = total + got[8 * n : 8 * n + 8]
    return jnp.sum(total, axis=0, keepdims=True)


def lane_value(row, lane):
    return jnp.sum(jnp.where(lanes((1, 128)) == lane, row, 0.0), axis=1, keepdims=True)


def whole(v):
    return jnp.sum(jnp.sum(v, axis=0, keepdims=True), axis=1, keepdims=True)


def caps_after(row, primal, const):
    shape = (ROWS, 128)
    spread = jnp.where((lanes(shape) & 63) == subs(shape), jnp.broadcast_to(row, shape), 0.0)
    totals = half_sums(spread)
    tons_all = lane_value(row, LANE_TONS)
    over = (totals - BLOCKS * table(const, LIMITS)) / tons_all
    return jnp.maximum(table(primal, CAPS) + primal[WEIGHT, 0:1] * over, 0.0)


def restart(row, primal, const):
    mean = (table(primal, CAP_SUM) + caps_after(row, primal, const)) / INNER
    move_cap = whole((mean - table(primal, CAP_FIRST)) ** 2) * (1.0 / 64.0)
    primal_move = lane_value(row, LANE_PRIMAL)
    dual_move = lane_value(row, LANE_DUAL) + move_cap
    weight = primal[WEIGHT, 0:1]
    return mean, jnp.sqrt(weight * jnp.sqrt((dual_move + EPS) / (primal_move + EPS)))


def primal_step(inner, caps, weight, primal, dual, const, new, x_one, x_two, y_one, y_two, row, rates):
    shape = (8, 128)
    tons = const[TONS]
    value = const[VALUE]
    lean = tons / ROOT
    periods = period_table()
    rates[0] = jnp.exp(-RATE * periods)
    rates[1] = SLOPE * (NP - periods)
    put_table(new, CAPS, caps)
    put_table(new, CAP_FIRST, caps if inner == 0 else table(primal, CAP_FIRST))
    if inner == 0:
        put_table(new, CAP_SUM, jnp.zeros((ROWS, 128), F32))
    else:
        put_table(new, CAP_SUM, table(primal, CAP_SUM) + caps)
    new[WEIGHT] = jnp.broadcast_to(weight, shape)
    half = later_half(shape)
    odd_x = const[ODD_X] > 0.5
    odd_y = const[ODD_Y] > 0.5
    carry = jnp.zeros(shape, F32)
    moved = jnp.zeros(shape, F32)
    mined = []
    for r in range(ROWS):
        gradient = dual[TAIL + r] + tons * line(new, CAPS, r) / ROOT
        tau = 1.0 / (weight * (rates[1, r : r + 1] + lean))
        old = primal[SHARES + r]
        now = jnp.maximum(old - tau * (gradient - value * rates[0, r : r + 1]), 0.0)
        if inner == 0:
            new[SHARES + r] = now
            new[SHARE_SUM + r] = now
            new[SHARE_FIRST + r] = old
        elif inner < INNER - 1:
            new[SHARES + r] = now
            new[SHARE_SUM + r] = primal[SHARE_SUM + r] + now
            new[SHARE_FIRST + r] = primal[SHARE_FIRST + r]
        else:
            mean = (primal[SHARE_SUM + r] + now) / INNER
            new[SHARES + r] = mean
            moved = moved + (mean - primal[SHARE_FIRST + r]) ** 2
        ahead = 2.0 * now - old
        pair = ahead + swap(ahead)
        cumulative = carry + jnp.where(half, pair, ahead)
        carry = carry + pair
        new[HEAD + r] = cumulative
        at = slice(r % 8, r % 8 + 1)
        for x in range(2):
            tile = x * TABLE + r // 8
            new[FIRST + tile, at] = cumulative[4 * x : 4 * x + 1]
            new[LAST + tile, at] = cumulative[4 * x + 3 : 4 * x + 4]
        if r % 2 == 0:
            even = cumulative
        else:
            lows, highs = mix(even, cumulative)
            x_one[r // 2] = jnp.where(odd_x, lows, highs)
            x_two[r // 2] = jnp.where(odd_x, highs, lows)
        mined.append(tons * ahead)
    for n in range(2 * TABLE):
        y_one[n] = jnp.where(odd_y, new[FIRST + n], new[LAST + n])
        y_two[n] = jnp.where(odd_y, new[LAST + n], new[FIRST + n])
    mined.append(tons)
    sums = half_sums(jnp.concatenate(mined, axis=0))
    lane = lanes(shape)
    total = jnp.where(lane == LANE_TONS, sums[8 * ROWS :], 0.0)
    for r in range(ROWS):
        total = total + jnp.where((lane & 63) == r, sums[8 * r : 8 * r + 8], 0.0)
    total = jnp.sum(total, axis=0, keepdims=True)
    if inner == INNER - 1:
        total = total + jnp.where(lanes((1, 128)) == LANE_PRIMAL, whole(moved), 0.0)
    row[...] = jnp.broadcast_to(total, row.shape)


def primal_first_kernel(primal, dual, const, *rest):
    primal_step(0, table(primal, CAPS), primal[WEIGHT, 0:1], primal, dual, const, *rest)


def primal_kernel(inner, got, primal, dual, const, *rest):
    caps = caps_after(summed_row(got), primal, const)
    primal_step(inner, caps, primal[WEIGHT, 0:1], primal, dual, const, *rest)


def primal_restart_kernel(got, primal, dual, const, *rest):
    mean, weight = restart(summed_row(got), primal, const)
    primal_step(0, mean, weight, primal, dual, const, *rest)


def finish_kernel(got, primal, const, caps_new, weight_new):
    mean, weight = restart(jnp.sum(got[...], axis=0, keepdims=True), primal, const)
    caps_new[...] = mean
    weight_new[...] = jnp.broadcast_to(weight, weight_new.shape)


def dual_tables(primal, const, y_one, y_two, dual, steps, ahead):
    odd_y = const[ODD_Y, 0:1] > 0.5
    periods = period_table()
    weight = primal[WEIGHT, 0:1]
    steps[0] = weight / (2.0 * (periods + 1.0))
    steps[1] = weight / (periods + 1.0)
    new = []
    for n, inside in ((0, FIRST), (1, LAST)):
        new.append([])
        for x in range(2):
            at = 2 * n + x
            one, two = table(y_one, x * TABLE), table(y_two, x * TABLE)
            there = jnp.where(odd_y, two, one) if n else jnp.where(odd_y, one, two)
            ahead[n, x] = down(there)
            here = table(primal, inside + x * TABLE)
            price = table(dual, edge_at(n, x)) + steps[0] * (there - down(here))
            new[n].append(jnp.maximum(price, 0.0) * const[EDGES, at : at + 1])
    return new


def dual_pair(s, primal, const, x_one, x_two, dual, steps, ahead):
    odd = const[ODD_X] > 0.5
    lower = jnp.where(odd, x_one[s], x_two[s])
    upper = jnp.where(odd, x_two[s], x_one[s])
    outside = mix(lower, upper)
    return [dual_row(2 * s + a, outside[a], primal, const, dual, steps, ahead) for a in range(2)]


def dual_row(r, outside, primal, const, dual, steps, ahead_rows):
    one = slice(r, r + 1)
    step = steps[0, one]
    here = primal[HEAD + r]
    under = down(here)
    away = down(outside)
    other = turn(under)
    sub = subs((8, 128))
    after = pltpu.roll(under, 7, 0)
    before = pltpu.roll(under, 1, 0)
    ahead = [
        under,
        jnp.where(low(), other, away),
        jnp.where(low(), away, other),
        jnp.where(
            sub == 3, ahead_rows[1, 0, one], jnp.where(sub == 7, ahead_rows[1, 1, one], after)
        ),
        jnp.where(
            sub == 0, ahead_rows[0, 0, one], jnp.where(sub == 4, ahead_rows[0, 1, one], before)
        ),
    ]
    p = [
        jnp.maximum(dual[PRICES + k * ROWS + r] + step * (here - ahead[k]), 0.0) * const[k]
        for k in range(ARCS)
    ]
    b = jnp.maximum(dual[BOUNDS + r] + steps[1, one] * (here - 1.0), 0.0)
    h = jnp.maximum(dual[HALOS + r] + step * (outside - under), 0.0) * const[HALO]
    return p, b, h


def dual_kernel(primal, const, x_one, x_two, y_one, y_two, dual, new, steps, ahead):
    edges = dual_tables(primal, const, y_one, y_two, dual, steps, ahead)
    for n in range(2):
        for x in range(2):
            put_table(new, edge_at(n, x), edges[n][x])
    carry = jnp.zeros((8, 128), F32)
    for s in reversed(range(ROWS // 2)):
        both = dual_pair(s, primal, const, x_one, x_two, dual, steps, ahead)
        for a in (1, 0):
            carry = put_dual(new, 2 * s + a, *both[a], carry)


def mean_of(one, two, three):
    return (one + two + three) / INNER


def mean_row(r, dual0, dual1, dual, p, b, moved):
    mean = []
    for k in range(ARCS):
        at = PRICES + k * ROWS + r
        mean.append(mean_of(dual1[at], dual[at], p[k]))
        moved = moved + (mean[k] - dual0[at]) ** 2
    b = mean_of(dual1[BOUNDS + r], dual[BOUNDS + r], b)
    return mean, b, moved + (b - dual0[BOUNDS + r]) ** 2


def with_moves(row, moved):
    return row[0:1] + jnp.where(lanes((1, 128)) == LANE_DUAL, whole(moved), 0.0)


def dual_restart_kernel(
    primal, const, x_one, x_two, y_one, y_two, dual, row, dual0_at, dual1_at,
    new, row_new, steps, ahead, dual0, dual1, sems,
):
    copies = fetch([(dual0_at.at[0:HALOS], dual0), (dual1_at.at[0:TAIL], dual1)], sems)
    edges = dual_tables(primal, const, y_one, y_two, dual, steps, ahead)
    for copy in copies:
        copy.wait()
    for n in range(2):
        for x in range(2):
            at = edge_at(n, x)
            put_table(new, at, mean_of(table(dual1, at), table(dual, at), edges[n][x]))
    carry = jnp.zeros((8, 128), F32)
    moved = jnp.zeros((8, 128), F32)
    for s in reversed(range(ROWS // 2)):
        both = dual_pair(s, primal, const, x_one, x_two, dual, steps, ahead)
        for a in (1, 0):
            r = 2 * s + a
            p, b, h = both[a]
            p, b, moved = mean_row(r, dual0, dual1, dual, p, b, moved)
            h = mean_of(dual1[HALOS + r], dual[HALOS + r], h)
            carry = put_dual(new, r, p, b, h, carry)
    row_new[...] = jnp.broadcast_to(with_moves(row, moved), row_new.shape)


def dual_final_kernel(
    primal, const, x_one, x_two, y_one, y_two, dual, row, dual0_at, dual1_at,
    send, steps, ahead, dual0, dual1, sems,
):
    copies = fetch([(dual0_at.at[0:HALOS], dual0), (dual1_at.at[0:HALOS], dual1)], sems)
    dual_tables(primal, const, y_one, y_two, dual, steps, ahead)
    for copy in copies:
        copy.wait()
    moved = jnp.zeros((8, 128), F32)
    for s in range(ROWS // 2):
        both = dual_pair(s, primal, const, x_one, x_two, dual, steps, ahead)
        means = []
        for a in range(2):
            r = 2 * s + a
            p, b, _ = both[a]
            p, b, moved = mean_row(r, dual0, dual1, dual, p, b, moved)
            means.append(p + [b, primal[SHARES + r]])
        for field in range(ROW):
            send[s, field], send[16 + s, field] = mix(means[0][field], means[1][field])
    tile = jnp.broadcast_to(with_moves(row, moved), (8, 128))
    for i in range(TILES):
        send[i, ROW] = tile


def plane_sum_kernel(got, out):
    total = got[0, ROW]
    for i in range(1, TILES):
        total = total + got[i, ROW]
    out[...] = total


def turn_back_kernel(got, share, prec, bound):
    def take(field, target):
        rows = [
            mix(got[member(2 * m), field], got[member(2 * m + 1), field]) for m in range(TILES // 2)
        ]
        for a in range(2):
            turned = jnp.concatenate([pair[a] for pair in rows], axis=0).T
            target(2 * a, turned[0:64])
            target(2 * a + 1, turned[64:128])

    for k in range(ARCS):

        def store(t, v, k=k):
            prec[k, t] = v

        take(k, store)

    def store_bound(t, v):
        bound[t] = v

    def store_share(t, v):
        share[t] = v

    take(BOUND, store_bound)
    take(SHARE, store_share)


def f32(*shape):
    return jax.ShapeDtypeStruct(shape, F32)


VMEM = pl.BlockSpec(memory_space=pltpu.VMEM)
SMEM = pl.BlockSpec(memory_space=pltpu.SMEM)
ANY = pl.BlockSpec(memory_space=pl.ANY)


def call(kernel, outs, scratch=(), scalars=0, far=0, out_space=VMEM, aliases=None, vmem=12):
    def run(*args):
        near = len(args) - scalars - far
        return pl.pallas_call(
            kernel,
            out_shape=[f32(*shape) for shape in outs],
            in_specs=[SMEM] * scalars + [VMEM] * near + [ANY] * far,
            out_specs=[out_space] * len(outs),
            scratch_shapes=[
                pltpu.VMEM(shape, F32) if isinstance(shape, tuple) else shape for shape in scratch
            ],
            input_output_aliases=aliases or {},
            compiler_params=pltpu.CompilerParams(vmem_limit_bytes=vmem * 1024 * 1024),
            cost_estimate=pl.CostEstimate(
                flops=10**6, bytes_accessed=4 * 10**6, transcendentals=0
            ),
        )(*args)

    return run


def semaphores(n):
    return pltpu.SemaphoreType.DMA((n,))


STEP_OUTS = [
    (PRIMAL, 8, 128), (ROWS // 2, 8, 128), (ROWS // 2, 8, 128), (2 * TABLE, 8, 128),
    (2 * TABLE, 8, 128), (DEVICES, 128),
]
STEP_SCRATCH = [(2, ROWS, 128)]
DUAL_ARRAY = (DUAL, 8, 128)
DUAL_SCRATCH = [(2, ROWS, 128), (2, 2, ROWS, 128)]
PACK_VMEM = 62
EVERY = ("strip", "period")


def share_row(row):
    return lax.all_to_all(row, EVERY, 0, 0, tiled=True)


def share_planes(row):
    planes = DEVICES // PLANE
    groups = [[PLANE * z + i for z in range(planes)] for i in range(PLANE)]
    return lax.all_to_all(row, EVERY, 0, 0, axis_index_groups=groups, tiled=True)


def exchange(slots):
    groups = [[PLANE * z + i for i in range(PLANE)] for z in range(DEVICES // PLANE)]
    return lax.all_to_all(slots, EVERY, 0, 0, axis_index_groups=groups)


def swap_x(value, odd):
    planes = DEVICES // PLANE
    pairs = []
    for z in range(planes):
        other = z + 1 if z % 2 == odd else z - 1
        if 0 <= other < planes:
            pairs += [(PLANE * z + i, PLANE * other + i) for i in range(PLANE)]
    return lax.ppermute(value, EVERY, pairs)


def swap_y(value, odd):
    pairs = []
    for j in range(TILES):
        other = j + 1 if j % 2 == odd else j - 1
        if 0 <= other < TILES:
            pairs += [
                (PLANE * z + member(j), PLANE * z + member(other)) for z in range(DEVICES // PLANE)
            ]
    return lax.ppermute(value, EVERY, pairs)


def halo(x_one, x_two, y_one, y_two):
    return swap_x(x_one, 0), swap_x(x_two, 1), swap_y(y_one, 0), swap_y(y_two, 1)


def per_device(
    u_start,
    dual_prec,
    dual_bound,
    dual_cap,
    capacity,
    block_value,
    ton_class,
    density,
    slope_code,
    omega_start,
):
    x, tile = lax.axis_index("strip"), lax.axis_index("period")
    arc = 2 - x % 2
    inside = jnp.where(x % 2 == 1, x + 1 < NX, x >= 1)
    toward = jnp.where(inside, slope_code >> (arc - 1) & 1, 0).astype(F32)[None]
    top = lax.broadcasted_iota(jnp.int32, (4, NZ, NY), 1) == 0
    rim = jnp.where(top, toward, lax.dynamic_index_in_dim(dual_prec[:, 0], arc, 0, False))
    swaps = [(i, i + 1 if i % 2 else i - 1) for i in range(1, NX - 1)]
    rim = lax.ppermute(rim, "strip", swaps)
    place = jnp.stack([x, tile]).astype(jnp.int32)
    small = jnp.concatenate([dual_cap, capacity, density])
    plane = (NZ, NY)
    slots = (TILES, SLOTS, 8, 128)
    (send,) = call(
        pack_kernel,
        [slots],
        [
            pltpu.VMEM((1, NY), jnp.int32), pltpu.VMEM(plane, jnp.int32), plane, (4,) + plane,
            (ARCS, 4) + plane, (4,) + plane, semaphores(6),
        ],
        scalars=2,
        far=6,
        vmem=PACK_VMEM,
    )(
        small, place, slope_code, ton_class[0], block_value[0], u_start[0], dual_prec[:, 0],
        dual_bound[0],
    )
    (send,) = call(
        rim_kernel,
        [slots],
        [(TILES, 8, 128), pltpu.SemaphoreType.DMA],
        far=1,
        out_space=ANY,
        aliases={1: 0},
    )(rim, send)
    got = exchange(send)
    primal, dual, const = call(
        unpack_kernel, [(PRIMAL, 8, 128), DUAL_ARRAY, (CONSTANTS, 8, 128)], scalars=2
    )(omega_start, place, got)
    row_sums = None
    for outer in range(OUTER):
        duals = [dual]
        for inner in range(INNER):
            if inner > 0:
                step = functools.partial(primal_kernel, inner)
            else:
                step = primal_first_kernel if outer == 0 else primal_restart_kernel
            sums = [] if row_sums is None else [row_sums]
            primal, *sides, row = call(step, STEP_OUTS, STEP_SCRATCH)(*sums, primal, dual, const)
            sides = halo(*sides)
            if inner < INNER - 1:
                row_sums = share_row(row)
                (dual,) = call(dual_kernel, [DUAL_ARRAY], DUAL_SCRATCH)(
                    primal, const, *sides, dual
                )
                duals.append(dual)
            elif outer < OUTER - 1:
                dual, row = call(
                    dual_restart_kernel,
                    [DUAL_ARRAY, (DEVICES, 128)],
                    DUAL_SCRATCH + [(HALOS, 8, 128), (TAIL, 8, 128), semaphores(2)],
                    far=2,
                )(primal, const, *sides, dual, row, duals[0], duals[1])
                row_sums = share_row(row)
            else:
                (send,) = call(
                    dual_final_kernel,
                    [(TILES, ROW + 1, 8, 128)],
                    DUAL_SCRATCH + [(HALOS, 8, 128), (HALOS, 8, 128), semaphores(2)],
                    far=2,
                )(primal, const, *sides, dual, row, duals[0], duals[1])
                got = exchange(send)
                (row,) = call(plane_sum_kernel, [(8, 128)])(got)
                row_sums = share_planes(row)
    mined, arcs, bounds = call(
        turn_back_kernel, [(4, NZ, NY), (ARCS, 4, NZ, NY), (4, NZ, NY)]
    )(got)
    caps, weight = call(finish_kernel, [(ROWS, 128), (8, 128)])(row_sums, primal, const)
    own = lax.dynamic_slice(caps, (2 * tile, 0), (2, 128))[:, ::64]
    return (
        mined[None],
        arcs[:, None],
        bounds[None],
        jnp.reshape(own, (4,)),
        weight[0, 0:1],
    )


def solution(mesh):
    in_specs = (
        P("strip", "period", None, None),
        P(None, "strip", "period", None, None),
        P("strip", "period", None, None),
        P("period"),
        P("period"),
        P("strip", None, None),
        P("strip", None, None),
        P(),
        P("strip", None),
        P(),
    )
    out_specs = (
        P("strip", "period", None, None),
        P(None, "strip", "period", None, None),
        P("strip", "period", None, None),
        P("period"),
        P(),
    )
    return jax.shard_map(
        per_device, mesh=mesh, in_specs=in_specs, out_specs=out_specs, check_vma=False
    )
```

time: 239 us -> 231 us (0.967)
  blocking collectives: 82.2 us -> 50.6 us
  waiting for transfers between devices: 29.7 us -> 51.6 us
  starting transfers between devices: 82.8 us -> 91.8 us
  local copies, waits for them, and re-layouts: 20.9 us -> 13.1 us
    all_to_all x2 -> x1, blocking collectives: 55.6 us -> 24 us  [exchange(): return lax.all_to_all(slots, EVERY, 0, 0, axis_index_groups=groups)]
    all_to_all x0 -> x1, waiting for transfers between devices: none -> 17.8 us  [exchange(): return lax.all_to_all(slots, EVERY, 0, 0, axis_index_groups=groups)]
    all_to_all x0 -> x1, starting transfers between devices: none -> 11.9 us  [exchange(): return lax.all_to_all(slots, EVERY, 0, 0, axis_index_groups=groups)]
    unnamed x66 -> x30, local copies, waits for them, and re-layouts: 19.6 us -> 11.9 us
    all_to_all x4, waiting for transfers between devices: 10.4 us -> 14.6 us  [share_row(): return lax.all_to_all(row, EVERY, 0, 0, tiled=True)]
  transfers between devices with their start and end apart: 30 -> 31, of which waited for: 11 -> 12; matrix products, arithmetic and copies ran while one was open for 0% -> 1% of each run, Pallas kernels for 2% -> 3%
where the time goes in v4:
time: 231 us; the launch traced here: 230 us
  starting transfers between devices  91.8 us (40%)
  waiting for transfers between devices  51.6 us (22%)
  blocking collectives  50.6 us (22%)
  Pallas kernels  17.3 us (7%)
  local copies, waits for them, and re-layouts  13.1 us (6%)
  other arithmetic  3.51 us (2%)
    all_to_all x4, starting transfers between devices, share_row(): return lax.all_to_all(row, EVERY, 0, 0, tiled=True)  36.1 us
    all_to_all x1, blocking collectives, share_row(): return lax.all_to_all(row, EVERY, 0, 0, tiled=True)  26.6 us
    all_to_all x1, blocking collectives, exchange(): return lax.all_to_all(slots, EVERY, 0, 0, axis_index_groups=groups)  24 us
    ppermute x12, starting transfers between devices, swap_y(): return lax.ppermute(value, EVERY, pairs)  22 us
    all_to_all x1, waiting for transfers between devices, exchange(): return lax.all_to_all(slots, EVERY, 0, 0, axis_index_groups=groups)  17.8 us
    pallas_call x18, Pallas kernels, run(): pl.pallas_call(kernel, out_shape=[f32(*shape) for shape in outs], in_spec...  17.3 us
    all_to_all x4, waiting for transfers between devices, share_row(): return lax.all_to_all(row, EVERY, 0, 0, tiled=True)  14.6 us
    ppermute x12, waiting for transfers between devices, swap_y(): return lax.ppermute(value, EVERY, pairs)  13.9 us
  transfers between devices with their start and end apart: 31, of which 12 were waited for; matrix products, arithmetic and copies ran while one was open for 1% of the time, Pallas kernels for 3%

profile of v4, /device:TPU:1, one launch (start us, length us, event | category | flops | bytes accessed | tf_op | source)
XLA Modules:
  0.0 229.6 jit_solution(213311769569742755)
XLA Ops:
  4.9 3.3 %shard_map.137.send = f32[32,9,8,128]{3,2,1,0:T(8,128)} custom-call(f32[16]{0:T(128)} %pad_maximum_fusion.small, s32[2]{0:T(128)} %pad_add_fusion.place, s32[1,128]{1,0:T(1,128)} %slope_at.1, s32[64,128]{1,0:T(8,128)} %bitcast.51, f32[64,128]{1,0:T(8,128)} %bitcast.52, f32[4,64,128]{2,1,0:T(8,128)} %bitcast.49, f32[5,4,64,128]{3,2,1,0:T(8,128)} %bitcast.48, ...), custom_call_target="tpu_custom_call" | custom-call | flops 1000000 | bytes 4000000 | tf_op jit(solution)/shard_map/pallas_call | solution.py:599
  10.7 11.9 %all-to-all-start = ((f32[32,9,8,128]{3,2,1,0:T(8,128)}), f32[32,9,8,128]{3,2,1,0:T(8,128)S(1)}, u32[]{:S(2)}, u32[]{:S(2)}) async-start(f32[32,9,8,128]{3,2,1,0:T(8,128)} %copy-done.1), calls=%async_computation | async-start | bytes 2359296 | tf_op jit(solution)/shard_map/all_to_all | solution.py:644
  23.2 17.8 %all-to-all-done.got = f32[32,9,8,128]{3,2,1,0:T(8,128)S(1)} async-done(((f32[32,9,8,128]{3,2,1,0:T(8,128)}), f32[32,9,8,128]{3,2,1,0:T(8,128)S(1)}, u32[]{:S(2)}, u32[]{:S(2)}) %all-to-all-start) | async-done | bytes 1179680 | tf_op jit(solution)/shard_map/all_to_all | solution.py:644
  45.4 11.1 %all-to-all-start.1 = ((f32[256,1,128]{2,1,0:T(1,128)}), f32[256,1,128]{2,1,0:T(1,128)S(1)}, u32[]{:S(2)}, u32[]{:S(2)}) async-start(f32[256,1,128]{2,1,0:T(1,128)} %bitcast.10), calls=%async_computation.1 | async-start | bytes 262144 | tf_op jit(solution)/shard_map/all_to_all | solution.py:633
  59.5 3.0 %collective-permute-start.4 = (f32[8,8,128]{2,1,0:T(8,128)S(1)}, f32[8,8,128]{2,1,0:T(8,128)S(1)}, u32[]{:S(2)}, u32[]{:S(2)}) collective-permute-start(f32[8,8,128]{2,1,0:T(8,128)S(1)} %get-tuple-element.59), channel_id=1, source_target_pairs={{1,4},{33,36},{65,68},{97,100},{129,132},{161,164},{193,196},{225,... | collective-permute-start | bytes 98312 | tf_op jit(solution)/shard_map/ppermute | solution.py:665
  62.6 2.5 %collective-permute-done.4.y_two = f32[8,8,128]{2,1,0:T(8,128)S(1)} collective-permute-done((f32[8,8,128]{2,1,0:T(8,128)S(1)}, f32[8,8,128]{2,1,0:T(8,128)S(1)}, u32[]{:S(2)}, u32[]{:S(2)}) %collective-permute-start.4) | collective-permute-done | bytes 32800 | tf_op jit(solution)/shard_map/ppermute | solution.py:665
  65.6 4.2 %all-to-all-done.1 = f32[256,1,128]{2,1,0:T(1,128)S(1)} async-done(((f32[256,1,128]{2,1,0:T(1,128)}), f32[256,1,128]{2,1,0:T(1,128)S(1)}, u32[]{:S(2)}, u32[]{:S(2)}) %all-to-all-start.1) | async-done | bytes 131104 | tf_op jit(solution)/shard_map/all_to_all | solution.py:633
  72.0 9.8 %all-to-all-start.2 = ((f32[256,1,128]{2,1,0:T(1,128)}), f32[256,1,128]{2,1,0:T(1,128)S(1)}, u32[]{:S(2)}, u32[]{:S(2)}) async-start(f32[256,1,128]{2,1,0:T(1,128)} %bitcast.13), calls=%async_computation.2 | async-start | bytes 262144 | tf_op jit(solution)/shard_map/all_to_all | solution.py:633
  84.8 3.0 %collective-permute-start.8 = (f32[8,8,128]{2,1,0:T(8,128)S(1)}, f32[8,8,128]{2,1,0:T(8,128)S(1)}, u32[]{:S(2)}, u32[]{:S(2)}) collective-permute-start(f32[8,8,128]{2,1,0:T(8,128)S(1)} %get-tuple-element.65), channel_id=1, source_target_pairs={{1,4},{33,36},{65,68},{97,100},{129,132},{161,164},{193,196},{225,... | collective-permute-start | bytes 98312 | tf_op jit(solution)/shard_map/ppermute | solution.py:665
  87.9 2.5 %collective-permute-done.8.y_two = f32[8,8,128]{2,1,0:T(8,128)S(1)} collective-permute-done((f32[8,8,128]{2,1,0:T(8,128)S(1)}, f32[8,8,128]{2,1,0:T(8,128)S(1)}, u32[]{:S(2)}, u32[]{:S(2)}) %collective-permute-start.8) | collective-permute-done | bytes 32800 | tf_op jit(solution)/shard_map/ppermute | solution.py:665
  92.0 3.1 %all-to-all-done.2 = f32[256,1,128]{2,1,0:T(1,128)S(1)} async-done(((f32[256,1,128]{2,1,0:T(1,128)}), f32[256,1,128]{2,1,0:T(1,128)S(1)}, u32[]{:S(2)}, u32[]{:S(2)}) %all-to-all-start.2) | async-done | bytes 131104 | tf_op jit(solution)/shard_map/all_to_all | solution.py:633
  99.4 3.4 %collective-permute-start.12 = (f32[8,8,128]{2,1,0:T(8,128)S(1)}, f32[8,8,128]{2,1,0:T(8,128)S(1)}, u32[]{:S(2)}, u32[]{:S(2)}) collective-permute-start(f32[8,8,128]{2,1,0:T(8,128)S(1)} %get-tuple-element.70), channel_id=1, source_target_pairs={{1,4},{33,36},{65,68},{97,100},{129,132},{161,164},{193,196},{225,... | collective-permute-start | bytes 98312 | tf_op jit(solution)/shard_map/ppermute | solution.py:665
  107.2 26.6 %all_to_all.76 = f32[256,1,128]{2,1,0:T(1,128)S(1)} all-to-all(f32[256,1,128]{2,1,0:T(1,128)S(1)} %bitcast.46), channel_id=1, replica_groups=mesh['strip'=16,'period'=16] {'strip','period'}, dimensions={0} | all-to-all | bytes 262144 | tf_op jit(solution)/shard_map/all_to_all | solution.py:633
  135.3 5.4 %all-to-all-start.4 = ((f32[256,1,128]{2,1,0:T(1,128)}), f32[256,1,128]{2,1,0:T(1,128)S(1)}, u32[]{:S(2)}, u32[]{:S(2)}) async-start(f32[256,1,128]{2,1,0:T(1,128)} %bitcast.19), calls=%async_computation.4 | async-start | bytes 262144 | tf_op jit(solution)/shard_map/all_to_all | solution.py:633
  143.8 3.0 %collective-permute-start.16 = (f32[8,8,128]{2,1,0:T(8,128)S(1)}, f32[8,8,128]{2,1,0:T(8,128)S(1)}, u32[]{:S(2)}, u32[]{:S(2)}) collective-permute-start(f32[8,8,128]{2,1,0:T(8,128)S(1)} %get-tuple-element.79), channel_id=1, source_target_pairs={{1,4},{33,36},{65,68},{97,100},{129,132},{161,164},{193,196},{225,... | collective-permute-start | bytes 98312 | tf_op jit(solution)/shard_map/ppermute | solution.py:665
  146.9 2.5 %collective-permute-done.16.y_two = f32[8,8,128]{2,1,0:T(8,128)S(1)} collective-permute-done((f32[8,8,128]{2,1,0:T(8,128)S(1)}, f32[8,8,128]{2,1,0:T(8,128)S(1)}, u32[]{:S(2)}, u32[]{:S(2)}) %collective-permute-start.16) | collective-permute-done | bytes 32800 | tf_op jit(solution)/shard_map/ppermute | solution.py:665
  149.9 4.2 %all-to-all-done.4 = f32[256,1,128]{2,1,0:T(1,128)S(1)} async-done(((f32[256,1,128]{2,1,0:T(1,128)}), f32[256,1,128]{2,1,0:T(1,128)S(1)}, u32[]{:S(2)}, u32[]{:S(2)}) %all-to-all-start.4) | async-done | bytes 131104 | tf_op jit(solution)/shard_map/all_to_all | solution.py:633
  156.3 9.8 %all-to-all-start.5 = ((f32[256,1,128]{2,1,0:T(1,128)}), f32[256,1,128]{2,1,0:T(1,128)S(1)}, u32[]{:S(2)}, u32[]{:S(2)}) async-start(f32[256,1,128]{2,1,0:T(1,128)} %bitcast.22), calls=%async_computation.5 | async-start | bytes 262144 | tf_op jit(solution)/shard_map/all_to_all | solution.py:633
  169.1 3.0 %collective-permute-start.20 = (f32[8,8,128]{2,1,0:T(8,128)S(1)}, f32[8,8,128]{2,1,0:T(8,128)S(1)}, u32[]{:S(2)}, u32[]{:S(2)}) collective-permute-start(f32[8,8,128]{2,1,0:T(8,128)S(1)} %get-tuple-element.85), channel_id=1, source_target_pairs={{1,4},{33,36},{65,68},{97,100},{129,132},{161,164},{193,196},{225,... | collective-permute-start | bytes 98312 | tf_op jit(solution)/shard_map/ppermute | solution.py:665
  176.3 3.1 %all-to-all-done.5 = f32[256,1,128]{2,1,0:T(1,128)S(1)} async-done(((f32[256,1,128]{2,1,0:T(1,128)}), f32[256,1,128]{2,1,0:T(1,128)S(1)}, u32[]{:S(2)}, u32[]{:S(2)}) %all-to-all-start.5) | async-done | bytes 131104 | tf_op jit(solution)/shard_map/all_to_all | solution.py:633
  183.3 3.4 %collective-permute-start.24 = (f32[8,8,128]{2,1,0:T(8,128)S(1)}, f32[8,8,128]{2,1,0:T(8,128)S(1)}, u32[]{:S(2)}, u32[]{:S(2)}) collective-permute-start(f32[8,8,128]{2,1,0:T(8,128)S(1)} %get-tuple-element.90), channel_id=1, source_target_pairs={{1,4},{33,36},{65,68},{97,100},{129,132},{161,164},{193,196},{225,... | collective-permute-start | bytes 98312 | tf_op jit(solution)/shard_map/ppermute | solution.py:665
  189.3 24.0 %all_to_all.77.got = f32[32,8,8,128]{3,2,1,0:T(8,128)S(1)} all-to-all(f32[32,8,8,128]{3,2,1,0:T(8,128)S(1)} %shard_map.151), channel_id=1, replica_groups={{0,1,2,3,4,5,6,7,8,9,10,11,12,13,14,15,16,17,18,19,20,21,22,23,24,25,26..., dimensions={0} | all-to-all | bytes 2097152 | tf_op jit(solution)/shard_map/all_to_all | solution.py:644
  214.0 7.6 %all-to-all-start.7 = ((f32[8,1,128]{2,1,0:T(1,128)}), f32[8,1,128]{2,1,0:T(1,128)S(1)}, u32[]{:S(2)}, u32[]{:S(2)}) async-start(f32[8,1,128]{2,1,0:T(1,128)} %bitcast.29), calls=%async_computation.7 | async-start | bytes 8192 | tf_op jit(solution)/shard_map/all_to_all | solution.py:639
  222.7 5.4 %all-to-all-done.7 = f32[8,1,128]{2,1,0:T(1,128)S(1)} async-done(((f32[8,1,128]{2,1,0:T(1,128)}), f32[8,1,128]{2,1,0:T(1,128)S(1)}, u32[]{:S(2)}, u32[]{:S(2)}) %all-to-all-start.7) | async-done | bytes 4128 | tf_op jit(solution)/shard_map/all_to_all | solution.py:639
  (97 shorter events, 54.2 us)
Async XLA Ops:
  2.3 5.9 %collective-permute-start = (f32[4,64,128]{2,1,0:T(8,128)S(1)}, f32[4,64,128]{2,1,0:T(8,128)S(1)}, u32[]{:S(2)}, u32[]{:S(2)}) collective-permute-start(f32[4,64,128]{2,1,0:T(8,128)S(1)} %bitcast_select_fusion), channel_id=1, source_target_pairs={{16,32},{32,16},{48,64},{64,48},{80,96},{96,80},{112,128},{128,112... | collective-permute-start | bytes 393224 | tf_op jit(solution)/shard_map/ppermute | solution.py:691
  10.7 30.4 %all-to-all-start = ((f32[32,9,8,128]{3,2,1,0:T(8,128)}), f32[32,9,8,128]{3,2,1,0:T(8,128)S(1)}, u32[]{:S(2)}, u32[]{:S(2)}) async-start(f32[32,9,8,128]{3,2,1,0:T(8,128)} %copy-done.1), calls=%async_computation | async-start | bytes 2359296 | tf_op jit(solution)/shard_map/all_to_all | solution.py:644
  45.4 24.4 %all-to-all-start.1 = ((f32[256,1,128]{2,1,0:T(1,128)}), f32[256,1,128]{2,1,0:T(1,128)S(1)}, u32[]{:S(2)}, u32[]{:S(2)}) async-start(f32[256,1,128]{2,1,0:T(1,128)} %bitcast.10), calls=%async_computation.1 | async-start | bytes 262144 | tf_op jit(solution)/shard_map/all_to_all | solution.py:633
  56.5 8.6 %collective-permute-start.1 = (f32[16,8,128]{2,1,0:T(8,128)S(1)}, f32[16,8,128]{2,1,0:T(8,128)S(1)}, u32[]{:S(2)}, u32[]{:S(2)}) collective-permute-start(f32[16,8,128]{2,1,0:T(8,128)S(1)} %get-tuple-element.56), channel_id=1, source_target_pairs={{0,32},{1,33},{2,34},{3,35},{4,36},{5,37},{6,38},{7,39},{8,40},{9,... | collective-permute-start | bytes 196616 | tf_op jit(solution)/shard_map/ppermute | solution.py:654
  58.1 7.0 %collective-permute-start.2 = (f32[16,8,128]{2,1,0:T(8,128)S(1)}, f32[16,8,128]{2,1,0:T(8,128)S(1)}, u32[]{:S(2)}, u32[]{:S(2)}) collective-permute-start(f32[16,8,128]{2,1,0:T(8,128)S(1)} %get-tuple-element.57), channel_id=1, source_target_pairs={{32,64},{33,65},{34,66},{35,67},{36,68},{37,69},{38,70},{39,71},{4... | collective-permute-start | bytes 196616 | tf_op jit(solution)/shard_map/ppermute | solution.py:654
  59.5 5.6 %collective-permute-start.4 = (f32[8,8,128]{2,1,0:T(8,128)S(1)}, f32[8,8,128]{2,1,0:T(8,128)S(1)}, u32[]{:S(2)}, u32[]{:S(2)}) collective-permute-start(f32[8,8,128]{2,1,0:T(8,128)S(1)} %get-tuple-element.59), channel_id=1, source_target_pairs={{1,4},{33,36},{65,68},{97,100},{129,132},{161,164},{193,196},{225,... | collective-permute-start | bytes 98312 | tf_op jit(solution)/shard_map/ppermute | solution.py:665
  72.0 23.1 %all-to-all-start.2 = ((f32[256,1,128]{2,1,0:T(1,128)}), f32[256,1,128]{2,1,0:T(1,128)S(1)}, u32[]{:S(2)}, u32[]{:S(2)}) async-start(f32[256,1,128]{2,1,0:T(1,128)} %bitcast.13), calls=%async_computation.2 | async-start | bytes 262144 | tf_op jit(solution)/shard_map/all_to_all | solution.py:633
  81.8 8.6 %collective-permute-start.5 = (f32[16,8,128]{2,1,0:T(8,128)S(1)}, f32[16,8,128]{2,1,0:T(8,128)S(1)}, u32[]{:S(2)}, u32[]{:S(2)}) collective-permute-start(f32[16,8,128]{2,1,0:T(8,128)S(1)} %get-tuple-element.62), channel_id=1, source_target_pairs={{0,32},{1,33},{2,34},{3,35},{4,36},{5,37},{6,38},{7,39},{8,40},{9,... | collective-permute-start | bytes 196616 | tf_op jit(solution)/shard_map/ppermute | solution.py:654
  83.4 7.0 %collective-permute-start.6 = (f32[16,8,128]{2,1,0:T(8,128)S(1)}, f32[16,8,128]{2,1,0:T(8,128)S(1)}, u32[]{:S(2)}, u32[]{:S(2)}) collective-permute-start(f32[16,8,128]{2,1,0:T(8,128)S(1)} %get-tuple-element.63), channel_id=1, source_target_pairs={{32,64},{33,65},{34,66},{35,67},{36,68},{37,69},{38,70},{39,71},{4... | collective-permute-start | bytes 196616 | tf_op jit(solution)/shard_map/ppermute | solution.py:654
  84.8 5.6 %collective-permute-start.8 = (f32[8,8,128]{2,1,0:T(8,128)S(1)}, f32[8,8,128]{2,1,0:T(8,128)S(1)}, u32[]{:S(2)}, u32[]{:S(2)}) collective-permute-start(f32[8,8,128]{2,1,0:T(8,128)S(1)} %get-tuple-element.65), channel_id=1, source_target_pairs={{1,4},{33,36},{65,68},{97,100},{129,132},{161,164},{193,196},{225,... | collective-permute-start | bytes 98312 | tf_op jit(solution)/shard_map/ppermute | solution.py:665
  96.9 7.8 %collective-permute-start.9 = (f32[16,8,128]{2,1,0:T(8,128)S(1)}, f32[16,8,128]{2,1,0:T(8,128)S(1)}, u32[]{:S(2)}, u32[]{:S(2)}) collective-permute-start(f32[16,8,128]{2,1,0:T(8,128)S(1)} %get-tuple-element.67), channel_id=1, source_target_pairs={{0,32},{1,33},{2,34},{3,35},{4,36},{5,37},{6,38},{7,39},{8,40},{9,... | collective-permute-start | bytes 196616 | tf_op jit(solution)/shard_map/ppermute | solution.py:654
  98.7 6.0 %collective-permute-start.10 = (f32[16,8,128]{2,1,0:T(8,128)S(1)}, f32[16,8,128]{2,1,0:T(8,128)S(1)}, u32[]{:S(2)}, u32[]{:S(2)}) collective-permute-start(f32[16,8,128]{2,1,0:T(8,128)S(1)} %get-tuple-element.68), channel_id=1, source_target_pairs={{32,64},{33,65},{34,66},{35,67},{36,68},{37,69},{38,70},{39,71},{4... | collective-permute-start | bytes 196616 | tf_op jit(solution)/shard_map/ppermute | solution.py:654
  99.4 5.2 %collective-permute-start.12 = (f32[8,8,128]{2,1,0:T(8,128)S(1)}, f32[8,8,128]{2,1,0:T(8,128)S(1)}, u32[]{:S(2)}, u32[]{:S(2)}) collective-permute-start(f32[8,8,128]{2,1,0:T(8,128)S(1)} %get-tuple-element.70), channel_id=1, source_target_pairs={{1,4},{33,36},{65,68},{97,100},{129,132},{161,164},{193,196},{225,... | collective-permute-start | bytes 98312 | tf_op jit(solution)/shard_map/ppermute | solution.py:665
  135.3 18.9 %all-to-all-start.4 = ((f32[256,1,128]{2,1,0:T(1,128)}), f32[256,1,128]{2,1,0:T(1,128)S(1)}, u32[]{:S(2)}, u32[]{:S(2)}) async-start(f32[256,1,128]{2,1,0:T(1,128)} %bitcast.19), calls=%async_computation.4 | async-start | bytes 262144 | tf_op jit(solution)/shard_map/all_to_all | solution.py:633
  140.7 8.7 %collective-permute-start.13 = (f32[16,8,128]{2,1,0:T(8,128)S(1)}, f32[16,8,128]{2,1,0:T(8,128)S(1)}, u32[]{:S(2)}, u32[]{:S(2)}) collective-permute-start(f32[16,8,128]{2,1,0:T(8,128)S(1)} %get-tuple-element.76), channel_id=1, source_target_pairs={{0,32},{1,33},{2,34},{3,35},{4,36},{5,37},{6,38},{7,39},{8,40},{9,... | collective-permute-start | bytes 196616 | tf_op jit(solution)/shard_map/ppermute | solution.py:654
  142.4 7.0 %collective-permute-start.14 = (f32[16,8,128]{2,1,0:T(8,128)S(1)}, f32[16,8,128]{2,1,0:T(8,128)S(1)}, u32[]{:S(2)}, u32[]{:S(2)}) collective-permute-start(f32[16,8,128]{2,1,0:T(8,128)S(1)} %get-tuple-element.77), channel_id=1, source_target_pairs={{32,64},{33,65},{34,66},{35,67},{36,68},{37,69},{38,70},{39,71},{4... | collective-permute-start | bytes 196616 | tf_op jit(solution)/shard_map/ppermute | solution.py:654
  143.8 5.6 %collective-permute-start.16 = (f32[8,8,128]{2,1,0:T(8,128)S(1)}, f32[8,8,128]{2,1,0:T(8,128)S(1)}, u32[]{:S(2)}, u32[]{:S(2)}) collective-permute-start(f32[8,8,128]{2,1,0:T(8,128)S(1)} %get-tuple-element.79), channel_id=1, source_target_pairs={{1,4},{33,36},{65,68},{97,100},{129,132},{161,164},{193,196},{225,... | collective-permute-start | bytes 98312 | tf_op jit(solution)/shard_map/ppermute | solution.py:665
  156.3 23.1 %all-to-all-start.5 = ((f32[256,1,128]{2,1,0:T(1,128)}), f32[256,1,128]{2,1,0:T(1,128)S(1)}, u32[]{:S(2)}, u32[]{:S(2)}) async-start(f32[256,1,128]{2,1,0:T(1,128)} %bitcast.22), calls=%async_computation.5 | async-start | bytes 262144 | tf_op jit(solution)/shard_map/all_to_all | solution.py:633
  166.1 8.6 %collective-permute-start.17 = (f32[16,8,128]{2,1,0:T(8,128)S(1)}, f32[16,8,128]{2,1,0:T(8,128)S(1)}, u32[]{:S(2)}, u32[]{:S(2)}) collective-permute-start(f32[16,8,128]{2,1,0:T(8,128)S(1)} %get-tuple-element.82), channel_id=1, source_target_pairs={{0,32},{1,33},{2,34},{3,35},{4,36},{5,37},{6,38},{7,39},{8,40},{9,... | collective-permute-start | bytes 196616 | tf_op jit(solution)/shard_map/ppermute | solution.py:654
  167.7 7.0 %collective-permute-start.18 = (f32[16,8,128]{2,1,0:T(8,128)S(1)}, f32[16,8,128]{2,1,0:T(8,128)S(1)}, u32[]{:S(2)}, u32[]{:S(2)}) collective-permute-start(f32[16,8,128]{2,1,0:T(8,128)S(1)} %get-tuple-element.83), channel_id=1, source_target_pairs={{32,64},{33,65},{34,66},{35,67},{36,68},{37,69},{38,70},{39,71},{4... | collective-permute-start | bytes 196616 | tf_op jit(solution)/shard_map/ppermute | solution.py:654
  169.1 5.6 %collective-permute-start.20 = (f32[8,8,128]{2,1,0:T(8,128)S(1)}, f32[8,8,128]{2,1,0:T(8,128)S(1)}, u32[]{:S(2)}, u32[]{:S(2)}) collective-permute-start(f32[8,8,128]{2,1,0:T(8,128)S(1)} %get-tuple-element.85), channel_id=1, source_target_pairs={{1,4},{33,36},{65,68},{97,100},{129,132},{161,164},{193,196},{225,... | collective-permute-start | bytes 98312 | tf_op jit(solution)/shard_map/ppermute | solution.py:665
  181.2 7.3 %collective-permute-start.21 = (f32[16,8,128]{2,1,0:T(8,128)S(1)}, f32[16,8,128]{2,1,0:T(8,128)S(1)}, u32[]{:S(2)}, u32[]{:S(2)}) collective-permute-start(f32[16,8,128]{2,1,0:T(8,128)S(1)} %get-tuple-element.87), channel_id=1, source_target_pairs={{0,32},{1,33},{2,34},{3,35},{4,36},{5,37},{6,38},{7,39},{8,40},{9,... | collective-permute-start | bytes 196616 | tf_op jit(solution)/shard_map/ppermute | solution.py:654
  182.6 6.0 %collective-permute-start.22 = (f32[16,8,128]{2,1,0:T(8,128)S(1)}, f32[16,8,128]{2,1,0:T(8,128)S(1)}, u32[]{:S(2)}, u32[]{:S(2)}) collective-permute-start(f32[16,8,128]{2,1,0:T(8,128)S(1)} %get-tuple-element.88), channel_id=1, source_target_pairs={{32,64},{33,65},{34,66},{35,67},{36,68},{37,69},{38,70},{39,71},{4... | collective-permute-start | bytes 196616 | tf_op jit(solution)/shard_map/ppermute | solution.py:654
  214.0 14.1 %all-to-all-start.7 = ((f32[8,1,128]{2,1,0:T(1,128)}), f32[8,1,128]{2,1,0:T(1,128)S(1)}, u32[]{:S(2)}, u32[]{:S(2)}) async-start(f32[8,1,128]{2,1,0:T(1,128)} %bitcast.29), calls=%async_computation.7 | async-start | bytes 8192 | tf_op jit(solution)/shard_map/all_to_all | solution.py:639
  (22 other events, 106.3 us)

commit v5 on v4

--- a/solution.py
+++ b/solution.py
@@ -28,7 +28,7 @@
 ARCS = 5
 BOUND, SHARE, RIM, EXTRA = 5, 6, 7, 8
 SLOTS = 9
-LANE_PRIMAL, LANE_DUAL, LANE_TONS = 40, 41, 42
+LANE_PRIMAL, LANE_DUAL, LANE_TONS = 32, 33, 34
 HALO, EDGES, TONS, VALUE, ODD_X, ODD_Y, LIMITS = 5, 6, 7, 8, 9, 10, 11
 CONSTANTS = 15
 TABLE = ROWS // 8
@@ -38,11 +38,11 @@
 FIRST = WEIGHT + 1
 LAST = FIRST + 2 * TABLE
 PRIMAL = LAST + 2 * TABLE
-PRICES, BOUNDS, HALOS = 0, ARCS * ROWS, (ARCS + 1) * ROWS
-EDGE_ROWS = (ARCS + 2) * ROWS
-TAIL = EDGE_ROWS + 4 * TABLE
-DUAL = TAIL + ROWS
-ROW = 7
+PRICES, BOUNDS = 0, ARCS * ROWS
+DUAL = BOUNDS + ROWS
+HALOS, EDGE_ROWS = 0, ROWS
+INWARD = EDGE_ROWS + 4 * TABLE
+BACK = 7
 
 
 def member(tile):
@@ -140,23 +140,34 @@
         target(member(2 * m + 1), odd)
 
 
+def rim_kernel(slope_at, prec_at, rim, slope, sems):
+    x = lax.axis_index("strip")
+    odd = x % 2
+    arc = 2 - odd
+    copies = fetch([(slope_at, slope), (prec_at.at[arc], rim)], sems)
+    inside = jnp.where(odd == 1, x + 1 < NX, x >= 1).astype(jnp.int32)
+    for copy in copies:
+        copy.wait()
+    toward = ((slope[...] >> (arc - 1)) & inside).astype(F32)
+    for t in range(rim.shape[0]):
+        rim[t, 0:1] = toward
+
+
 def pack_kernel(
-    small, place, slope_at, ton_class_at, value_at, share_at, prec_at, bound_at,
-    out, slope, ton_class, value, share, prec, bound, sems,
+    caps_at, limits_at, density_at, slope_at, ton_class_at, value_at, share_at, prec_at, bound_at,
+    out, caps, limits, density, slope, ton_class, value, share, prec, bound, sems,
 ):
     copies = fetch(
         [
             (slope_at, slope), (ton_class_at, ton_class), (value_at, value), (prec_at, prec),
-            (bound_at, bound), (share_at, share),
+            (bound_at, bound), (share_at, share), (caps_at, caps), (limits_at, limits),
+            (density_at, density),
         ],
         sems,
     )
-    caps = [small[t] for t in range(4)]
-    limits = [small[4 + t] for t in range(4)]
-    density = [small[8 + c] for c in range(8)]
     for copy in copies:
         copy.wait()
-    x = place[0]
+    x = lax.axis_index("strip")
     row = (1, 128)
     code = slope[...]
     column = lanes(row)
@@ -203,20 +214,22 @@
                 out[i, EXTRA, 2 + a : 3 + a] = zero
 
 
-def rim_kernel(rim, send, out, tiles, sem):
+def put_rim_kernel(rim_at, send, out, rim, tiles, sems):
+    (copy,) = fetch([(rim_at, rim)], sems)
+    copy.wait()
+
     def target(slot, tile):
         tiles[slot] = tile
 
     put_tiles(lambda t: rim[t], target)
-    copy = pltpu.make_async_copy(tiles, out.at[:, RIM], sem)
-    copy.start()
+    (copy,) = fetch([(tiles, out.at[:, RIM])], sems)
     copy.wait()
 
 
-def adjoint_row(prices, bound, halo, dual, r, carry):
+def adjoint_row(prices, bound, halo, inward, r, carry):
     shape = (8, 128)
     sub = subs(shape)
-    edge = [[line(dual, edge_at(n, x), r) for x in range(2)] for n in range(2)]
+    edge = [[line(inward, edge_at(n, x), r) for x in range(2)] for n in range(2)]
     total = prices[0] + prices[1] + prices[2] + prices[3] + prices[4] + bound
     across = turn(jnp.where(low(), prices[1], prices[2]))
     before = pltpu.roll(prices[3], 1, 0)
@@ -229,20 +242,20 @@
     return carry + jnp.where(later_half(shape), g, pair), carry + pair
 
 
-def put_dual(dual, r, prices, bound, halo, carry):
+def put_dual(dual, inward, tail, r, prices, bound, halo, carry):
     for k in range(ARCS):
         dual[PRICES + k * ROWS + r] = prices[k]
     dual[BOUNDS + r] = bound
-    dual[HALOS + r] = halo
-    dual[TAIL + r], carry = adjoint_row(prices, bound, halo, dual, r, carry)
+    inward[HALOS + r] = halo
+    tail[r], carry = adjoint_row(prices, bound, halo, inward, r, carry)
     return carry
 
 
-def unpack_kernel(small, place, got, primal, dual, const):
+def unpack_kernel(got, weight, primal, dual, inward, tail, const):
     shape = (8, 128)
-    primal[WEIGHT] = jnp.full(shape, small[0])
-    const[ODD_X] = jnp.full(shape, place[0] // 2 % 2).astype(F32)
-    const[ODD_Y] = jnp.full(shape, place[1] % 2).astype(F32)
+    primal[WEIGHT] = jnp.broadcast_to(weight[...], shape)
+    const[ODD_X] = jnp.full(shape, lax.axis_index("strip") // 2 % 2).astype(F32)
+    const[ODD_Y] = jnp.full(shape, lax.axis_index("period") % 2).astype(F32)
     lane = lanes(shape)
     deep = ((lane & 63) >= 1).astype(F32)
     half = later_half(shape)
@@ -270,7 +283,7 @@
             for x in range(2):
                 at = 2 * n + x
                 edge = got[16 * x + s, EXTRA, 2 * n : 2 * n + 2]
-                dual[edge_at(n, x) + tile, within] = edge * const[EDGES, at : at + 1]
+                inward[edge_at(n, x) + tile, within] = edge * const[EDGES, at : at + 1]
     carry = jnp.zeros(shape, F32)
     for s in reversed(range(ROWS // 2)):
         p = [pair(s, k) for k in range(ARCS)]
@@ -287,7 +300,7 @@
             const[LIMITS + r // 8, at] = spare[1:2]
             primal[SHARES + r] = u[a]
             here = [p[k][a] * const[k] for k in range(ARCS)]
-            carry = put_dual(dual, r, here, b[a], h[a] * const[HALO], carry)
+            carry = put_dual(dual, inward, tail, r, here, b[a], h[a] * const[HALO], carry)
 
 
 def summed_row(got):
@@ -323,7 +336,7 @@
     return mean, jnp.sqrt(weight * jnp.sqrt((dual_move + EPS) / (primal_move + EPS)))
 
 
-def primal_step(inner, caps, weight, primal, dual, const, new, x_one, x_two, y_one, y_two, row, rates):
+def primal_step(inner, caps, weight, primal, tail, const, new, x_one, x_two, y_one, y_two, row, rates):
     shape = (8, 128)
     tons = const[TONS]
     value = const[VALUE]
@@ -345,7 +358,7 @@
     moved = jnp.zeros(shape, F32)
     mined = []
     for r in range(ROWS):
-        gradient = dual[TAIL + r] + tons * line(new, CAPS, r) / ROOT
+        gradient = tail[r] + tons * line(new, CAPS, r) / ROOT
         tau = 1.0 / (weight * (rates[1, r : r + 1] + lean))
         old = primal[SHARES + r]
         now = jnp.maximum(old - tau * (gradient - value * rates[0, r : r + 1]), 0.0)
@@ -393,27 +406,31 @@
     row[...] = jnp.broadcast_to(total, row.shape)
 
 
-def primal_first_kernel(primal, dual, const, *rest):
-    primal_step(0, table(primal, CAPS), primal[WEIGHT, 0:1], primal, dual, const, *rest)
-
-
-def primal_kernel(inner, got, primal, dual, const, *rest):
+def primal_first_kernel(primal, tail, const, *rest):
+    primal_step(0, table(primal, CAPS), primal[WEIGHT, 0:1], primal, tail, const, *rest)
+
+
+def primal_kernel(inner, got, primal, tail, const, *rest):
     caps = caps_after(summed_row(got), primal, const)
-    primal_step(inner, caps, primal[WEIGHT, 0:1], primal, dual, const, *rest)
-
-
-def primal_restart_kernel(got, primal, dual, const, *rest):
+    primal_step(inner, caps, primal[WEIGHT, 0:1], primal, tail, const, *rest)
+
+
+def primal_restart_kernel(got, primal, tail, const, *rest):
     mean, weight = restart(summed_row(got), primal, const)
-    primal_step(0, mean, weight, primal, dual, const, *rest)
+    primal_step(0, mean, weight, primal, tail, const, *rest)
 
 
 def finish_kernel(got, primal, const, caps_new, weight_new):
     mean, weight = restart(jnp.sum(got[...], axis=0, keepdims=True), primal, const)
-    caps_new[...] = mean
-    weight_new[...] = jnp.broadcast_to(weight, weight_new.shape)
-
-
-def dual_tables(primal, const, y_one, y_two, dual, steps, ahead):
+    own = lax.axis_index("period")
+    shape = mean.shape
+    for t in range(4):
+        here = (subs(shape) == 2 * own + t // 2) & (lanes(shape) == 64 * (t % 2))
+        caps_new[t] = jnp.sum(jnp.where(here, mean, 0.0))
+    weight_new[0] = jnp.max(weight)
+
+
+def dual_tables(primal, const, y_one, y_two, inward, steps, ahead):
     odd_y = const[ODD_Y, 0:1] > 0.5
     periods = period_table()
     weight = primal[WEIGHT, 0:1]
@@ -428,20 +445,23 @@
             there = jnp.where(odd_y, two, one) if n else jnp.where(odd_y, one, two)
             ahead[n, x] = down(there)
             here = table(primal, inside + x * TABLE)
-            price = table(dual, edge_at(n, x)) + steps[0] * (there - down(here))
+            price = table(inward, edge_at(n, x)) + steps[0] * (there - down(here))
             new[n].append(jnp.maximum(price, 0.0) * const[EDGES, at : at + 1])
     return new
 
 
-def dual_pair(s, primal, const, x_one, x_two, dual, steps, ahead):
+def dual_pair(s, primal, const, x_one, x_two, dual, inward, steps, ahead):
     odd = const[ODD_X] > 0.5
     lower = jnp.where(odd, x_one[s], x_two[s])
     upper = jnp.where(odd, x_two[s], x_one[s])
     outside = mix(lower, upper)
-    return [dual_row(2 * s + a, outside[a], primal, const, dual, steps, ahead) for a in range(2)]
-
-
-def dual_row(r, outside, primal, const, dual, steps, ahead_rows):
+    return [
+        dual_row(2 * s + a, outside[a], primal, const, dual, inward, steps, ahead)
+        for a in range(2)
+    ]
+
+
+def dual_row(r, outside, primal, const, dual, inward, steps, ahead_rows):
     one = slice(r, r + 1)
     step = steps[0, one]
     here = primal[HEAD + r]
@@ -467,20 +487,40 @@
         for k in range(ARCS)
     ]
     b = jnp.maximum(dual[BOUNDS + r] + steps[1, one] * (here - 1.0), 0.0)
-    h = jnp.maximum(dual[HALOS + r] + step * (outside - under), 0.0) * const[HALO]
+    h = jnp.maximum(inward[HALOS + r] + step * (outside - under), 0.0) * const[HALO]
     return p, b, h
 
 
-def dual_kernel(primal, const, x_one, x_two, y_one, y_two, dual, new, steps, ahead):
-    edges = dual_tables(primal, const, y_one, y_two, dual, steps, ahead)
+def dual_kernel(
+    primal, const, x_one, x_two, y_one, y_two, dual, inward, new, inward_new, tail, steps, ahead
+):
+    edges = dual_tables(primal, const, y_one, y_two, inward, steps, ahead)
     for n in range(2):
         for x in range(2):
-            put_table(new, edge_at(n, x), edges[n][x])
+            put_table(inward_new, edge_at(n, x), edges[n][x])
     carry = jnp.zeros((8, 128), F32)
     for s in reversed(range(ROWS // 2)):
-        both = dual_pair(s, primal, const, x_one, x_two, dual, steps, ahead)
+        both = dual_pair(s, primal, const, x_one, x_two, dual, inward, steps, ahead)
         for a in (1, 0):
-            carry = put_dual(new, 2 * s + a, *both[a], carry)
+            carry = put_dual(new, inward_new, tail, 2 * s + a, *both[a], carry)
+
+
+def start_kernel(
+    got, weight, dual, inward, const, new, x_one, x_two, y_one, y_two, row, primal, tail, rates
+):
+    unpack_kernel(got, weight, primal, dual, inward, tail, const)
+    primal_first_kernel(primal, tail, const, new, x_one, x_two, y_one, y_two, row, rates)
+
+
+def step_kernel(
+    inner, got, primal, const, x_one, x_two, y_one, y_two, dual, inward, dual_new, inward_new, *rest
+):
+    *outs, rates, steps, ahead, tail = rest
+    dual_kernel(
+        primal, const, x_one, x_two, y_one, y_two, dual, inward, dual_new, inward_new, tail, steps,
+        ahead,
+    )
+    primal_kernel(inner, got, primal, tail, const, *outs, rates)
 
 
 def mean_of(one, two, three):
@@ -502,59 +542,72 @@
 
 
 def dual_restart_kernel(
-    primal, const, x_one, x_two, y_one, y_two, dual, row, dual0_at, dual1_at,
-    new, row_new, steps, ahead, dual0, dual1, sems,
+    primal, const, x_one, x_two, y_one, y_two, dual, inward, row, inward1, dual0, dual1,
+    new, inward_new, tail, row_new, steps, ahead,
 ):
-    copies = fetch([(dual0_at.at[0:HALOS], dual0), (dual1_at.at[0:TAIL], dual1)], sems)
-    edges = dual_tables(primal, const, y_one, y_two, dual, steps, ahead)
-    for copy in copies:
-        copy.wait()
+    edges = dual_tables(primal, const, y_one, y_two, inward, steps, ahead)
     for n in range(2):
         for x in range(2):
             at = edge_at(n, x)
-            put_table(new, at, mean_of(table(dual1, at), table(dual, at), edges[n][x]))
+            mean = mean_of(table(inward1, at), table(inward, at), edges[n][x])
+            put_table(inward_new, at, mean)
     carry = jnp.zeros((8, 128), F32)
     moved = jnp.zeros((8, 128), F32)
     for s in reversed(range(ROWS // 2)):
-        both = dual_pair(s, primal, const, x_one, x_two, dual, steps, ahead)
+        both = dual_pair(s, primal, const, x_one, x_two, dual, inward, steps, ahead)
         for a in (1, 0):
             r = 2 * s + a
             p, b, h = both[a]
             p, b, moved = mean_row(r, dual0, dual1, dual, p, b, moved)
-            h = mean_of(dual1[HALOS + r], dual[HALOS + r], h)
-            carry = put_dual(new, r, p, b, h, carry)
+            h = mean_of(inward1[HALOS + r], inward[HALOS + r], h)
+            carry = put_dual(new, inward_new, tail, r, p, b, h, carry)
     row_new[...] = jnp.broadcast_to(with_moves(row, moved), row_new.shape)
 
 
+def spread_row(row):
+    shape = (ROWS + 8, 128)
+    spread = jnp.where((lanes(shape) & 63) == subs(shape), jnp.broadcast_to(row, shape), 0.0)
+    return half_sums(spread)
+
+
 def dual_final_kernel(
-    primal, const, x_one, x_two, y_one, y_two, dual, row, dual0_at, dual1_at,
-    send, steps, ahead, dual0, dual1, sems,
+    primal, const, x_one, x_two, y_one, y_two, dual, inward, row, dual0, dual1,
+    send, steps, ahead,
 ):
-    copies = fetch([(dual0_at.at[0:HALOS], dual0), (dual1_at.at[0:HALOS], dual1)], sems)
-    dual_tables(primal, const, y_one, y_two, dual, steps, ahead)
-    for copy in copies:
-        copy.wait()
+    dual_tables(primal, const, y_one, y_two, inward, steps, ahead)
     moved = jnp.zeros((8, 128), F32)
     for s in range(ROWS // 2):
-        both = dual_pair(s, primal, const, x_one, x_two, dual, steps, ahead)
+        both = dual_pair(s, primal, const, x_one, x_two, dual, inward, steps, ahead)
         means = []
         for a in range(2):
             r = 2 * s + a
             p, b, _ = both[a]
             p, b, moved = mean_row(r, dual0, dual1, dual, p, b, moved)
             means.append(p + [b, primal[SHARES + r]])
-        for field in range(ROW):
+        for field in range(ARCS, BACK):
             send[s, field], send[16 + s, field] = mix(means[0][field], means[1][field])
-    tile = jnp.broadcast_to(with_moves(row, moved), (8, 128))
-    for i in range(TILES):
-        send[i, ROW] = tile
+        for k in range(ARCS):
+            send[s, k], send[16 + s, k] = mix(means[0][k], means[1][k])
+    sums = spread_row(with_moves(row, moved))
+    top = (lanes((8, 128)) & 63) == 0
+    for k in range(ARCS):
+        tile = sums[8 * k : 8 * k + 8]
+        for i in range(TILES):
+            send[i, k] = jnp.where(top, tile, send[i, k])
 
 
 def plane_sum_kernel(got, out):
-    total = got[0, ROW]
-    for i in range(1, TILES):
-        total = total + got[i, ROW]
-    out[...] = total
+    top = (lanes((8, 128)) & 63) == 0
+    tiles = []
+    for k in range(ARCS):
+        total = got[0, k]
+        for i in range(1, TILES):
+            total = total + got[i, k]
+        tiles.append(jnp.where(top, total, 0.0))
+    sums = half_sums(jnp.concatenate(tiles, axis=0))
+    shape = sums.shape
+    row = jnp.sum(jnp.where((lanes(shape) & 63) == subs(shape), sums, 0.0), axis=0, keepdims=True)
+    out[...] = jnp.broadcast_to(row, out.shape)
 
 
 def turn_back_kernel(got, share, prec, bound):
@@ -570,7 +623,7 @@
     for k in range(ARCS):
 
         def store(t, v, k=k):
-            prec[k, t] = v
+            prec[k, t] = jnp.where(subs(v.shape) == 0, 0.0, v)
 
         take(k, store)
 
@@ -593,14 +646,13 @@
 ANY = pl.BlockSpec(memory_space=pl.ANY)
 
 
-def call(kernel, outs, scratch=(), scalars=0, far=0, out_space=VMEM, aliases=None, vmem=12):
+def call(kernel, outs, scratch=(), far=0, out_spaces=None, aliases=None, vmem=12):
     def run(*args):
-        near = len(args) - scalars - far
         return pl.pallas_call(
             kernel,
             out_shape=[f32(*shape) for shape in outs],
-            in_specs=[SMEM] * scalars + [VMEM] * near + [ANY] * far,
-            out_specs=[out_space] * len(outs),
+            in_specs=[VMEM] * (len(args) - far) + [ANY] * far,
+            out_specs=out_spaces or [VMEM] * len(outs),
             scratch_shapes=[
                 pltpu.VMEM(shape, F32) if isinstance(shape, tuple) else shape for shape in scratch
             ],
@@ -624,8 +676,11 @@
 ]
 STEP_SCRATCH = [(2, ROWS, 128)]
 DUAL_ARRAY = (DUAL, 8, 128)
+INWARD_ARRAY = (INWARD, 8, 128)
+TAIL_ARRAY = (ROWS, 8, 128)
+DUAL_OUTS = [DUAL_ARRAY, INWARD_ARRAY, TAIL_ARRAY]
 DUAL_SCRATCH = [(2, ROWS, 128), (2, 2, ROWS, 128)]
-PACK_VMEM = 62
+ALL_VMEM = 62
 EVERY = ("strip", "period")
 
 
@@ -666,7 +721,8 @@
 
 
 def halo(x_one, x_two, y_one, y_two):
-    return swap_x(x_one, 0), swap_x(x_two, 1), swap_y(y_one, 0), swap_y(y_two, 1)
+    y_one, y_two = swap_y(y_one, 0), swap_y(y_two, 1)
+    return swap_x(x_one, 0), swap_x(x_two, 1), y_one, y_two
 
 
 def per_device(
@@ -681,90 +737,84 @@
     slope_code,
     omega_start,
 ):
-    x, tile = lax.axis_index("strip"), lax.axis_index("period")
-    arc = 2 - x % 2
-    inside = jnp.where(x % 2 == 1, x + 1 < NX, x >= 1)
-    toward = jnp.where(inside, slope_code >> (arc - 1) & 1, 0).astype(F32)[None]
-    top = lax.broadcasted_iota(jnp.int32, (4, NZ, NY), 1) == 0
-    rim = jnp.where(top, toward, lax.dynamic_index_in_dim(dual_prec[:, 0], arc, 0, False))
+    plane = (NZ, NY)
+    slots = (TILES, SLOTS, 8, 128)
+    prec = dual_prec[:, 0]
+    ints = pltpu.VMEM((1, NY), jnp.int32)
+    (rim,) = call(rim_kernel, [(4,) + plane], [ints, semaphores(2)], far=2, vmem=ALL_VMEM)(
+        slope_code, prec
+    )
     swaps = [(i, i + 1 if i % 2 else i - 1) for i in range(1, NX - 1)]
     rim = lax.ppermute(rim, "strip", swaps)
-    place = jnp.stack([x, tile]).astype(jnp.int32)
-    small = jnp.concatenate([dual_cap, capacity, density])
-    plane = (NZ, NY)
-    slots = (TILES, SLOTS, 8, 128)
     (send,) = call(
         pack_kernel,
         [slots],
         [
-            pltpu.VMEM((1, NY), jnp.int32), pltpu.VMEM(plane, jnp.int32), plane, (4,) + plane,
-            (ARCS, 4) + plane, (4,) + plane, semaphores(6),
+            pltpu.SMEM((4,), F32), pltpu.SMEM((4,), F32), pltpu.SMEM((8,), F32), ints,
+            pltpu.VMEM(plane, jnp.int32), plane, (4,) + plane, (ARCS, 4) + plane, (4,) + plane,
+            semaphores(9),
         ],
-        scalars=2,
-        far=6,
-        vmem=PACK_VMEM,
+        far=9,
+        vmem=ALL_VMEM,
     )(
-        small, place, slope_code, ton_class[0], block_value[0], u_start[0], dual_prec[:, 0],
+        dual_cap, capacity, density, slope_code, ton_class[0], block_value[0], u_start[0], prec,
         dual_bound[0],
     )
     (send,) = call(
-        rim_kernel,
+        put_rim_kernel,
         [slots],
-        [(TILES, 8, 128), pltpu.SemaphoreType.DMA],
-        far=1,
-        out_space=ANY,
+        [(4,) + plane, (TILES, 8, 128), semaphores(1)],
+        far=2,
+        out_spaces=[ANY],
         aliases={1: 0},
+        vmem=ALL_VMEM,
     )(rim, send)
     got = exchange(send)
-    primal, dual, const = call(
-        unpack_kernel, [(PRIMAL, 8, 128), DUAL_ARRAY, (CONSTANTS, 8, 128)], scalars=2
-    )(omega_start, place, got)
-    row_sums = None
+    dual, inward, const, primal, *sides, row = call(
+        start_kernel,
+        [DUAL_ARRAY, INWARD_ARRAY, (CONSTANTS, 8, 128)] + STEP_OUTS,
+        [(PRIMAL, 8, 128), TAIL_ARRAY] + STEP_SCRATCH,
+    )(got, jnp.reshape(omega_start, (1, 1)))
     for outer in range(OUTER):
-        duals = [dual]
-        for inner in range(INNER):
-            if inner > 0:
-                step = functools.partial(primal_kernel, inner)
-            else:
-                step = primal_first_kernel if outer == 0 else primal_restart_kernel
-            sums = [] if row_sums is None else [row_sums]
-            primal, *sides, row = call(step, STEP_OUTS, STEP_SCRATCH)(*sums, primal, dual, const)
-            sides = halo(*sides)
-            if inner < INNER - 1:
-                row_sums = share_row(row)
-                (dual,) = call(dual_kernel, [DUAL_ARRAY], DUAL_SCRATCH)(
-                    primal, const, *sides, dual
-                )
-                duals.append(dual)
-            elif outer < OUTER - 1:
-                dual, row = call(
-                    dual_restart_kernel,
-                    [DUAL_ARRAY, (DEVICES, 128)],
-                    DUAL_SCRATCH + [(HALOS, 8, 128), (TAIL, 8, 128), semaphores(2)],
-                    far=2,
-                )(primal, const, *sides, dual, row, duals[0], duals[1])
-                row_sums = share_row(row)
-            else:
-                (send,) = call(
-                    dual_final_kernel,
-                    [(TILES, ROW + 1, 8, 128)],
-                    DUAL_SCRATCH + [(HALOS, 8, 128), (HALOS, 8, 128), semaphores(2)],
-                    far=2,
-                )(primal, const, *sides, dual, row, duals[0], duals[1])
-                got = exchange(send)
-                (row,) = call(plane_sum_kernel, [(8, 128)])(got)
-                row_sums = share_planes(row)
+        if outer > 0:
+            primal, *sides, row = call(primal_restart_kernel, STEP_OUTS, STEP_SCRATCH)(
+                row_sums, primal, tail, const
+            )
+        duals, inwards = [dual], [inward]
+        for inner in range(1, INNER):
+            row_sums = share_row(row)
+            dual, inward, primal, *sides, row = call(
+                functools.partial(step_kernel, inner),
+                [DUAL_ARRAY, INWARD_ARRAY] + STEP_OUTS,
+                STEP_SCRATCH + DUAL_SCRATCH + [TAIL_ARRAY],
+            )(row_sums, primal, const, *halo(*sides), dual, inward)
+            duals.append(dual)
+            inwards.append(inward)
+        sides = halo(*sides)
+        if outer < OUTER - 1:
+            dual, inward, tail, row = call(
+                dual_restart_kernel, DUAL_OUTS + [(DEVICES, 128)], DUAL_SCRATCH
+            )(primal, const, *sides, dual, inward, row, inwards[1], duals[0], duals[1])
+            row_sums = share_row(row)
+        else:
+            (send,) = call(dual_final_kernel, [(TILES, BACK, 8, 128)], DUAL_SCRATCH)(
+                primal, const, *sides, dual, inward, row, duals[0], duals[1]
+            )
+            got = exchange(send)
+            (row,) = call(plane_sum_kernel, [(8, 128)])(got)
+            row_sums = share_planes(row)
     mined, arcs, bounds = call(
         turn_back_kernel, [(4, NZ, NY), (ARCS, 4, NZ, NY), (4, NZ, NY)]
     )(got)
-    caps, weight = call(finish_kernel, [(ROWS, 128), (8, 128)])(row_sums, primal, const)
-    own = lax.dynamic_slice(caps, (2 * tile, 0), (2, 128))[:, ::64]
+    caps, weight = call(finish_kernel, [(4,), (1,)], out_spaces=[SMEM, SMEM])(
+        row_sums, primal, const
+    )
     return (
         mined[None],
         arcs[:, None],
         bounds[None],
-        jnp.reshape(own, (4,)),
-        weight[0, 0:1],
+        caps,
+        weight,
     )
 
 

time: 231 us -> 227 us (0.983)
  other arithmetic: 3.51 us -> 0 us
  blocking collectives: 50.6 us -> 47.9 us
  waiting for transfers between devices: 51.6 us -> 54.2 us
    pallas_call x18 -> x14, Pallas kernels: 17.3 us -> 18 us  [run(): pl.pallas_call(kernel, out_shape=[f32(*shape) for shape in outs], in_spec...]
    unnamed x30 -> x36, local copies, waits for them, and re-layouts: 11.9 us -> 11.6 us
  transfers between devices with their start and end apart: 31 -> 31, of which waited for: 12 -> 12; matrix products, arithmetic and copies ran while one was open for 1% -> 0% of each run, Pallas kernels for 3% -> 2%
where the time goes in v5:
time: 227 us; the launch traced here: 226 us
  starting transfers between devices  92.9 us (41%)
  waiting for transfers between devices  54.2 us (24%)
  blocking collectives  47.9 us (21%)
  Pallas kernels  18 us (8%)
  local copies, waits for them, and re-layouts  11.6 us (5%)
    all_to_all x4, starting transfers between devices, share_row(): return lax.all_to_all(row, EVERY, 0, 0, tiled=True)  37.6 us
    all_to_all x1, blocking collectives, share_row(): return lax.all_to_all(row, EVERY, 0, 0, tiled=True)  25.3 us
    all_to_all x1, blocking collectives, exchange(): return lax.all_to_all(slots, EVERY, 0, 0, axis_index_groups=groups)  22.6 us
    ppermute x12, starting transfers between devices, swap_y(): return lax.ppermute(value, EVERY, pairs)  21.2 us
    pallas_call x14, Pallas kernels, run(): pl.pallas_call(kernel, out_shape=[f32(*shape) for shape in outs], in_spec...  18 us
    all_to_all x1, waiting for transfers between devices, exchange(): return lax.all_to_all(slots, EVERY, 0, 0, axis_index_groups=groups)  17.8 us
    all_to_all x4, waiting for transfers between devices, share_row(): return lax.all_to_all(row, EVERY, 0, 0, tiled=True)  15.7 us
    ppermute x12, waiting for transfers between devices, swap_y(): return lax.ppermute(value, EVERY, pairs)  15.2 us
  transfers between devices with their start and end apart: 31, of which 12 were waited for; matrix products, arithmetic and copies ran while one was open for 0% of the time, Pallas kernels for 2%

profile of v5, /device:TPU:1, one launch (start us, length us, event | category | flops | bytes accessed | tf_op | source)
XLA Modules:
  0.0 226.3 jit_solution(5969346625541256813)
XLA Ops:
  2.9 2.7 %shard_map.138.send = f32[32,9,8,128]{3,2,1,0:T(8,128)} custom-call(f32[4]{0:T(128)} %caps_at.1, f32[4]{0:T(128)} %limits_at.1, f32[8]{0:T(128)} %density_at.1, s32[1,128]{1,0:T(1,128)} %slope_at.3, s32[64,128]{1,0:T(8,128)} %bitcast.48, f32[64,128]{1,0:T(8,128)} %bitcast.49, f32[4,64,128]{2,1,0:T(8,128)} %bitcast.46, f32[5,4,64,128]{3,2,1,0:T(8,128)} %bitcast.45, ...), custom_call_target="tpu_custom_call" | custom-call | flops 1000000 | bytes 4000000 | tf_op jit(solution)/shard_map/pallas_call | solution.py:651
  8.0 13.1 %all-to-all-start = ((f32[32,9,8,128]{3,2,1,0:T(8,128)}), f32[32,9,8,128]{3,2,1,0:T(8,128)S(1)}, u32[]{:S(2)}, u32[]{:S(2)}) async-start(f32[32,9,8,128]{3,2,1,0:T(8,128)} %shard_map.139), calls=%async_computation | async-start | bytes 2359296 | tf_op jit(solution)/shard_map/all_to_all | solution.py:699
  21.8 17.8 %all-to-all-done.got = f32[32,9,8,128]{3,2,1,0:T(8,128)S(1)} async-done(((f32[32,9,8,128]{3,2,1,0:T(8,128)}), f32[32,9,8,128]{3,2,1,0:T(8,128)S(1)}, u32[]{:S(2)}, u32[]{:S(2)}) %all-to-all-start) | async-done | bytes 1179680 | tf_op jit(solution)/shard_map/all_to_all | solution.py:699
  41.1 12.4 %all-to-all-start.1 = ((f32[256,1,128]{2,1,0:T(1,128)}), f32[256,1,128]{2,1,0:T(1,128)S(1)}, u32[]{:S(2)}, u32[]{:S(2)}) async-start(f32[256,1,128]{2,1,0:T(1,128)} %bitcast.7), calls=%async_computation.1 | async-start | bytes 262144 | tf_op jit(solution)/shard_map/all_to_all | solution.py:688
  56.5 3.0 %collective-permute-start.4 = (f32[8,8,128]{2,1,0:T(8,128)S(1)}, f32[8,8,128]{2,1,0:T(8,128)S(1)}, u32[]{:S(2)}, u32[]{:S(2)}) collective-permute-start(f32[8,8,128]{2,1,0:T(8,128)S(1)} %get-tuple-element.67), channel_id=1, source_target_pairs={{1,4},{33,36},{65,68},{97,100},{129,132},{161,164},{193,196},{225,... | collective-permute-start | bytes 98312 | tf_op jit(solution)/shard_map/ppermute | solution.py:720
  59.5 2.5 %collective-permute-done.4.y_two = f32[8,8,128]{2,1,0:T(8,128)S(1)} collective-permute-done((f32[8,8,128]{2,1,0:T(8,128)S(1)}, f32[8,8,128]{2,1,0:T(8,128)S(1)}, u32[]{:S(2)}, u32[]{:S(2)}) %collective-permute-start.4) | collective-permute-done | bytes 32800 | tf_op jit(solution)/shard_map/ppermute | solution.py:720
  62.1 4.7 %all-to-all-done.1 = f32[256,1,128]{2,1,0:T(1,128)S(1)} async-done(((f32[256,1,128]{2,1,0:T(1,128)}), f32[256,1,128]{2,1,0:T(1,128)S(1)}, u32[]{:S(2)}, u32[]{:S(2)}) %all-to-all-start.1) | async-done | bytes 131104 | tf_op jit(solution)/shard_map/all_to_all | solution.py:688
  70.6 9.3 %all-to-all-start.2 = ((f32[256,1,128]{2,1,0:T(1,128)}), f32[256,1,128]{2,1,0:T(1,128)S(1)}, u32[]{:S(2)}, u32[]{:S(2)}) async-start(f32[256,1,128]{2,1,0:T(1,128)} %bitcast.10), calls=%async_computation.2 | async-start | bytes 262144 | tf_op jit(solution)/shard_map/all_to_all | solution.py:688
  82.9 3.0 %collective-permute-start.8 = (f32[8,8,128]{2,1,0:T(8,128)S(1)}, f32[8,8,128]{2,1,0:T(8,128)S(1)}, u32[]{:S(2)}, u32[]{:S(2)}) collective-permute-start(f32[8,8,128]{2,1,0:T(8,128)S(1)} %get-tuple-element.75), channel_id=1, source_target_pairs={{1,4},{33,36},{65,68},{97,100},{129,132},{161,164},{193,196},{225,... | collective-permute-start | bytes 98312 | tf_op jit(solution)/shard_map/ppermute | solution.py:720
  88.5 4.5 %all-to-all-done.2 = f32[256,1,128]{2,1,0:T(1,128)S(1)} async-done(((f32[256,1,128]{2,1,0:T(1,128)}), f32[256,1,128]{2,1,0:T(1,128)S(1)}, u32[]{:S(2)}, u32[]{:S(2)}) %all-to-all-start.2) | async-done | bytes 131104 | tf_op jit(solution)/shard_map/all_to_all | solution.py:688
  98.3 2.9 %collective-permute-done.12.y_two = f32[8,8,128]{2,1,0:T(8,128)S(1)} collective-permute-done((f32[8,8,128]{2,1,0:T(8,128)S(1)}, f32[8,8,128]{2,1,0:T(8,128)S(1)}, u32[]{:S(2)}, u32[]{:S(2)}) %collective-permute-start.12) | collective-permute-done | bytes 32800 | tf_op jit(solution)/shard_map/ppermute | solution.py:720
  102.0 25.3 %all_to_all.76 = f32[256,1,128]{2,1,0:T(1,128)S(1)} all-to-all(f32[256,1,128]{2,1,0:T(1,128)S(1)} %bitcast.42), channel_id=1, replica_groups=mesh['strip'=16,'period'=16] {'strip','period'}, dimensions={0} | all-to-all | bytes 262144 | tf_op jit(solution)/shard_map/all_to_all | solution.py:688
  128.8 5.4 %all-to-all-start.4 = ((f32[256,1,128]{2,1,0:T(1,128)}), f32[256,1,128]{2,1,0:T(1,128)S(1)}, u32[]{:S(2)}, u32[]{:S(2)}) async-start(f32[256,1,128]{2,1,0:T(1,128)} %bitcast.16), calls=%async_computation.4 | async-start | bytes 262144 | tf_op jit(solution)/shard_map/all_to_all | solution.py:688
  137.4 3.0 %collective-permute-start.16 = (f32[8,8,128]{2,1,0:T(8,128)S(1)}, f32[8,8,128]{2,1,0:T(8,128)S(1)}, u32[]{:S(2)}, u32[]{:S(2)}) collective-permute-start(f32[8,8,128]{2,1,0:T(8,128)S(1)} %get-tuple-element.93), channel_id=1, source_target_pairs={{1,4},{33,36},{65,68},{97,100},{129,132},{161,164},{193,196},{225,... | collective-permute-start | bytes 98312 | tf_op jit(solution)/shard_map/ppermute | solution.py:720
  140.4 2.5 %collective-permute-done.16.y_two = f32[8,8,128]{2,1,0:T(8,128)S(1)} collective-permute-done((f32[8,8,128]{2,1,0:T(8,128)S(1)}, f32[8,8,128]{2,1,0:T(8,128)S(1)}, u32[]{:S(2)}, u32[]{:S(2)}) %collective-permute-start.16) | collective-permute-done | bytes 32800 | tf_op jit(solution)/shard_map/ppermute | solution.py:720
  144.2 3.4 %all-to-all-done.4 = f32[256,1,128]{2,1,0:T(1,128)S(1)} async-done(((f32[256,1,128]{2,1,0:T(1,128)}), f32[256,1,128]{2,1,0:T(1,128)S(1)}, u32[]{:S(2)}, u32[]{:S(2)}) %all-to-all-start.4) | async-done | bytes 131104 | tf_op jit(solution)/shard_map/all_to_all | solution.py:688
  153.3 10.5 %all-to-all-start.5 = ((f32[256,1,128]{2,1,0:T(1,128)}), f32[256,1,128]{2,1,0:T(1,128)S(1)}, u32[]{:S(2)}, u32[]{:S(2)}) async-start(f32[256,1,128]{2,1,0:T(1,128)} %bitcast.41), calls=%async_computation.5 | async-start | bytes 262144 | tf_op jit(solution)/shard_map/all_to_all | solution.py:688
  166.8 3.0 %collective-permute-start.20 = (f32[8,8,128]{2,1,0:T(8,128)}, f32[8,8,128]{2,1,0:T(8,128)S(1)}, u32[]{:S(2)}, u32[]{:S(2)}) collective-permute-start(f32[8,8,128]{2,1,0:T(8,128)} %copy-done.14), channel_id=1, source_target_pairs={{1,4},{33,36},{65,68},{97,100},{129,132},{161,164},{193,196},{225,... | collective-permute-start | bytes 98312 | tf_op jit(solution)/shard_map/ppermute | solution.py:720
  169.9 2.8 %collective-permute-done.20.y_two = f32[8,8,128]{2,1,0:T(8,128)S(1)} collective-permute-done((f32[8,8,128]{2,1,0:T(8,128)}, f32[8,8,128]{2,1,0:T(8,128)S(1)}, u32[]{:S(2)}, u32[]{:S(2)}) %collective-permute-start.20) | collective-permute-done | bytes 32800 | tf_op jit(solution)/shard_map/ppermute | solution.py:720
  173.9 3.1 %all-to-all-done.5 = f32[256,1,128]{2,1,0:T(1,128)S(1)} async-done(((f32[256,1,128]{2,1,0:T(1,128)}), f32[256,1,128]{2,1,0:T(1,128)S(1)}, u32[]{:S(2)}, u32[]{:S(2)}) %all-to-all-start.5) | async-done | bytes 131104 | tf_op jit(solution)/shard_map/all_to_all | solution.py:688
  181.6 3.2 %collective-permute-start.24 = (f32[8,8,128]{2,1,0:T(8,128)S(1)}, f32[8,8,128]{2,1,0:T(8,128)S(1)}, u32[]{:S(2)}, u32[]{:S(2)}) collective-permute-start(f32[8,8,128]{2,1,0:T(8,128)S(1)} %get-tuple-element.108), channel_id=1, source_target_pairs={{1,4},{33,36},{65,68},{97,100},{129,132},{161,164},{193,196},{225,... | collective-permute-start | bytes 98312 | tf_op jit(solution)/shard_map/ppermute | solution.py:720
  187.7 22.6 %all_to_all.77.got = f32[32,7,8,128]{3,2,1,0:T(8,128)S(1)} all-to-all(f32[32,7,8,128]{3,2,1,0:T(8,128)S(1)} %shard_map.147), channel_id=1, replica_groups={{0,1,2,3,4,5,6,7,8,9,10,11,12,13,14,15,16,17,18,19,20,21,22,23,24,25,26..., dimensions={0} | all-to-all | bytes 1835008 | tf_op jit(solution)/shard_map/all_to_all | solution.py:699
  211.1 7.6 %all-to-all-start.7 = ((f32[8,1,128]{2,1,0:T(1,128)}), f32[8,1,128]{2,1,0:T(1,128)S(1)}, u32[]{:S(2)}, u32[]{:S(2)}) async-start(f32[8,1,128]{2,1,0:T(1,128)} %bitcast.26), calls=%async_computation.7 | async-start | bytes 8192 | tf_op jit(solution)/shard_map/all_to_all | solution.py:694
  219.9 5.4 %all-to-all-done.7 = f32[8,1,128]{2,1,0:T(1,128)S(1)} async-done(((f32[8,1,128]{2,1,0:T(1,128)}), f32[8,1,128]{2,1,0:T(1,128)S(1)}, u32[]{:S(2)}, u32[]{:S(2)}) %all-to-all-start.7) | async-done | bytes 4128 | tf_op jit(solution)/shard_map/all_to_all | solution.py:694
  (90 shorter events, 50.5 us)
Async XLA Ops:
  8.0 31.6 %all-to-all-start = ((f32[32,9,8,128]{3,2,1,0:T(8,128)}), f32[32,9,8,128]{3,2,1,0:T(8,128)S(1)}, u32[]{:S(2)}, u32[]{:S(2)}) async-start(f32[32,9,8,128]{3,2,1,0:T(8,128)} %shard_map.139), calls=%async_computation | async-start | bytes 2359296 | tf_op jit(solution)/shard_map/all_to_all | solution.py:699
  41.1 25.7 %all-to-all-start.1 = ((f32[256,1,128]{2,1,0:T(1,128)}), f32[256,1,128]{2,1,0:T(1,128)S(1)}, u32[]{:S(2)}, u32[]{:S(2)}) async-start(f32[256,1,128]{2,1,0:T(1,128)} %bitcast.7), calls=%async_computation.1 | async-start | bytes 262144 | tf_op jit(solution)/shard_map/all_to_all | solution.py:688
  53.5 8.6 %collective-permute-start.1 = (f32[16,8,128]{2,1,0:T(8,128)S(1)}, f32[16,8,128]{2,1,0:T(8,128)S(1)}, u32[]{:S(2)}, u32[]{:S(2)}) collective-permute-start(f32[16,8,128]{2,1,0:T(8,128)S(1)} %get-tuple-element.64), channel_id=1, source_target_pairs={{0,32},{1,33},{2,34},{3,35},{4,36},{5,37},{6,38},{7,39},{8,40},{9,... | collective-permute-start | bytes 196616 | tf_op jit(solution)/shard_map/ppermute | solution.py:709
  55.1 7.0 %collective-permute-start.2 = (f32[16,8,128]{2,1,0:T(8,128)S(1)}, f32[16,8,128]{2,1,0:T(8,128)S(1)}, u32[]{:S(2)}, u32[]{:S(2)}) collective-permute-start(f32[16,8,128]{2,1,0:T(8,128)S(1)} %get-tuple-element.65), channel_id=1, source_target_pairs={{32,64},{33,65},{34,66},{35,67},{36,68},{37,69},{38,70},{39,71},{4... | collective-permute-start | bytes 196616 | tf_op jit(solution)/shard_map/ppermute | solution.py:709
  56.5 5.6 %collective-permute-start.4 = (f32[8,8,128]{2,1,0:T(8,128)S(1)}, f32[8,8,128]{2,1,0:T(8,128)S(1)}, u32[]{:S(2)}, u32[]{:S(2)}) collective-permute-start(f32[8,8,128]{2,1,0:T(8,128)S(1)} %get-tuple-element.67), channel_id=1, source_target_pairs={{1,4},{33,36},{65,68},{97,100},{129,132},{161,164},{193,196},{225,... | collective-permute-start | bytes 98312 | tf_op jit(solution)/shard_map/ppermute | solution.py:720
  70.6 22.4 %all-to-all-start.2 = ((f32[256,1,128]{2,1,0:T(1,128)}), f32[256,1,128]{2,1,0:T(1,128)S(1)}, u32[]{:S(2)}, u32[]{:S(2)}) async-start(f32[256,1,128]{2,1,0:T(1,128)} %bitcast.10), calls=%async_computation.2 | async-start | bytes 262144 | tf_op jit(solution)/shard_map/all_to_all | solution.py:688
  79.9 8.6 %collective-permute-start.5 = (f32[16,8,128]{2,1,0:T(8,128)}, f32[16,8,128]{2,1,0:T(8,128)S(1)}, u32[]{:S(2)}, u32[]{:S(2)}) collective-permute-start(f32[16,8,128]{2,1,0:T(8,128)} %copy-done.12), channel_id=1, source_target_pairs={{0,32},{1,33},{2,34},{3,35},{4,36},{5,37},{6,38},{7,39},{8,40},{9,... | collective-permute-start | bytes 196616 | tf_op jit(solution)/shard_map/ppermute | solution.py:709
  81.5 7.0 %collective-permute-start.6 = (f32[16,8,128]{2,1,0:T(8,128)S(1)}, f32[16,8,128]{2,1,0:T(8,128)S(1)}, u32[]{:S(2)}, u32[]{:S(2)}) collective-permute-start(f32[16,8,128]{2,1,0:T(8,128)S(1)} %get-tuple-element.73), channel_id=1, source_target_pairs={{32,64},{33,65},{34,66},{35,67},{36,68},{37,69},{38,70},{39,71},{4... | collective-permute-start | bytes 196616 | tf_op jit(solution)/shard_map/ppermute | solution.py:709
  82.9 5.6 %collective-permute-start.8 = (f32[8,8,128]{2,1,0:T(8,128)S(1)}, f32[8,8,128]{2,1,0:T(8,128)S(1)}, u32[]{:S(2)}, u32[]{:S(2)}) collective-permute-start(f32[8,8,128]{2,1,0:T(8,128)S(1)} %get-tuple-element.75), channel_id=1, source_target_pairs={{1,4},{33,36},{65,68},{97,100},{129,132},{161,164},{193,196},{225,... | collective-permute-start | bytes 98312 | tf_op jit(solution)/shard_map/ppermute | solution.py:720
  94.0 7.2 %collective-permute-start.9 = (f32[16,8,128]{2,1,0:T(8,128)S(1)}, f32[16,8,128]{2,1,0:T(8,128)S(1)}, u32[]{:S(2)}, u32[]{:S(2)}) collective-permute-start(f32[16,8,128]{2,1,0:T(8,128)S(1)} %get-tuple-element.79), channel_id=1, source_target_pairs={{0,32},{1,33},{2,34},{3,35},{4,36},{5,37},{6,38},{7,39},{8,40},{9,... | collective-permute-start | bytes 196616 | tf_op jit(solution)/shard_map/ppermute | solution.py:709
  94.9 6.3 %collective-permute-start.10 = (f32[16,8,128]{2,1,0:T(8,128)S(1)}, f32[16,8,128]{2,1,0:T(8,128)S(1)}, u32[]{:S(2)}, u32[]{:S(2)}) collective-permute-start(f32[16,8,128]{2,1,0:T(8,128)S(1)} %get-tuple-element.80), channel_id=1, source_target_pairs={{32,64},{33,65},{34,66},{35,67},{36,68},{37,69},{38,70},{39,71},{4... | collective-permute-start | bytes 196616 | tf_op jit(solution)/shard_map/ppermute | solution.py:709
  96.0 5.2 %collective-permute-start.12 = (f32[8,8,128]{2,1,0:T(8,128)S(1)}, f32[8,8,128]{2,1,0:T(8,128)S(1)}, u32[]{:S(2)}, u32[]{:S(2)}) collective-permute-start(f32[8,8,128]{2,1,0:T(8,128)S(1)} %get-tuple-element.82), channel_id=1, source_target_pairs={{1,4},{33,36},{65,68},{97,100},{129,132},{161,164},{193,196},{225,... | collective-permute-start | bytes 98312 | tf_op jit(solution)/shard_map/ppermute | solution.py:720
  128.8 18.9 %all-to-all-start.4 = ((f32[256,1,128]{2,1,0:T(1,128)}), f32[256,1,128]{2,1,0:T(1,128)S(1)}, u32[]{:S(2)}, u32[]{:S(2)}) async-start(f32[256,1,128]{2,1,0:T(1,128)} %bitcast.16), calls=%async_computation.4 | async-start | bytes 262144 | tf_op jit(solution)/shard_map/all_to_all | solution.py:688
  134.2 9.4 %collective-permute-start.13 = (f32[16,8,128]{2,1,0:T(8,128)S(1)}, f32[16,8,128]{2,1,0:T(8,128)S(1)}, u32[]{:S(2)}, u32[]{:S(2)}) collective-permute-start(f32[16,8,128]{2,1,0:T(8,128)S(1)} %get-tuple-element.90), channel_id=1, source_target_pairs={{0,32},{1,33},{2,34},{3,35},{4,36},{5,37},{6,38},{7,39},{8,40},{9,... | collective-permute-start | bytes 196616 | tf_op jit(solution)/shard_map/ppermute | solution.py:709
  135.9 7.6 %collective-permute-start.14 = (f32[16,8,128]{2,1,0:T(8,128)S(1)}, f32[16,8,128]{2,1,0:T(8,128)S(1)}, u32[]{:S(2)}, u32[]{:S(2)}) collective-permute-start(f32[16,8,128]{2,1,0:T(8,128)S(1)} %get-tuple-element.91), channel_id=1, source_target_pairs={{32,64},{33,65},{34,66},{35,67},{36,68},{37,69},{38,70},{39,71},{4... | collective-permute-start | bytes 196616 | tf_op jit(solution)/shard_map/ppermute | solution.py:709
  137.4 5.6 %collective-permute-start.16 = (f32[8,8,128]{2,1,0:T(8,128)S(1)}, f32[8,8,128]{2,1,0:T(8,128)S(1)}, u32[]{:S(2)}, u32[]{:S(2)}) collective-permute-start(f32[8,8,128]{2,1,0:T(8,128)S(1)} %get-tuple-element.93), channel_id=1, source_target_pairs={{1,4},{33,36},{65,68},{97,100},{129,132},{161,164},{193,196},{225,... | collective-permute-start | bytes 98312 | tf_op jit(solution)/shard_map/ppermute | solution.py:720
  153.3 23.6 %all-to-all-start.5 = ((f32[256,1,128]{2,1,0:T(1,128)}), f32[256,1,128]{2,1,0:T(1,128)S(1)}, u32[]{:S(2)}, u32[]{:S(2)}) async-start(f32[256,1,128]{2,1,0:T(1,128)} %bitcast.41), calls=%async_computation.5 | async-start | bytes 262144 | tf_op jit(solution)/shard_map/all_to_all | solution.py:688
  163.8 9.4 %collective-permute-start.17 = (f32[16,8,128]{2,1,0:T(8,128)}, f32[16,8,128]{2,1,0:T(8,128)S(1)}, u32[]{:S(2)}, u32[]{:S(2)}) collective-permute-start(f32[16,8,128]{2,1,0:T(8,128)} %copy-done.13), channel_id=1, source_target_pairs={{0,32},{1,33},{2,34},{3,35},{4,36},{5,37},{6,38},{7,39},{8,40},{9,... | collective-permute-start | bytes 196616 | tf_op jit(solution)/shard_map/ppermute | solution.py:709
  165.4 7.8 %collective-permute-start.18 = (f32[16,8,128]{2,1,0:T(8,128)}, f32[16,8,128]{2,1,0:T(8,128)S(1)}, u32[]{:S(2)}, u32[]{:S(2)}) collective-permute-start(f32[16,8,128]{2,1,0:T(8,128)} %copy-done.11), channel_id=1, source_target_pairs={{32,64},{33,65},{34,66},{35,67},{36,68},{37,69},{38,70},{39,71},{4... | collective-permute-start | bytes 196616 | tf_op jit(solution)/shard_map/ppermute | solution.py:709
  166.8 5.8 %collective-permute-start.20 = (f32[8,8,128]{2,1,0:T(8,128)}, f32[8,8,128]{2,1,0:T(8,128)S(1)}, u32[]{:S(2)}, u32[]{:S(2)}) collective-permute-start(f32[8,8,128]{2,1,0:T(8,128)} %copy-done.14), channel_id=1, source_target_pairs={{1,4},{33,36},{65,68},{97,100},{129,132},{161,164},{193,196},{225,... | collective-permute-start | bytes 98312 | tf_op jit(solution)/shard_map/ppermute | solution.py:720
  179.5 7.3 %collective-permute-start.21 = (f32[16,8,128]{2,1,0:T(8,128)S(1)}, f32[16,8,128]{2,1,0:T(8,128)S(1)}, u32[]{:S(2)}, u32[]{:S(2)}) collective-permute-start(f32[16,8,128]{2,1,0:T(8,128)S(1)} %get-tuple-element.105), channel_id=1, source_target_pairs={{0,32},{1,33},{2,34},{3,35},{4,36},{5,37},{6,38},{7,39},{8,40},{9,... | collective-permute-start | bytes 196616 | tf_op jit(solution)/shard_map/ppermute | solution.py:709
  180.9 6.0 %collective-permute-start.22 = (f32[16,8,128]{2,1,0:T(8,128)S(1)}, f32[16,8,128]{2,1,0:T(8,128)S(1)}, u32[]{:S(2)}, u32[]{:S(2)}) collective-permute-start(f32[16,8,128]{2,1,0:T(8,128)S(1)} %get-tuple-element.106), channel_id=1, source_target_pairs={{32,64},{33,65},{34,66},{35,67},{36,68},{37,69},{38,70},{39,71},{4... | collective-permute-start | bytes 196616 | tf_op jit(solution)/shard_map/ppermute | solution.py:709
  181.6 5.2 %collective-permute-start.24 = (f32[8,8,128]{2,1,0:T(8,128)S(1)}, f32[8,8,128]{2,1,0:T(8,128)S(1)}, u32[]{:S(2)}, u32[]{:S(2)}) collective-permute-start(f32[8,8,128]{2,1,0:T(8,128)S(1)} %get-tuple-element.108), channel_id=1, source_target_pairs={{1,4},{33,36},{65,68},{97,100},{129,132},{161,164},{193,196},{225,... | collective-permute-start | bytes 98312 | tf_op jit(solution)/shard_map/ppermute | solution.py:720
  211.1 14.1 %all-to-all-start.7 = ((f32[8,1,128]{2,1,0:T(1,128)}), f32[8,1,128]{2,1,0:T(1,128)S(1)}, u32[]{:S(2)}, u32[]{:S(2)}) async-start(f32[8,1,128]{2,1,0:T(1,128)} %bitcast.26), calls=%async_computation.7 | async-start | bytes 8192 | tf_op jit(solution)/shard_map/all_to_all | solution.py:694
  (25 other events, 62.0 us)

commit v6 on v5

--- a/solution.py
+++ b/solution.py
@@ -777,9 +777,9 @@
     )(got, jnp.reshape(omega_start, (1, 1)))
     for outer in range(OUTER):
         if outer > 0:
-            primal, *sides, row = call(primal_restart_kernel, STEP_OUTS, STEP_SCRATCH)(
-                row_sums, primal, tail, const
-            )
+            primal, *sides, row = call(
+                primal_restart_kernel, STEP_OUTS, STEP_SCRATCH, aliases={0: 5, 1: 0}
+            )(row_sums, primal, tail, const)
         duals, inwards = [dual], [inward]
         for inner in range(1, INNER):
             row_sums = share_row(row)
@@ -787,13 +787,17 @@
                 functools.partial(step_kernel, inner),
                 [DUAL_ARRAY, INWARD_ARRAY] + STEP_OUTS,
                 STEP_SCRATCH + DUAL_SCRATCH + [TAIL_ARRAY],
+                aliases={0: 7, 1: 2, 3: 3, 4: 4, 5: 5, 6: 6} | ({8: 1} if inner == 1 else {}),
             )(row_sums, primal, const, *halo(*sides), dual, inward)
             duals.append(dual)
             inwards.append(inward)
         sides = halo(*sides)
         if outer < OUTER - 1:
             dual, inward, tail, row = call(
-                dual_restart_kernel, DUAL_OUTS + [(DEVICES, 128)], DUAL_SCRATCH
+                dual_restart_kernel,
+                DUAL_OUTS + [(DEVICES, 128)],
+                DUAL_SCRATCH,
+                aliases={8: 3, 9: 1, 11: 0},
             )(primal, const, *sides, dual, inward, row, inwards[1], duals[0], duals[1])
             row_sums = share_row(row)
         else:

time: 227 us -> 225 us (level)
  local copies, waits for them, and re-layouts: 11.6 us -> 3.81 us
  Pallas kernels: 18 us -> 21.3 us
  waiting for transfers between devices: 54.2 us -> 56.9 us
    unnamed x36 -> x10, local copies, waits for them, and re-layouts: 11.6 us -> 3.81 us
    pallas_call x14, Pallas kernels: 18 us -> 21.3 us  [run(): pl.pallas_call(kernel, out_shape=[f32(*shape) for shape in outs], in_spec...]
where the time goes in v6:
time: 225 us; the launch traced here: 224 us
  starting transfers between devices  93.3 us (41%)
  waiting for transfers between devices  56.9 us (25%)
  blocking collectives  47 us (21%)
  Pallas kernels  21.3 us (9%)
  local copies, waits for them, and re-layouts  3.81 us (2%)
    all_to_all x4, starting transfers between devices, share_row(): return lax.all_to_all(row, EVERY, 0, 0, tiled=True)  39.6 us
    all_to_all x1, blocking collectives, share_row(): return lax.all_to_all(row, EVERY, 0, 0, tiled=True)  25.8 us
    pallas_call x14, Pallas kernels, run(): pl.pallas_call(kernel, out_shape=[f32(*shape) for shape in outs], in_spec...  21.3 us
    all_to_all x1, blocking collectives, exchange(): return lax.all_to_all(slots, EVERY, 0, 0, axis_index_groups=groups)  21.2 us
    ppermute x12, starting transfers between devices, swap_y(): return lax.ppermute(value, EVERY, pairs)  20.4 us
    all_to_all x1, waiting for transfers between devices, exchange(): return lax.all_to_all(slots, EVERY, 0, 0, axis_index_groups=groups)  17.8 us
    all_to_all x4, waiting for transfers between devices, share_row(): return lax.all_to_all(row, EVERY, 0, 0, tiled=True)  17.5 us
    ppermute x12, waiting for transfers between devices, swap_y(): return lax.ppermute(value, EVERY, pairs)  16.1 us
  transfers between devices with their start and end apart: 31, of which 12 were waited for; matrix products, arithmetic and copies ran while one was open for 0% of the time, Pallas kernels for 2%

profile of v6, /device:TPU:1, one launch (start us, length us, event | category | flops | bytes accessed | tf_op | source)
XLA Modules:
  0.0 224.1 jit_solution(71078927383458585)
XLA Ops:
  2.9 2.7 %shard_map.138.send = f32[32,9,8,128]{3,2,1,0:T(8,128)} custom-call(f32[4]{0:T(128)} %caps_at.1, f32[4]{0:T(128)} %limits_at.1, f32[8]{0:T(128)} %density_at.1, s32[1,128]{1,0:T(1,128)} %slope_at.3, s32[64,128]{1,0:T(8,128)} %bitcast.44, f32[64,128]{1,0:T(8,128)} %bitcast.45, f32[4,64,128]{2,1,0:T(8,128)} %bitcast.42, f32[5,4,64,128]{3,2,1,0:T(8,128)} %bitcast.41, ...), custom_call_target="tpu_custom_call" | custom-call | flops 1000000 | bytes 4000000 | tf_op jit(solution)/shard_map/pallas_call | solution.py:651
  8.0 13.1 %all-to-all-start = ((f32[32,9,8,128]{3,2,1,0:T(8,128)}), f32[32,9,8,128]{3,2,1,0:T(8,128)S(1)}, u32[]{:S(2)}, u32[]{:S(2)}) async-start(f32[32,9,8,128]{3,2,1,0:T(8,128)} %shard_map.139), calls=%async_computation | async-start | bytes 2359296 | tf_op jit(solution)/shard_map/all_to_all | solution.py:699
  21.8 17.8 %all-to-all-done.got = f32[32,9,8,128]{3,2,1,0:T(8,128)S(1)} async-done(((f32[32,9,8,128]{3,2,1,0:T(8,128)}), f32[32,9,8,128]{3,2,1,0:T(8,128)S(1)}, u32[]{:S(2)}, u32[]{:S(2)}) %all-to-all-start) | async-done | bytes 1179680 | tf_op jit(solution)/shard_map/all_to_all | solution.py:699
  41.9 13.4 %all-to-all-start.1 = ((f32[256,1,128]{2,1,0:T(1,128)}), f32[256,1,128]{2,1,0:T(1,128)}, u32[]{:S(2)}, u32[]{:S(2)}) async-start(f32[256,1,128]{2,1,0:T(1,128)} %bitcast.7), calls=%async_computation.1 | async-start | bytes 262144 | tf_op jit(solution)/shard_map/all_to_all | solution.py:688
  58.4 3.0 %collective-permute-start.4 = (f32[8,8,128]{2,1,0:T(8,128)S(1)}, f32[8,8,128]{2,1,0:T(8,128)S(1)}, u32[]{:S(2)}, u32[]{:S(2)}) collective-permute-start(f32[8,8,128]{2,1,0:T(8,128)S(1)} %get-tuple-element.67), channel_id=1, source_target_pairs={{1,4},{33,36},{65,68},{97,100},{129,132},{161,164},{193,196},{225,... | collective-permute-start | bytes 98312 | tf_op jit(solution)/shard_map/ppermute | solution.py:720
  61.4 2.7 %collective-permute-done.4.y_two = f32[8,8,128]{2,1,0:T(8,128)S(1)} collective-permute-done((f32[8,8,128]{2,1,0:T(8,128)S(1)}, f32[8,8,128]{2,1,0:T(8,128)S(1)}, u32[]{:S(2)}, u32[]{:S(2)}) %collective-permute-start.4) | collective-permute-done | bytes 32800 | tf_op jit(solution)/shard_map/ppermute | solution.py:720
  64.1 4.0 %all-to-all-done.1 = f32[256,1,128]{2,1,0:T(1,128)} async-done(((f32[256,1,128]{2,1,0:T(1,128)}), f32[256,1,128]{2,1,0:T(1,128)}, u32[]{:S(2)}, u32[]{:S(2)}) %all-to-all-start.1) | async-done | bytes 131104 | tf_op jit(solution)/shard_map/all_to_all | solution.py:688
  71.8 9.7 %all-to-all-start.2 = ((f32[256,1,128]{2,1,0:T(1,128)}), f32[256,1,128]{2,1,0:T(1,128)S(1)}, u32[]{:S(2)}, u32[]{:S(2)}) async-start(f32[256,1,128]{2,1,0:T(1,128)} %bitcast.10), calls=%async_computation.2 | async-start | bytes 262144 | tf_op jit(solution)/shard_map/all_to_all | solution.py:688
  84.6 3.0 %collective-permute-start.8 = (f32[8,8,128]{2,1,0:T(8,128)S(1)}, f32[8,8,128]{2,1,0:T(8,128)S(1)}, u32[]{:S(2)}, u32[]{:S(2)}) collective-permute-start(f32[8,8,128]{2,1,0:T(8,128)S(1)} %get-tuple-element.75), channel_id=1, source_target_pairs={{1,4},{33,36},{65,68},{97,100},{129,132},{161,164},{193,196},{225,... | collective-permute-start | bytes 98312 | tf_op jit(solution)/shard_map/ppermute | solution.py:720
  90.2 4.7 %all-to-all-done.2 = f32[256,1,128]{2,1,0:T(1,128)S(1)} async-done(((f32[256,1,128]{2,1,0:T(1,128)}), f32[256,1,128]{2,1,0:T(1,128)S(1)}, u32[]{:S(2)}, u32[]{:S(2)}) %all-to-all-start.2) | async-done | bytes 131104 | tf_op jit(solution)/shard_map/all_to_all | solution.py:688
  100.2 2.8 %collective-permute-done.12.y_two = f32[8,8,128]{2,1,0:T(8,128)S(1)} collective-permute-done((f32[8,8,128]{2,1,0:T(8,128)S(1)}, f32[8,8,128]{2,1,0:T(8,128)S(1)}, u32[]{:S(2)}, u32[]{:S(2)}) %collective-permute-start.12) | collective-permute-done | bytes 32800 | tf_op jit(solution)/shard_map/ppermute | solution.py:720
  103.8 25.8 %all_to_all.76 = f32[256,1,128]{2,1,0:T(1,128)} all-to-all(f32[256,1,128]{2,1,0:T(1,128)S(1)} %bitcast.37), channel_id=1, replica_groups=mesh['strip'=16,'period'=16] {'strip','period'}, dimensions={0} | all-to-all | bytes 262144 | tf_op jit(solution)/shard_map/all_to_all | solution.py:688
  132.0 6.7 %all-to-all-start.4 = ((f32[256,1,128]{2,1,0:T(1,128)}), f32[256,1,128]{2,1,0:T(1,128)}, u32[]{:S(2)}, u32[]{:S(2)}) async-start(f32[256,1,128]{2,1,0:T(1,128)} %bitcast.16), calls=%async_computation.4 | async-start | bytes 262144 | tf_op jit(solution)/shard_map/all_to_all | solution.py:688
  141.5 3.0 %collective-permute-start.16 = (f32[8,8,128]{2,1,0:T(8,128)S(1)}, f32[8,8,128]{2,1,0:T(8,128)S(1)}, u32[]{:S(2)}, u32[]{:S(2)}) collective-permute-start(f32[8,8,128]{2,1,0:T(8,128)S(1)} %get-tuple-element.93), channel_id=1, source_target_pairs={{1,4},{33,36},{65,68},{97,100},{129,132},{161,164},{193,196},{225,... | collective-permute-start | bytes 98312 | tf_op jit(solution)/shard_map/ppermute | solution.py:720
  144.5 2.7 %collective-permute-done.16.y_two = f32[8,8,128]{2,1,0:T(8,128)S(1)} collective-permute-done((f32[8,8,128]{2,1,0:T(8,128)S(1)}, f32[8,8,128]{2,1,0:T(8,128)S(1)}, u32[]{:S(2)}, u32[]{:S(2)}) %collective-permute-start.16) | collective-permute-done | bytes 32800 | tf_op jit(solution)/shard_map/ppermute | solution.py:720
  147.2 4.0 %all-to-all-done.4 = f32[256,1,128]{2,1,0:T(1,128)} async-done(((f32[256,1,128]{2,1,0:T(1,128)}), f32[256,1,128]{2,1,0:T(1,128)}, u32[]{:S(2)}, u32[]{:S(2)}) %all-to-all-start.4) | async-done | bytes 131104 | tf_op jit(solution)/shard_map/all_to_all | solution.py:688
  151.3 2.6 %shard_map.145 = (f32[192,8,128]{2,1,0:T(8,128)S(1)}, f32[48,8,128]{2,1,0:T(8,128)S(1)}, f32[157,8,128]{2,1,0:T(8,128)S(1)}, f32[16,8,128]{2,1,0:T(8,128)S(1)}, ...) custom-call(f32[256,128]{1,0:T(8,128)} %bitcast.17.got, ...), custom_call_target="tpu_custom_call", output_to_operand_aliasing={{7}: (0, {}), {2}: (1, {}), {3}: (3, {}), {4}: (4, {}), {5}... | custom-call | flops 1000000 | bytes 4000000 | tf_op jit(solution)/shard_map/pallas_call | solution.py:651
  153.9 9.7 %all-to-all-start.5 = ((f32[256,1,128]{2,1,0:T(1,128)}), f32[256,1,128]{2,1,0:T(1,128)S(1)}, u32[]{:S(2)}, u32[]{:S(2)}) async-start(f32[256,1,128]{2,1,0:T(1,128)} %bitcast.19), calls=%async_computation.5 | async-start | bytes 262144 | tf_op jit(solution)/shard_map/all_to_all | solution.py:688
  166.6 3.0 %collective-permute-start.20 = (f32[8,8,128]{2,1,0:T(8,128)S(1)}, f32[8,8,128]{2,1,0:T(8,128)S(1)}, u32[]{:S(2)}, u32[]{:S(2)}) collective-permute-start(f32[8,8,128]{2,1,0:T(8,128)S(1)} %get-tuple-element.101), channel_id=1, source_target_pairs={{1,4},{33,36},{65,68},{97,100},{129,132},{161,164},{193,196},{225,... | collective-permute-start | bytes 98312 | tf_op jit(solution)/shard_map/ppermute | solution.py:720
  172.2 4.7 %all-to-all-done.5 = f32[256,1,128]{2,1,0:T(1,128)S(1)} async-done(((f32[256,1,128]{2,1,0:T(1,128)}), f32[256,1,128]{2,1,0:T(1,128)S(1)}, u32[]{:S(2)}, u32[]{:S(2)}) %all-to-all-start.5) | async-done | bytes 131104 | tf_op jit(solution)/shard_map/all_to_all | solution.py:688
  182.2 2.8 %collective-permute-done.24.y_two = f32[8,8,128]{2,1,0:T(8,128)S(1)} collective-permute-done((f32[8,8,128]{2,1,0:T(8,128)S(1)}, f32[8,8,128]{2,1,0:T(8,128)S(1)}, u32[]{:S(2)}, u32[]{:S(2)}) %collective-permute-start.24) | collective-permute-done | bytes 32800 | tf_op jit(solution)/shard_map/ppermute | solution.py:720
  186.9 21.2 %all_to_all.77.got = f32[32,7,8,128]{3,2,1,0:T(8,128)S(1)} all-to-all(f32[32,7,8,128]{3,2,1,0:T(8,128)S(1)} %shard_map.147), channel_id=1, replica_groups={{0,1,2,3,4,5,6,7,8,9,10,11,12,13,14,15,16,17,18,19,20,21,22,23,24,25,26..., dimensions={0} | all-to-all | bytes 1835008 | tf_op jit(solution)/shard_map/all_to_all | solution.py:699
  208.9 7.6 %all-to-all-start.7 = ((f32[8,1,128]{2,1,0:T(1,128)}), f32[8,1,128]{2,1,0:T(1,128)S(1)}, u32[]{:S(2)}, u32[]{:S(2)}) async-start(f32[8,1,128]{2,1,0:T(1,128)} %bitcast.26), calls=%async_computation.7 | async-start | bytes 8192 | tf_op jit(solution)/shard_map/all_to_all | solution.py:694
  217.7 5.4 %all-to-all-done.7 = f32[8,1,128]{2,1,0:T(1,128)S(1)} async-done(((f32[8,1,128]{2,1,0:T(1,128)}), f32[8,1,128]{2,1,0:T(1,128)S(1)}, u32[]{:S(2)}, u32[]{:S(2)}) %all-to-all-start.7) | async-done | bytes 4128 | tf_op jit(solution)/shard_map/all_to_all | solution.py:694
  (64 shorter events, 45.9 us)
Async XLA Ops:
  8.0 31.6 %all-to-all-start = ((f32[32,9,8,128]{3,2,1,0:T(8,128)}), f32[32,9,8,128]{3,2,1,0:T(8,128)S(1)}, u32[]{:S(2)}, u32[]{:S(2)}) async-start(f32[32,9,8,128]{3,2,1,0:T(8,128)} %shard_map.139), calls=%async_computation | async-start | bytes 2359296 | tf_op jit(solution)/shard_map/all_to_all | solution.py:699
  41.9 26.2 %all-to-all-start.1 = ((f32[256,1,128]{2,1,0:T(1,128)}), f32[256,1,128]{2,1,0:T(1,128)}, u32[]{:S(2)}, u32[]{:S(2)}) async-start(f32[256,1,128]{2,1,0:T(1,128)} %bitcast.7), calls=%async_computation.1 | async-start | bytes 262144 | tf_op jit(solution)/shard_map/all_to_all | solution.py:688
  55.3 8.8 %collective-permute-start.1 = (f32[16,8,128]{2,1,0:T(8,128)S(1)}, f32[16,8,128]{2,1,0:T(8,128)S(1)}, u32[]{:S(2)}, u32[]{:S(2)}) collective-permute-start(f32[16,8,128]{2,1,0:T(8,128)S(1)} %get-tuple-element.64), channel_id=1, source_target_pairs={{0,32},{1,33},{2,34},{3,35},{4,36},{5,37},{6,38},{7,39},{8,40},{9,... | collective-permute-start | bytes 196616 | tf_op jit(solution)/shard_map/ppermute | solution.py:709
  56.9 7.2 %collective-permute-start.2 = (f32[16,8,128]{2,1,0:T(8,128)S(1)}, f32[16,8,128]{2,1,0:T(8,128)S(1)}, u32[]{:S(2)}, u32[]{:S(2)}) collective-permute-start(f32[16,8,128]{2,1,0:T(8,128)S(1)} %get-tuple-element.65), channel_id=1, source_target_pairs={{32,64},{33,65},{34,66},{35,67},{36,68},{37,69},{38,70},{39,71},{4... | collective-permute-start | bytes 196616 | tf_op jit(solution)/shard_map/ppermute | solution.py:709
  58.4 5.7 %collective-permute-start.4 = (f32[8,8,128]{2,1,0:T(8,128)S(1)}, f32[8,8,128]{2,1,0:T(8,128)S(1)}, u32[]{:S(2)}, u32[]{:S(2)}) collective-permute-start(f32[8,8,128]{2,1,0:T(8,128)S(1)} %get-tuple-element.67), channel_id=1, source_target_pairs={{1,4},{33,36},{65,68},{97,100},{129,132},{161,164},{193,196},{225,... | collective-permute-start | bytes 98312 | tf_op jit(solution)/shard_map/ppermute | solution.py:720
  71.8 23.1 %all-to-all-start.2 = ((f32[256,1,128]{2,1,0:T(1,128)}), f32[256,1,128]{2,1,0:T(1,128)S(1)}, u32[]{:S(2)}, u32[]{:S(2)}) async-start(f32[256,1,128]{2,1,0:T(1,128)} %bitcast.10), calls=%async_computation.2 | async-start | bytes 262144 | tf_op jit(solution)/shard_map/all_to_all | solution.py:688
  81.6 8.6 %collective-permute-start.5 = (f32[16,8,128]{2,1,0:T(8,128)S(1)}, f32[16,8,128]{2,1,0:T(8,128)S(1)}, u32[]{:S(2)}, u32[]{:S(2)}) collective-permute-start(f32[16,8,128]{2,1,0:T(8,128)S(1)} %get-tuple-element.72), channel_id=1, source_target_pairs={{0,32},{1,33},{2,34},{3,35},{4,36},{5,37},{6,38},{7,39},{8,40},{9,... | collective-permute-start | bytes 196616 | tf_op jit(solution)/shard_map/ppermute | solution.py:709
  83.2 7.0 %collective-permute-start.6 = (f32[16,8,128]{2,1,0:T(8,128)S(1)}, f32[16,8,128]{2,1,0:T(8,128)S(1)}, u32[]{:S(2)}, u32[]{:S(2)}) collective-permute-start(f32[16,8,128]{2,1,0:T(8,128)S(1)} %get-tuple-element.73), channel_id=1, source_target_pairs={{32,64},{33,65},{34,66},{35,67},{36,68},{37,69},{38,70},{39,71},{4... | collective-permute-start | bytes 196616 | tf_op jit(solution)/shard_map/ppermute | solution.py:709
  84.6 5.6 %collective-permute-start.8 = (f32[8,8,128]{2,1,0:T(8,128)S(1)}, f32[8,8,128]{2,1,0:T(8,128)S(1)}, u32[]{:S(2)}, u32[]{:S(2)}) collective-permute-start(f32[8,8,128]{2,1,0:T(8,128)S(1)} %get-tuple-element.75), channel_id=1, source_target_pairs={{1,4},{33,36},{65,68},{97,100},{129,132},{161,164},{193,196},{225,... | collective-permute-start | bytes 98312 | tf_op jit(solution)/shard_map/ppermute | solution.py:720
  95.9 7.1 %collective-permute-start.9 = (f32[16,8,128]{2,1,0:T(8,128)S(1)}, f32[16,8,128]{2,1,0:T(8,128)S(1)}, u32[]{:S(2)}, u32[]{:S(2)}) collective-permute-start(f32[16,8,128]{2,1,0:T(8,128)S(1)} %get-tuple-element.79), channel_id=1, source_target_pairs={{0,32},{1,33},{2,34},{3,35},{4,36},{5,37},{6,38},{7,39},{8,40},{9,... | collective-permute-start | bytes 196616 | tf_op jit(solution)/shard_map/ppermute | solution.py:709
  96.9 6.1 %collective-permute-start.10 = (f32[16,8,128]{2,1,0:T(8,128)S(1)}, f32[16,8,128]{2,1,0:T(8,128)S(1)}, u32[]{:S(2)}, u32[]{:S(2)}) collective-permute-start(f32[16,8,128]{2,1,0:T(8,128)S(1)} %get-tuple-element.80), channel_id=1, source_target_pairs={{32,64},{33,65},{34,66},{35,67},{36,68},{37,69},{38,70},{39,71},{4... | collective-permute-start | bytes 196616 | tf_op jit(solution)/shard_map/ppermute | solution.py:709
  97.8 5.2 %collective-permute-start.12 = (f32[8,8,128]{2,1,0:T(8,128)S(1)}, f32[8,8,128]{2,1,0:T(8,128)S(1)}, u32[]{:S(2)}, u32[]{:S(2)}) collective-permute-start(f32[8,8,128]{2,1,0:T(8,128)S(1)} %get-tuple-element.82), channel_id=1, source_target_pairs={{1,4},{33,36},{65,68},{97,100},{129,132},{161,164},{193,196},{225,... | collective-permute-start | bytes 98312 | tf_op jit(solution)/shard_map/ppermute | solution.py:720
  132.0 19.3 %all-to-all-start.4 = ((f32[256,1,128]{2,1,0:T(1,128)}), f32[256,1,128]{2,1,0:T(1,128)}, u32[]{:S(2)}, u32[]{:S(2)}) async-start(f32[256,1,128]{2,1,0:T(1,128)} %bitcast.16), calls=%async_computation.4 | async-start | bytes 262144 | tf_op jit(solution)/shard_map/all_to_all | solution.py:688
  138.7 8.5 %collective-permute-start.13 = (f32[16,8,128]{2,1,0:T(8,128)S(1)}, f32[16,8,128]{2,1,0:T(8,128)S(1)}, u32[]{:S(2)}, u32[]{:S(2)}) collective-permute-start(f32[16,8,128]{2,1,0:T(8,128)S(1)} %get-tuple-element.90), channel_id=1, source_target_pairs={{0,32},{1,33},{2,34},{3,35},{4,36},{5,37},{6,38},{7,39},{8,40},{9,... | collective-permute-start | bytes 196616 | tf_op jit(solution)/shard_map/ppermute | solution.py:709
  140.0 7.2 %collective-permute-start.14 = (f32[16,8,128]{2,1,0:T(8,128)S(1)}, f32[16,8,128]{2,1,0:T(8,128)S(1)}, u32[]{:S(2)}, u32[]{:S(2)}) collective-permute-start(f32[16,8,128]{2,1,0:T(8,128)S(1)} %get-tuple-element.91), channel_id=1, source_target_pairs={{32,64},{33,65},{34,66},{35,67},{36,68},{37,69},{38,70},{39,71},{4... | collective-permute-start | bytes 196616 | tf_op jit(solution)/shard_map/ppermute | solution.py:709
  141.5 5.7 %collective-permute-start.16 = (f32[8,8,128]{2,1,0:T(8,128)S(1)}, f32[8,8,128]{2,1,0:T(8,128)S(1)}, u32[]{:S(2)}, u32[]{:S(2)}) collective-permute-start(f32[8,8,128]{2,1,0:T(8,128)S(1)} %get-tuple-element.93), channel_id=1, source_target_pairs={{1,4},{33,36},{65,68},{97,100},{129,132},{161,164},{193,196},{225,... | collective-permute-start | bytes 98312 | tf_op jit(solution)/shard_map/ppermute | solution.py:720
  153.9 23.1 %all-to-all-start.5 = ((f32[256,1,128]{2,1,0:T(1,128)}), f32[256,1,128]{2,1,0:T(1,128)S(1)}, u32[]{:S(2)}, u32[]{:S(2)}) async-start(f32[256,1,128]{2,1,0:T(1,128)} %bitcast.19), calls=%async_computation.5 | async-start | bytes 262144 | tf_op jit(solution)/shard_map/all_to_all | solution.py:688
  163.6 8.6 %collective-permute-start.17 = (f32[16,8,128]{2,1,0:T(8,128)S(1)}, f32[16,8,128]{2,1,0:T(8,128)S(1)}, u32[]{:S(2)}, u32[]{:S(2)}) collective-permute-start(f32[16,8,128]{2,1,0:T(8,128)S(1)} %get-tuple-element.98), channel_id=1, source_target_pairs={{0,32},{1,33},{2,34},{3,35},{4,36},{5,37},{6,38},{7,39},{8,40},{9,... | collective-permute-start | bytes 196616 | tf_op jit(solution)/shard_map/ppermute | solution.py:709
  165.2 7.0 %collective-permute-start.18 = (f32[16,8,128]{2,1,0:T(8,128)S(1)}, f32[16,8,128]{2,1,0:T(8,128)S(1)}, u32[]{:S(2)}, u32[]{:S(2)}) collective-permute-start(f32[16,8,128]{2,1,0:T(8,128)S(1)} %get-tuple-element.99), channel_id=1, source_target_pairs={{32,64},{33,65},{34,66},{35,67},{36,68},{37,69},{38,70},{39,71},{4... | collective-permute-start | bytes 196616 | tf_op jit(solution)/shard_map/ppermute | solution.py:709
  166.6 5.6 %collective-permute-start.20 = (f32[8,8,128]{2,1,0:T(8,128)S(1)}, f32[8,8,128]{2,1,0:T(8,128)S(1)}, u32[]{:S(2)}, u32[]{:S(2)}) collective-permute-start(f32[8,8,128]{2,1,0:T(8,128)S(1)} %get-tuple-element.101), channel_id=1, source_target_pairs={{1,4},{33,36},{65,68},{97,100},{129,132},{161,164},{193,196},{225,... | collective-permute-start | bytes 98312 | tf_op jit(solution)/shard_map/ppermute | solution.py:720
  177.9 7.1 %collective-permute-start.21 = (f32[16,8,128]{2,1,0:T(8,128)S(1)}, f32[16,8,128]{2,1,0:T(8,128)S(1)}, u32[]{:S(2)}, u32[]{:S(2)}) collective-permute-start(f32[16,8,128]{2,1,0:T(8,128)S(1)} %get-tuple-element.105), channel_id=1, source_target_pairs={{0,32},{1,33},{2,34},{3,35},{4,36},{5,37},{6,38},{7,39},{8,40},{9,... | collective-permute-start | bytes 196616 | tf_op jit(solution)/shard_map/ppermute | solution.py:709
  178.8 6.1 %collective-permute-start.22 = (f32[16,8,128]{2,1,0:T(8,128)S(1)}, f32[16,8,128]{2,1,0:T(8,128)S(1)}, u32[]{:S(2)}, u32[]{:S(2)}) collective-permute-start(f32[16,8,128]{2,1,0:T(8,128)S(1)} %get-tuple-element.106), channel_id=1, source_target_pairs={{32,64},{33,65},{34,66},{35,67},{36,68},{37,69},{38,70},{39,71},{4... | collective-permute-start | bytes 196616 | tf_op jit(solution)/shard_map/ppermute | solution.py:709
  179.7 5.2 %collective-permute-start.24 = (f32[8,8,128]{2,1,0:T(8,128)S(1)}, f32[8,8,128]{2,1,0:T(8,128)S(1)}, u32[]{:S(2)}, u32[]{:S(2)}) collective-permute-start(f32[8,8,128]{2,1,0:T(8,128)S(1)} %get-tuple-element.108), channel_id=1, source_target_pairs={{1,4},{33,36},{65,68},{97,100},{129,132},{161,164},{193,196},{225,... | collective-permute-start | bytes 98312 | tf_op jit(solution)/shard_map/ppermute | solution.py:720
  208.9 14.1 %all-to-all-start.7 = ((f32[8,1,128]{2,1,0:T(1,128)}), f32[8,1,128]{2,1,0:T(1,128)S(1)}, u32[]{:S(2)}, u32[]{:S(2)}) async-start(f32[8,1,128]{2,1,0:T(1,128)} %bitcast.26), calls=%async_computation.7 | async-start | bytes 8192 | tf_op jit(solution)/shard_map/all_to_all | solution.py:694
  (12 other events, 58.9 us)

commit v7 on v6

--- a/solution.py
+++ b/solution.py
@@ -778,7 +778,7 @@
     for outer in range(OUTER):
         if outer > 0:
             primal, *sides, row = call(
-                primal_restart_kernel, STEP_OUTS, STEP_SCRATCH, aliases={0: 5, 1: 0}
+                primal_restart_kernel, STEP_OUTS, STEP_SCRATCH, aliases={1: 0}
             )(row_sums, primal, tail, const)
         duals, inwards = [dual], [inward]
         for inner in range(1, INNER):
@@ -787,7 +787,7 @@
                 functools.partial(step_kernel, inner),
                 [DUAL_ARRAY, INWARD_ARRAY] + STEP_OUTS,
                 STEP_SCRATCH + DUAL_SCRATCH + [TAIL_ARRAY],
-                aliases={0: 7, 1: 2, 3: 3, 4: 4, 5: 5, 6: 6} | ({8: 1} if inner == 1 else {}),
+                aliases={1: 2, 3: 3, 4: 4, 5: 5, 6: 6} | ({8: 1} if inner == 1 else {}),
             )(row_sums, primal, const, *halo(*sides), dual, inward)
             duals.append(dual)
             inwards.append(inward)
@@ -797,7 +797,7 @@
                 dual_restart_kernel,
                 DUAL_OUTS + [(DEVICES, 128)],
                 DUAL_SCRATCH,
-                aliases={8: 3, 9: 1, 11: 0},
+                aliases={9: 1},
             )(primal, const, *sides, dual, inward, row, inwards[1], duals[0], duals[1])
             row_sums = share_row(row)
         else:

time: 225 us -> 218 us (0.969)
  starting transfers between devices: 93.3 us -> 90.5 us
  Pallas kernels: 21.3 us -> 18.8 us
    all_to_all x4, starting transfers between devices: 39.6 us -> 36.3 us  [share_row(): return lax.all_to_all(row, EVERY, 0, 0, tiled=True)]
    pallas_call x14, Pallas kernels: 21.3 us -> 18.8 us  [run(): pl.pallas_call(kernel, out_shape=[f32(*shape) for shape in outs], in_spec...]
where the time goes in v7:
time: 218 us; the launch traced here: 217 us
  starting transfers between devices  90.5 us (42%)
  waiting for transfers between devices  57.7 us (26%)
  blocking collectives  46.6 us (21%)
  Pallas kernels  18.8 us (9%)
    all_to_all x4, starting transfers between devices, share_row(): return lax.all_to_all(row, EVERY, 0, 0, tiled=True)  36.3 us
    all_to_all x1, blocking collectives, share_row(): return lax.all_to_all(row, EVERY, 0, 0, tiled=True)  25.3 us
    all_to_all x1, blocking collectives, exchange(): return lax.all_to_all(slots, EVERY, 0, 0, axis_index_groups=groups)  21.3 us
    ppermute x12, starting transfers between devices, swap_y(): return lax.ppermute(value, EVERY, pairs)  20.6 us
    pallas_call x14, Pallas kernels, run(): pl.pallas_call(kernel, out_shape=[f32(*shape) for shape in outs], in_spec...  18.8 us
    all_to_all x4, waiting for transfers between devices, share_row(): return lax.all_to_all(row, EVERY, 0, 0, tiled=True)  18.7 us
    all_to_all x1, waiting for transfers between devices, exchange(): return lax.all_to_all(slots, EVERY, 0, 0, axis_index_groups=groups)  17.8 us
    ppermute x12, waiting for transfers between devices, swap_y(): return lax.ppermute(value, EVERY, pairs)  15.7 us
  transfers between devices with their start and end apart: 31, of which 12 were waited for; matrix products, arithmetic and copies ran while one was open for 0% of the time, Pallas kernels for 2%

profile of v7, /device:TPU:1, one launch (start us, length us, event | category | flops | bytes accessed | tf_op | source)
XLA Modules:
  0.0 217.1 jit_solution(858317867969534396)
XLA Ops:
  2.9 2.7 %shard_map.138.send = f32[32,9,8,128]{3,2,1,0:T(8,128)} custom-call(f32[4]{0:T(128)} %caps_at.1, f32[4]{0:T(128)} %limits_at.1, f32[8]{0:T(128)} %density_at.1, s32[1,128]{1,0:T(1,128)} %slope_at.3, s32[64,128]{1,0:T(8,128)} %bitcast.47, f32[64,128]{1,0:T(8,128)} %bitcast.48, f32[4,64,128]{2,1,0:T(8,128)} %bitcast.45, f32[5,4,64,128]{3,2,1,0:T(8,128)} %bitcast.44, ...), custom_call_target="tpu_custom_call" | custom-call | flops 1000000 | bytes 4000000 | tf_op jit(solution)/shard_map/pallas_call | solution.py:651
  8.0 13.2 %all-to-all-start = ((f32[32,9,8,128]{3,2,1,0:T(8,128)}), f32[32,9,8,128]{3,2,1,0:T(8,128)S(1)}, u32[]{:S(2)}, u32[]{:S(2)}) async-start(f32[32,9,8,128]{3,2,1,0:T(8,128)} %shard_map.139), calls=%async_computation | async-start | bytes 2359296 | tf_op jit(solution)/shard_map/all_to_all | solution.py:699
  21.8 17.8 %all-to-all-done.got = f32[32,9,8,128]{3,2,1,0:T(8,128)S(1)} async-done(((f32[32,9,8,128]{3,2,1,0:T(8,128)}), f32[32,9,8,128]{3,2,1,0:T(8,128)S(1)}, u32[]{:S(2)}, u32[]{:S(2)}) %all-to-all-start) | async-done | bytes 1179680 | tf_op jit(solution)/shard_map/all_to_all | solution.py:699
  41.1 12.4 %all-to-all-start.1 = ((f32[256,1,128]{2,1,0:T(1,128)}), f32[256,1,128]{2,1,0:T(1,128)S(1)}, u32[]{:S(2)}, u32[]{:S(2)}) async-start(f32[256,1,128]{2,1,0:T(1,128)} %bitcast.7), calls=%async_computation.1 | async-start | bytes 262144 | tf_op jit(solution)/shard_map/all_to_all | solution.py:688
  56.5 3.0 %collective-permute-start.4 = (f32[8,8,128]{2,1,0:T(8,128)S(1)}, f32[8,8,128]{2,1,0:T(8,128)S(1)}, u32[]{:S(2)}, u32[]{:S(2)}) collective-permute-start(f32[8,8,128]{2,1,0:T(8,128)S(1)} %get-tuple-element.67), channel_id=1, source_target_pairs={{1,4},{33,36},{65,68},{97,100},{129,132},{161,164},{193,196},{225,... | collective-permute-start | bytes 98312 | tf_op jit(solution)/shard_map/ppermute | solution.py:720
  59.6 2.5 %collective-permute-done.4.y_two = f32[8,8,128]{2,1,0:T(8,128)S(1)} collective-permute-done((f32[8,8,128]{2,1,0:T(8,128)S(1)}, f32[8,8,128]{2,1,0:T(8,128)S(1)}, u32[]{:S(2)}, u32[]{:S(2)}) %collective-permute-start.4) | collective-permute-done | bytes 32800 | tf_op jit(solution)/shard_map/ppermute | solution.py:720
  62.1 4.7 %all-to-all-done.1 = f32[256,1,128]{2,1,0:T(1,128)S(1)} async-done(((f32[256,1,128]{2,1,0:T(1,128)}), f32[256,1,128]{2,1,0:T(1,128)S(1)}, u32[]{:S(2)}, u32[]{:S(2)}) %all-to-all-start.1) | async-done | bytes 131104 | tf_op jit(solution)/shard_map/all_to_all | solution.py:688
  68.5 9.3 %all-to-all-start.2 = ((f32[256,1,128]{2,1,0:T(1,128)}), f32[256,1,128]{2,1,0:T(1,128)S(1)}, u32[]{:S(2)}, u32[]{:S(2)}) async-start(f32[256,1,128]{2,1,0:T(1,128)} %bitcast.10), calls=%async_computation.2 | async-start | bytes 262144 | tf_op jit(solution)/shard_map/all_to_all | solution.py:688
  80.8 3.0 %collective-permute-start.8 = (f32[8,8,128]{2,1,0:T(8,128)S(1)}, f32[8,8,128]{2,1,0:T(8,128)S(1)}, u32[]{:S(2)}, u32[]{:S(2)}) collective-permute-start(f32[8,8,128]{2,1,0:T(8,128)S(1)} %get-tuple-element.75), channel_id=1, source_target_pairs={{1,4},{33,36},{65,68},{97,100},{129,132},{161,164},{193,196},{225,... | collective-permute-start | bytes 98312 | tf_op jit(solution)/shard_map/ppermute | solution.py:720
  83.8 2.5 %collective-permute-done.8.y_two = f32[8,8,128]{2,1,0:T(8,128)S(1)} collective-permute-done((f32[8,8,128]{2,1,0:T(8,128)S(1)}, f32[8,8,128]{2,1,0:T(8,128)S(1)}, u32[]{:S(2)}, u32[]{:S(2)}) %collective-permute-start.8) | collective-permute-done | bytes 32800 | tf_op jit(solution)/shard_map/ppermute | solution.py:720
  86.4 4.7 %all-to-all-done.2 = f32[256,1,128]{2,1,0:T(1,128)S(1)} async-done(((f32[256,1,128]{2,1,0:T(1,128)}), f32[256,1,128]{2,1,0:T(1,128)S(1)}, u32[]{:S(2)}, u32[]{:S(2)}) %all-to-all-start.2) | async-done | bytes 131104 | tf_op jit(solution)/shard_map/all_to_all | solution.py:688
  96.3 2.8 %collective-permute-done.12.y_two = f32[8,8,128]{2,1,0:T(8,128)S(1)} collective-permute-done((f32[8,8,128]{2,1,0:T(8,128)S(1)}, f32[8,8,128]{2,1,0:T(8,128)S(1)}, u32[]{:S(2)}, u32[]{:S(2)}) %collective-permute-start.12) | collective-permute-done | bytes 32800 | tf_op jit(solution)/shard_map/ppermute | solution.py:720
  101.0 25.3 %all_to_all.76 = f32[256,1,128]{2,1,0:T(1,128)S(1)} all-to-all(f32[256,1,128]{2,1,0:T(1,128)S(1)} %bitcast.41), channel_id=1, replica_groups=mesh['strip'=16,'period'=16] {'strip','period'}, dimensions={0} | all-to-all | bytes 262144 | tf_op jit(solution)/shard_map/all_to_all | solution.py:688
  127.8 5.4 %all-to-all-start.4 = ((f32[256,1,128]{2,1,0:T(1,128)}), f32[256,1,128]{2,1,0:T(1,128)S(1)}, u32[]{:S(2)}, u32[]{:S(2)}) async-start(f32[256,1,128]{2,1,0:T(1,128)} %bitcast.16), calls=%async_computation.4 | async-start | bytes 262144 | tf_op jit(solution)/shard_map/all_to_all | solution.py:688
  136.4 3.0 %collective-permute-start.16 = (f32[8,8,128]{2,1,0:T(8,128)S(1)}, f32[8,8,128]{2,1,0:T(8,128)S(1)}, u32[]{:S(2)}, u32[]{:S(2)}) collective-permute-start(f32[8,8,128]{2,1,0:T(8,128)S(1)} %get-tuple-element.93), channel_id=1, source_target_pairs={{1,4},{33,36},{65,68},{97,100},{129,132},{161,164},{193,196},{225,... | collective-permute-start | bytes 98312 | tf_op jit(solution)/shard_map/ppermute | solution.py:720
  139.5 2.5 %collective-permute-done.16.y_two = f32[8,8,128]{2,1,0:T(8,128)S(1)} collective-permute-done((f32[8,8,128]{2,1,0:T(8,128)S(1)}, f32[8,8,128]{2,1,0:T(8,128)S(1)}, u32[]{:S(2)}, u32[]{:S(2)}) %collective-permute-start.16) | collective-permute-done | bytes 32800 | tf_op jit(solution)/shard_map/ppermute | solution.py:720
  142.0 4.7 %all-to-all-done.4 = f32[256,1,128]{2,1,0:T(1,128)S(1)} async-done(((f32[256,1,128]{2,1,0:T(1,128)}), f32[256,1,128]{2,1,0:T(1,128)S(1)}, u32[]{:S(2)}, u32[]{:S(2)}) %all-to-all-start.4) | async-done | bytes 131104 | tf_op jit(solution)/shard_map/all_to_all | solution.py:688
  148.4 9.3 %all-to-all-start.5 = ((f32[256,1,128]{2,1,0:T(1,128)}), f32[256,1,128]{2,1,0:T(1,128)S(1)}, u32[]{:S(2)}, u32[]{:S(2)}) async-start(f32[256,1,128]{2,1,0:T(1,128)} %bitcast.19), calls=%async_computation.5 | async-start | bytes 262144 | tf_op jit(solution)/shard_map/all_to_all | solution.py:688
  160.7 3.0 %collective-permute-start.20 = (f32[8,8,128]{2,1,0:T(8,128)S(1)}, f32[8,8,128]{2,1,0:T(8,128)S(1)}, u32[]{:S(2)}, u32[]{:S(2)}) collective-permute-start(f32[8,8,128]{2,1,0:T(8,128)S(1)} %get-tuple-element.101), channel_id=1, source_target_pairs={{1,4},{33,36},{65,68},{97,100},{129,132},{161,164},{193,196},{225,... | collective-permute-start | bytes 98312 | tf_op jit(solution)/shard_map/ppermute | solution.py:720
  166.3 4.7 %all-to-all-done.5 = f32[256,1,128]{2,1,0:T(1,128)S(1)} async-done(((f32[256,1,128]{2,1,0:T(1,128)}), f32[256,1,128]{2,1,0:T(1,128)S(1)}, u32[]{:S(2)}, u32[]{:S(2)}) %all-to-all-start.5) | async-done | bytes 131104 | tf_op jit(solution)/shard_map/all_to_all | solution.py:688
  176.2 2.8 %collective-permute-done.24.y_two = f32[8,8,128]{2,1,0:T(8,128)S(1)} collective-permute-done((f32[8,8,128]{2,1,0:T(8,128)S(1)}, f32[8,8,128]{2,1,0:T(8,128)S(1)}, u32[]{:S(2)}, u32[]{:S(2)}) %collective-permute-start.24) | collective-permute-done | bytes 32800 | tf_op jit(solution)/shard_map/ppermute | solution.py:720
  179.8 21.3 %all_to_all.77.got = f32[32,7,8,128]{3,2,1,0:T(8,128)S(1)} all-to-all(f32[32,7,8,128]{3,2,1,0:T(8,128)S(1)} %shard_map.147), channel_id=1, replica_groups={{0,1,2,3,4,5,6,7,8,9,10,11,12,13,14,15,16,17,18,19,20,21,22,23,24,25,26..., dimensions={0} | all-to-all | bytes 1835008 | tf_op jit(solution)/shard_map/all_to_all | solution.py:699
  201.9 7.6 %all-to-all-start.7 = ((f32[8,1,128]{2,1,0:T(1,128)}), f32[8,1,128]{2,1,0:T(1,128)S(1)}, u32[]{:S(2)}, u32[]{:S(2)}) async-start(f32[8,1,128]{2,1,0:T(1,128)} %bitcast.26), calls=%async_computation.7 | async-start | bytes 8192 | tf_op jit(solution)/shard_map/all_to_all | solution.py:694
  210.7 5.4 %all-to-all-done.7 = f32[8,1,128]{2,1,0:T(1,128)S(1)} async-done(((f32[8,1,128]{2,1,0:T(1,128)}), f32[8,1,128]{2,1,0:T(1,128)S(1)}, u32[]{:S(2)}, u32[]{:S(2)}) %all-to-all-start.7) | async-done | bytes 4128 | tf_op jit(solution)/shard_map/all_to_all | solution.py:694
  (60 shorter events, 41.7 us)
Async XLA Ops:
  8.0 31.7 %all-to-all-start = ((f32[32,9,8,128]{3,2,1,0:T(8,128)}), f32[32,9,8,128]{3,2,1,0:T(8,128)S(1)}, u32[]{:S(2)}, u32[]{:S(2)}) async-start(f32[32,9,8,128]{3,2,1,0:T(8,128)} %shard_map.139), calls=%async_computation | async-start | bytes 2359296 | tf_op jit(solution)/shard_map/all_to_all | solution.py:699
  41.1 25.7 %all-to-all-start.1 = ((f32[256,1,128]{2,1,0:T(1,128)}), f32[256,1,128]{2,1,0:T(1,128)S(1)}, u32[]{:S(2)}, u32[]{:S(2)}) async-start(f32[256,1,128]{2,1,0:T(1,128)} %bitcast.7), calls=%async_computation.1 | async-start | bytes 262144 | tf_op jit(solution)/shard_map/all_to_all | solution.py:688
  53.5 8.6 %collective-permute-start.1 = (f32[16,8,128]{2,1,0:T(8,128)S(1)}, f32[16,8,128]{2,1,0:T(8,128)S(1)}, u32[]{:S(2)}, u32[]{:S(2)}) collective-permute-start(f32[16,8,128]{2,1,0:T(8,128)S(1)} %get-tuple-element.64), channel_id=1, source_target_pairs={{0,32},{1,33},{2,34},{3,35},{4,36},{5,37},{6,38},{7,39},{8,40},{9,... | collective-permute-start | bytes 196616 | tf_op jit(solution)/shard_map/ppermute | solution.py:709
  55.1 7.0 %collective-permute-start.2 = (f32[16,8,128]{2,1,0:T(8,128)S(1)}, f32[16,8,128]{2,1,0:T(8,128)S(1)}, u32[]{:S(2)}, u32[]{:S(2)}) collective-permute-start(f32[16,8,128]{2,1,0:T(8,128)S(1)} %get-tuple-element.65), channel_id=1, source_target_pairs={{32,64},{33,65},{34,66},{35,67},{36,68},{37,69},{38,70},{39,71},{4... | collective-permute-start | bytes 196616 | tf_op jit(solution)/shard_map/ppermute | solution.py:709
  56.5 5.6 %collective-permute-start.4 = (f32[8,8,128]{2,1,0:T(8,128)S(1)}, f32[8,8,128]{2,1,0:T(8,128)S(1)}, u32[]{:S(2)}, u32[]{:S(2)}) collective-permute-start(f32[8,8,128]{2,1,0:T(8,128)S(1)} %get-tuple-element.67), channel_id=1, source_target_pairs={{1,4},{33,36},{65,68},{97,100},{129,132},{161,164},{193,196},{225,... | collective-permute-start | bytes 98312 | tf_op jit(solution)/shard_map/ppermute | solution.py:720
  68.5 22.5 %all-to-all-start.2 = ((f32[256,1,128]{2,1,0:T(1,128)}), f32[256,1,128]{2,1,0:T(1,128)S(1)}, u32[]{:S(2)}, u32[]{:S(2)}) async-start(f32[256,1,128]{2,1,0:T(1,128)} %bitcast.10), calls=%async_computation.2 | async-start | bytes 262144 | tf_op jit(solution)/shard_map/all_to_all | solution.py:688
  77.8 8.6 %collective-permute-start.5 = (f32[16,8,128]{2,1,0:T(8,128)S(1)}, f32[16,8,128]{2,1,0:T(8,128)S(1)}, u32[]{:S(2)}, u32[]{:S(2)}) collective-permute-start(f32[16,8,128]{2,1,0:T(8,128)S(1)} %get-tuple-element.72), channel_id=1, source_target_pairs={{0,32},{1,33},{2,34},{3,35},{4,36},{5,37},{6,38},{7,39},{8,40},{9,... | collective-permute-start | bytes 196616 | tf_op jit(solution)/shard_map/ppermute | solution.py:709
  79.3 7.0 %collective-permute-start.6 = (f32[16,8,128]{2,1,0:T(8,128)S(1)}, f32[16,8,128]{2,1,0:T(8,128)S(1)}, u32[]{:S(2)}, u32[]{:S(2)}) collective-permute-start(f32[16,8,128]{2,1,0:T(8,128)S(1)} %get-tuple-element.73), channel_id=1, source_target_pairs={{32,64},{33,65},{34,66},{35,67},{36,68},{37,69},{38,70},{39,71},{4... | collective-permute-start | bytes 196616 | tf_op jit(solution)/shard_map/ppermute | solution.py:709
  80.8 5.6 %collective-permute-start.8 = (f32[8,8,128]{2,1,0:T(8,128)S(1)}, f32[8,8,128]{2,1,0:T(8,128)S(1)}, u32[]{:S(2)}, u32[]{:S(2)}) collective-permute-start(f32[8,8,128]{2,1,0:T(8,128)S(1)} %get-tuple-element.75), channel_id=1, source_target_pairs={{1,4},{33,36},{65,68},{97,100},{129,132},{161,164},{193,196},{225,... | collective-permute-start | bytes 98312 | tf_op jit(solution)/shard_map/ppermute | solution.py:720
  92.0 7.0 %collective-permute-start.9 = (f32[16,8,128]{2,1,0:T(8,128)S(1)}, f32[16,8,128]{2,1,0:T(8,128)S(1)}, u32[]{:S(2)}, u32[]{:S(2)}) collective-permute-start(f32[16,8,128]{2,1,0:T(8,128)S(1)} %get-tuple-element.79), channel_id=1, source_target_pairs={{0,32},{1,33},{2,34},{3,35},{4,36},{5,37},{6,38},{7,39},{8,40},{9,... | collective-permute-start | bytes 196616 | tf_op jit(solution)/shard_map/ppermute | solution.py:709
  92.9 6.2 %collective-permute-start.10 = (f32[16,8,128]{2,1,0:T(8,128)S(1)}, f32[16,8,128]{2,1,0:T(8,128)S(1)}, u32[]{:S(2)}, u32[]{:S(2)}) collective-permute-start(f32[16,8,128]{2,1,0:T(8,128)S(1)} %get-tuple-element.80), channel_id=1, source_target_pairs={{32,64},{33,65},{34,66},{35,67},{36,68},{37,69},{38,70},{39,71},{4... | collective-permute-start | bytes 196616 | tf_op jit(solution)/shard_map/ppermute | solution.py:709
  93.8 5.2 %collective-permute-start.12 = (f32[8,8,128]{2,1,0:T(8,128)S(1)}, f32[8,8,128]{2,1,0:T(8,128)S(1)}, u32[]{:S(2)}, u32[]{:S(2)}) collective-permute-start(f32[8,8,128]{2,1,0:T(8,128)S(1)} %get-tuple-element.82), channel_id=1, source_target_pairs={{1,4},{33,36},{65,68},{97,100},{129,132},{161,164},{193,196},{225,... | collective-permute-start | bytes 98312 | tf_op jit(solution)/shard_map/ppermute | solution.py:720
  127.8 18.9 %all-to-all-start.4 = ((f32[256,1,128]{2,1,0:T(1,128)}), f32[256,1,128]{2,1,0:T(1,128)S(1)}, u32[]{:S(2)}, u32[]{:S(2)}) async-start(f32[256,1,128]{2,1,0:T(1,128)} %bitcast.16), calls=%async_computation.4 | async-start | bytes 262144 | tf_op jit(solution)/shard_map/all_to_all | solution.py:688
  133.3 8.7 %collective-permute-start.13 = (f32[16,8,128]{2,1,0:T(8,128)S(1)}, f32[16,8,128]{2,1,0:T(8,128)S(1)}, u32[]{:S(2)}, u32[]{:S(2)}) collective-permute-start(f32[16,8,128]{2,1,0:T(8,128)S(1)} %get-tuple-element.90), channel_id=1, source_target_pairs={{0,32},{1,33},{2,34},{3,35},{4,36},{5,37},{6,38},{7,39},{8,40},{9,... | collective-permute-start | bytes 196616 | tf_op jit(solution)/shard_map/ppermute | solution.py:709
  135.0 7.0 %collective-permute-start.14 = (f32[16,8,128]{2,1,0:T(8,128)S(1)}, f32[16,8,128]{2,1,0:T(8,128)S(1)}, u32[]{:S(2)}, u32[]{:S(2)}) collective-permute-start(f32[16,8,128]{2,1,0:T(8,128)S(1)} %get-tuple-element.91), channel_id=1, source_target_pairs={{32,64},{33,65},{34,66},{35,67},{36,68},{37,69},{38,70},{39,71},{4... | collective-permute-start | bytes 196616 | tf_op jit(solution)/shard_map/ppermute | solution.py:709
  136.4 5.6 %collective-permute-start.16 = (f32[8,8,128]{2,1,0:T(8,128)S(1)}, f32[8,8,128]{2,1,0:T(8,128)S(1)}, u32[]{:S(2)}, u32[]{:S(2)}) collective-permute-start(f32[8,8,128]{2,1,0:T(8,128)S(1)} %get-tuple-element.93), channel_id=1, source_target_pairs={{1,4},{33,36},{65,68},{97,100},{129,132},{161,164},{193,196},{225,... | collective-permute-start | bytes 98312 | tf_op jit(solution)/shard_map/ppermute | solution.py:720
  148.4 22.5 %all-to-all-start.5 = ((f32[256,1,128]{2,1,0:T(1,128)}), f32[256,1,128]{2,1,0:T(1,128)S(1)}, u32[]{:S(2)}, u32[]{:S(2)}) async-start(f32[256,1,128]{2,1,0:T(1,128)} %bitcast.19), calls=%async_computation.5 | async-start | bytes 262144 | tf_op jit(solution)/shard_map/all_to_all | solution.py:688
  157.7 8.6 %collective-permute-start.17 = (f32[16,8,128]{2,1,0:T(8,128)S(1)}, f32[16,8,128]{2,1,0:T(8,128)S(1)}, u32[]{:S(2)}, u32[]{:S(2)}) collective-permute-start(f32[16,8,128]{2,1,0:T(8,128)S(1)} %get-tuple-element.98), channel_id=1, source_target_pairs={{0,32},{1,33},{2,34},{3,35},{4,36},{5,37},{6,38},{7,39},{8,40},{9,... | collective-permute-start | bytes 196616 | tf_op jit(solution)/shard_map/ppermute | solution.py:709
  159.3 7.0 %collective-permute-start.18 = (f32[16,8,128]{2,1,0:T(8,128)S(1)}, f32[16,8,128]{2,1,0:T(8,128)S(1)}, u32[]{:S(2)}, u32[]{:S(2)}) collective-permute-start(f32[16,8,128]{2,1,0:T(8,128)S(1)} %get-tuple-element.99), channel_id=1, source_target_pairs={{32,64},{33,65},{34,66},{35,67},{36,68},{37,69},{38,70},{39,71},{4... | collective-permute-start | bytes 196616 | tf_op jit(solution)/shard_map/ppermute | solution.py:709
  160.7 5.6 %collective-permute-start.20 = (f32[8,8,128]{2,1,0:T(8,128)S(1)}, f32[8,8,128]{2,1,0:T(8,128)S(1)}, u32[]{:S(2)}, u32[]{:S(2)}) collective-permute-start(f32[8,8,128]{2,1,0:T(8,128)S(1)} %get-tuple-element.101), channel_id=1, source_target_pairs={{1,4},{33,36},{65,68},{97,100},{129,132},{161,164},{193,196},{225,... | collective-permute-start | bytes 98312 | tf_op jit(solution)/shard_map/ppermute | solution.py:720
  171.9 7.0 %collective-permute-start.21 = (f32[16,8,128]{2,1,0:T(8,128)S(1)}, f32[16,8,128]{2,1,0:T(8,128)S(1)}, u32[]{:S(2)}, u32[]{:S(2)}) collective-permute-start(f32[16,8,128]{2,1,0:T(8,128)S(1)} %get-tuple-element.105), channel_id=1, source_target_pairs={{0,32},{1,33},{2,34},{3,35},{4,36},{5,37},{6,38},{7,39},{8,40},{9,... | collective-permute-start | bytes 196616 | tf_op jit(solution)/shard_map/ppermute | solution.py:709
  172.8 6.2 %collective-permute-start.22 = (f32[16,8,128]{2,1,0:T(8,128)S(1)}, f32[16,8,128]{2,1,0:T(8,128)S(1)}, u32[]{:S(2)}, u32[]{:S(2)}) collective-permute-start(f32[16,8,128]{2,1,0:T(8,128)S(1)} %get-tuple-element.106), channel_id=1, source_target_pairs={{32,64},{33,65},{34,66},{35,67},{36,68},{37,69},{38,70},{39,71},{4... | collective-permute-start | bytes 196616 | tf_op jit(solution)/shard_map/ppermute | solution.py:709
  173.7 5.2 %collective-permute-start.24 = (f32[8,8,128]{2,1,0:T(8,128)S(1)}, f32[8,8,128]{2,1,0:T(8,128)S(1)}, u32[]{:S(2)}, u32[]{:S(2)}) collective-permute-start(f32[8,8,128]{2,1,0:T(8,128)S(1)} %get-tuple-element.108), channel_id=1, source_target_pairs={{1,4},{33,36},{65,68},{97,100},{129,132},{161,164},{193,196},{225,... | collective-permute-start | bytes 98312 | tf_op jit(solution)/shard_map/ppermute | solution.py:720
  201.9 14.1 %all-to-all-start.7 = ((f32[8,1,128]{2,1,0:T(1,128)}), f32[8,1,128]{2,1,0:T(1,128)S(1)}, u32[]{:S(2)}, u32[]{:S(2)}) async-start(f32[8,1,128]{2,1,0:T(1,128)} %bitcast.26), calls=%async_computation.7 | async-start | bytes 8192 | tf_op jit(solution)/shard_map/all_to_all | solution.py:694
  (10 other events, 56.4 us)

commit v8 on v7

--- a/solution.py
+++ b/solution.py
@@ -29,7 +29,7 @@
 BOUND, SHARE, RIM, EXTRA = 5, 6, 7, 8
 SLOTS = 9
 LANE_PRIMAL, LANE_DUAL, LANE_TONS = 32, 33, 34
-HALO, EDGES, TONS, VALUE, ODD_X, ODD_Y, LIMITS = 5, 6, 7, 8, 9, 10, 11
+HALO, EDGES, TONS, VALUE, ODD_X, EVEN_Y, LIMITS = 5, 6, 7, 8, 9, 10, 11
 CONSTANTS = 15
 TABLE = ROWS // 8
 SHARES, SHARE_SUM, SHARE_FIRST, HEAD = 0, ROWS, 2 * ROWS, 3 * ROWS
@@ -255,7 +255,7 @@
     shape = (8, 128)
     primal[WEIGHT] = jnp.broadcast_to(weight[...], shape)
     const[ODD_X] = jnp.full(shape, lax.axis_index("strip") // 2 % 2).astype(F32)
-    const[ODD_Y] = jnp.full(shape, lax.axis_index("period") % 2).astype(F32)
+    const[EVEN_Y] = jnp.full(shape, 1 - lax.axis_index("period") % 2).astype(F32)
     lane = lanes(shape)
     deep = ((lane & 63) >= 1).astype(F32)
     half = later_half(shape)
@@ -353,7 +353,7 @@
     new[WEIGHT] = jnp.broadcast_to(weight, shape)
     half = later_half(shape)
     odd_x = const[ODD_X] > 0.5
-    odd_y = const[ODD_Y] > 0.5
+    even_y = const[EVEN_Y] > 0.5
     carry = jnp.zeros(shape, F32)
     moved = jnp.zeros(shape, F32)
     mined = []
@@ -392,8 +392,8 @@
             x_two[r // 2] = jnp.where(odd_x, highs, lows)
         mined.append(tons * ahead)
     for n in range(2 * TABLE):
-        y_one[n] = jnp.where(odd_y, new[FIRST + n], new[LAST + n])
-        y_two[n] = jnp.where(odd_y, new[LAST + n], new[FIRST + n])
+        y_one[n] = jnp.where(even_y, new[FIRST + n], new[LAST + n])
+        y_two[n] = jnp.where(even_y, new[LAST + n], new[FIRST + n])
     mined.append(tons)
     sums = half_sums(jnp.concatenate(mined, axis=0))
     lane = lanes(shape)
@@ -431,7 +431,7 @@
 
 
 def dual_tables(primal, const, y_one, y_two, inward, steps, ahead):
-    odd_y = const[ODD_Y, 0:1] > 0.5
+    even_y = const[EVEN_Y, 0:1] > 0.5
     periods = period_table()
     weight = primal[WEIGHT, 0:1]
     steps[0] = weight / (2.0 * (periods + 1.0))
@@ -442,7 +442,7 @@
         for x in range(2):
             at = 2 * n + x
             one, two = table(y_one, x * TABLE), table(y_two, x * TABLE)
-            there = jnp.where(odd_y, two, one) if n else jnp.where(odd_y, one, two)
+            there = jnp.where(even_y, two, one) if n else jnp.where(even_y, one, two)
             ahead[n, x] = down(there)
             here = table(primal, inside + x * TABLE)
             price = table(inward, edge_at(n, x)) + steps[0] * (there - down(here))
@@ -721,8 +721,7 @@
 
 
 def halo(x_one, x_two, y_one, y_two):
-    y_one, y_two = swap_y(y_one, 0), swap_y(y_two, 1)
-    return swap_x(x_one, 0), swap_x(x_two, 1), y_one, y_two
+    return swap_x(x_one, 0), swap_x(x_two, 1), swap_y(y_one, 1), swap_y(y_two, 0)
 
 
 def per_device(

time: 218 us -> 217 us (level)
    ppermute x12, waiting for transfers between devices: 15.7 us -> 13 us  [swap_y(): return lax.ppermute(value, EVERY, pairs)]
    all_to_all x4, waiting for transfers between devices: 18.7 us -> 21.2 us  [share_row(): return lax.all_to_all(row, EVERY, 0, 0, tiled=True)]
where the time goes in v8:
time: 217 us; the launch traced here: 216 us
  starting transfers between devices  89.7 us (41%)
  waiting for transfers between devices  57.5 us (26%)
  blocking collectives  46.5 us (21%)
  Pallas kernels  18.8 us (9%)
    all_to_all x4, starting transfers between devices, share_row(): return lax.all_to_all(row, EVERY, 0, 0, tiled=True)  36 us
    all_to_all x1, blocking collectives, share_row(): return lax.all_to_all(row, EVERY, 0, 0, tiled=True)  25.2 us
    all_to_all x1, blocking collectives, exchange(): return lax.all_to_all(slots, EVERY, 0, 0, axis_index_groups=groups)  21.3 us
    all_to_all x4, waiting for transfers between devices, share_row(): return lax.all_to_all(row, EVERY, 0, 0, tiled=True)  21.2 us
    ppermute x12, starting transfers between devices, swap_y(): return lax.ppermute(value, EVERY, pairs)  20.2 us
    pallas_call x14, Pallas kernels, run(): pl.pallas_call(kernel, out_shape=[f32(*shape) for shape in outs], in_spec...  18.8 us
    all_to_all x1, waiting for transfers between devices, exchange(): return lax.all_to_all(slots, EVERY, 0, 0, axis_index_groups=groups)  17.8 us
    all_to_all x1, starting transfers between devices, exchange(): return lax.all_to_all(slots, EVERY, 0, 0, axis_index_groups=groups)  13.2 us
  transfers between devices with their start and end apart: 31, of which 12 were waited for; matrix products, arithmetic and copies ran while one was open for 0% of the time, Pallas kernels for 2%

profile of v8, /device:TPU:1, one launch (start us, length us, event | category | flops | bytes accessed | tf_op | source)
XLA Modules:
  0.0 216.0 jit_solution(14236578527112598885)
XLA Ops:
  2.9 2.7 %shard_map.138.send = f32[32,9,8,128]{3,2,1,0:T(8,128)} custom-call(f32[4]{0:T(128)} %caps_at.1, f32[4]{0:T(128)} %limits_at.1, f32[8]{0:T(128)} %density_at.1, s32[1,128]{1,0:T(1,128)} %slope_at.3, s32[64,128]{1,0:T(8,128)} %bitcast.47, f32[64,128]{1,0:T(8,128)} %bitcast.48, f32[4,64,128]{2,1,0:T(8,128)} %bitcast.45, f32[5,4,64,128]{3,2,1,0:T(8,128)} %bitcast.44, ...), custom_call_target="tpu_custom_call" | custom-call | flops 1000000 | bytes 4000000 | tf_op jit(solution)/shard_map/pallas_call | solution.py:651
  8.0 13.2 %all-to-all-start = ((f32[32,9,8,128]{3,2,1,0:T(8,128)}), f32[32,9,8,128]{3,2,1,0:T(8,128)S(1)}, u32[]{:S(2)}, u32[]{:S(2)}) async-start(f32[32,9,8,128]{3,2,1,0:T(8,128)} %shard_map.139), calls=%async_computation | async-start | bytes 2359296 | tf_op jit(solution)/shard_map/all_to_all | solution.py:699
  21.8 17.8 %all-to-all-done.got = f32[32,9,8,128]{3,2,1,0:T(8,128)S(1)} async-done(((f32[32,9,8,128]{3,2,1,0:T(8,128)}), f32[32,9,8,128]{3,2,1,0:T(8,128)S(1)}, u32[]{:S(2)}, u32[]{:S(2)}) %all-to-all-start) | async-done | bytes 1179680 | tf_op jit(solution)/shard_map/all_to_all | solution.py:699
  41.1 12.4 %all-to-all-start.1 = ((f32[256,1,128]{2,1,0:T(1,128)}), f32[256,1,128]{2,1,0:T(1,128)S(1)}, u32[]{:S(2)}, u32[]{:S(2)}) async-start(f32[256,1,128]{2,1,0:T(1,128)} %bitcast.7), calls=%async_computation.1 | async-start | bytes 262144 | tf_op jit(solution)/shard_map/all_to_all | solution.py:688
  55.8 3.7 %collective-permute-start.3 = (f32[8,8,128]{2,1,0:T(8,128)S(1)}, f32[8,8,128]{2,1,0:T(8,128)S(1)}, u32[]{:S(2)}, u32[]{:S(2)}) collective-permute-start(f32[8,8,128]{2,1,0:T(8,128)S(1)} %get-tuple-element.66), channel_id=1, source_target_pairs={{1,4},{33,36},{65,68},{97,100},{129,132},{161,164},{193,196},{225,... | collective-permute-start | bytes 98312 | tf_op jit(solution)/shard_map/ppermute | solution.py:720
  59.6 1.9 collective-permute-done.3.y_one
  61.5 5.3 %all-to-all-done.1 = f32[256,1,128]{2,1,0:T(1,128)S(1)} async-done(((f32[256,1,128]{2,1,0:T(1,128)}), f32[256,1,128]{2,1,0:T(1,128)S(1)}, u32[]{:S(2)}, u32[]{:S(2)}) %all-to-all-start.1) | async-done | bytes 131104 | tf_op jit(solution)/shard_map/all_to_all | solution.py:688
  68.5 9.1 %all-to-all-start.2 = ((f32[256,1,128]{2,1,0:T(1,128)}), f32[256,1,128]{2,1,0:T(1,128)S(1)}, u32[]{:S(2)}, u32[]{:S(2)}) async-start(f32[256,1,128]{2,1,0:T(1,128)} %bitcast.10), calls=%async_computation.2 | async-start | bytes 262144 | tf_op jit(solution)/shard_map/all_to_all | solution.py:688
  79.8 3.7 %collective-permute-start.7 = (f32[8,8,128]{2,1,0:T(8,128)S(1)}, f32[8,8,128]{2,1,0:T(8,128)S(1)}, u32[]{:S(2)}, u32[]{:S(2)}) collective-permute-start(f32[8,8,128]{2,1,0:T(8,128)S(1)} %get-tuple-element.74), channel_id=1, source_target_pairs={{1,4},{33,36},{65,68},{97,100},{129,132},{161,164},{193,196},{225,... | collective-permute-start | bytes 98312 | tf_op jit(solution)/shard_map/ppermute | solution.py:720
  85.5 5.3 %all-to-all-done.2 = f32[256,1,128]{2,1,0:T(1,128)S(1)} async-done(((f32[256,1,128]{2,1,0:T(1,128)}), f32[256,1,128]{2,1,0:T(1,128)S(1)}, u32[]{:S(2)}, u32[]{:S(2)}) %all-to-all-start.2) | async-done | bytes 131104 | tf_op jit(solution)/shard_map/all_to_all | solution.py:688
  93.4 2.4 %collective-permute-start.11 = (f32[8,8,128]{2,1,0:T(8,128)S(1)}, f32[8,8,128]{2,1,0:T(8,128)S(1)}, u32[]{:S(2)}, u32[]{:S(2)}) collective-permute-start(f32[8,8,128]{2,1,0:T(8,128)S(1)} %get-tuple-element.81), channel_id=1, source_target_pairs={{1,4},{33,36},{65,68},{97,100},{129,132},{161,164},{193,196},{225,... | collective-permute-start | bytes 98312 | tf_op jit(solution)/shard_map/ppermute | solution.py:720
  95.9 2.7 %collective-permute-done.11.y_one = f32[8,8,128]{2,1,0:T(8,128)S(1)} collective-permute-done((f32[8,8,128]{2,1,0:T(8,128)S(1)}, f32[8,8,128]{2,1,0:T(8,128)S(1)}, u32[]{:S(2)}, u32[]{:S(2)}) %collective-permute-start.11) | collective-permute-done | bytes 32800 | tf_op jit(solution)/shard_map/ppermute | solution.py:720
  100.6 25.2 %all_to_all.76 = f32[256,1,128]{2,1,0:T(1,128)S(1)} all-to-all(f32[256,1,128]{2,1,0:T(1,128)S(1)} %bitcast.41), channel_id=1, replica_groups=mesh['strip'=16,'period'=16] {'strip','period'}, dimensions={0} | all-to-all | bytes 262144 | tf_op jit(solution)/shard_map/all_to_all | solution.py:688
  127.3 5.4 %all-to-all-start.4 = ((f32[256,1,128]{2,1,0:T(1,128)}), f32[256,1,128]{2,1,0:T(1,128)S(1)}, u32[]{:S(2)}, u32[]{:S(2)}) async-start(f32[256,1,128]{2,1,0:T(1,128)} %bitcast.16), calls=%async_computation.4 | async-start | bytes 262144 | tf_op jit(solution)/shard_map/all_to_all | solution.py:688
  135.1 3.7 %collective-permute-start.15 = (f32[8,8,128]{2,1,0:T(8,128)S(1)}, f32[8,8,128]{2,1,0:T(8,128)S(1)}, u32[]{:S(2)}, u32[]{:S(2)}) collective-permute-start(f32[8,8,128]{2,1,0:T(8,128)S(1)} %get-tuple-element.92), channel_id=1, source_target_pairs={{1,4},{33,36},{65,68},{97,100},{129,132},{161,164},{193,196},{225,... | collective-permute-start | bytes 98312 | tf_op jit(solution)/shard_map/ppermute | solution.py:720
  140.9 5.3 %all-to-all-done.4 = f32[256,1,128]{2,1,0:T(1,128)S(1)} async-done(((f32[256,1,128]{2,1,0:T(1,128)}), f32[256,1,128]{2,1,0:T(1,128)S(1)}, u32[]{:S(2)}, u32[]{:S(2)}) %all-to-all-start.4) | async-done | bytes 131104 | tf_op jit(solution)/shard_map/all_to_all | solution.py:688
  147.9 9.1 %all-to-all-start.5 = ((f32[256,1,128]{2,1,0:T(1,128)}), f32[256,1,128]{2,1,0:T(1,128)S(1)}, u32[]{:S(2)}, u32[]{:S(2)}) async-start(f32[256,1,128]{2,1,0:T(1,128)} %bitcast.19), calls=%async_computation.5 | async-start | bytes 262144 | tf_op jit(solution)/shard_map/all_to_all | solution.py:688
  159.2 3.7 %collective-permute-start.19 = (f32[8,8,128]{2,1,0:T(8,128)S(1)}, f32[8,8,128]{2,1,0:T(8,128)S(1)}, u32[]{:S(2)}, u32[]{:S(2)}) collective-permute-start(f32[8,8,128]{2,1,0:T(8,128)S(1)} %get-tuple-element.100), channel_id=1, source_target_pairs={{1,4},{33,36},{65,68},{97,100},{129,132},{161,164},{193,196},{225,... | collective-permute-start | bytes 98312 | tf_op jit(solution)/shard_map/ppermute | solution.py:720
  164.9 5.3 %all-to-all-done.5 = f32[256,1,128]{2,1,0:T(1,128)S(1)} async-done(((f32[256,1,128]{2,1,0:T(1,128)}), f32[256,1,128]{2,1,0:T(1,128)S(1)}, u32[]{:S(2)}, u32[]{:S(2)}) %all-to-all-start.5) | async-done | bytes 131104 | tf_op jit(solution)/shard_map/all_to_all | solution.py:688
  172.7 2.4 %collective-permute-start.23 = (f32[8,8,128]{2,1,0:T(8,128)S(1)}, f32[8,8,128]{2,1,0:T(8,128)S(1)}, u32[]{:S(2)}, u32[]{:S(2)}) collective-permute-start(f32[8,8,128]{2,1,0:T(8,128)S(1)} %get-tuple-element.107), channel_id=1, source_target_pairs={{1,4},{33,36},{65,68},{97,100},{129,132},{161,164},{193,196},{225,... | collective-permute-start | bytes 98312 | tf_op jit(solution)/shard_map/ppermute | solution.py:720
  175.3 2.7 %collective-permute-done.23.y_one = f32[8,8,128]{2,1,0:T(8,128)S(1)} collective-permute-done((f32[8,8,128]{2,1,0:T(8,128)S(1)}, f32[8,8,128]{2,1,0:T(8,128)S(1)}, u32[]{:S(2)}, u32[]{:S(2)}) %collective-permute-start.23) | collective-permute-done | bytes 32800 | tf_op jit(solution)/shard_map/ppermute | solution.py:720
  178.8 21.3 %all_to_all.77.got = f32[32,7,8,128]{3,2,1,0:T(8,128)S(1)} all-to-all(f32[32,7,8,128]{3,2,1,0:T(8,128)S(1)} %shard_map.147), channel_id=1, replica_groups={{0,1,2,3,4,5,6,7,8,9,10,11,12,13,14,15,16,17,18,19,20,21,22,23,24,25,26..., dimensions={0} | all-to-all | bytes 1835008 | tf_op jit(solution)/shard_map/all_to_all | solution.py:699
  200.8 7.6 %all-to-all-start.7 = ((f32[8,1,128]{2,1,0:T(1,128)}), f32[8,1,128]{2,1,0:T(1,128)S(1)}, u32[]{:S(2)}, u32[]{:S(2)}) async-start(f32[8,1,128]{2,1,0:T(1,128)} %bitcast.26), calls=%async_computation.7 | async-start | bytes 8192 | tf_op jit(solution)/shard_map/all_to_all | solution.py:694
  209.6 5.4 %all-to-all-done.7 = f32[8,1,128]{2,1,0:T(1,128)S(1)} async-done(((f32[8,1,128]{2,1,0:T(1,128)}), f32[8,1,128]{2,1,0:T(1,128)S(1)}, u32[]{:S(2)}, u32[]{:S(2)}) %all-to-all-start.7) | async-done | bytes 4128 | tf_op jit(solution)/shard_map/all_to_all | solution.py:694
  (60 shorter events, 37.0 us)
Async XLA Ops:
  8.0 31.7 %all-to-all-start = ((f32[32,9,8,128]{3,2,1,0:T(8,128)}), f32[32,9,8,128]{3,2,1,0:T(8,128)S(1)}, u32[]{:S(2)}, u32[]{:S(2)}) async-start(f32[32,9,8,128]{3,2,1,0:T(8,128)} %shard_map.139), calls=%async_computation | async-start | bytes 2359296 | tf_op jit(solution)/shard_map/all_to_all | solution.py:699
  41.1 25.7 %all-to-all-start.1 = ((f32[256,1,128]{2,1,0:T(1,128)}), f32[256,1,128]{2,1,0:T(1,128)S(1)}, u32[]{:S(2)}, u32[]{:S(2)}) async-start(f32[256,1,128]{2,1,0:T(1,128)} %bitcast.7), calls=%async_computation.1 | async-start | bytes 262144 | tf_op jit(solution)/shard_map/all_to_all | solution.py:688
  53.5 8.0 %collective-permute-start.1 = (f32[16,8,128]{2,1,0:T(8,128)S(1)}, f32[16,8,128]{2,1,0:T(8,128)S(1)}, u32[]{:S(2)}, u32[]{:S(2)}) collective-permute-start(f32[16,8,128]{2,1,0:T(8,128)S(1)} %get-tuple-element.64), channel_id=1, source_target_pairs={{0,32},{1,33},{2,34},{3,35},{4,36},{5,37},{6,38},{7,39},{8,40},{9,... | collective-permute-start | bytes 196616 | tf_op jit(solution)/shard_map/ppermute | solution.py:709
  55.1 6.4 %collective-permute-start.2 = (f32[16,8,128]{2,1,0:T(8,128)S(1)}, f32[16,8,128]{2,1,0:T(8,128)S(1)}, u32[]{:S(2)}, u32[]{:S(2)}) collective-permute-start(f32[16,8,128]{2,1,0:T(8,128)S(1)} %get-tuple-element.65), channel_id=1, source_target_pairs={{32,64},{33,65},{34,66},{35,67},{36,68},{37,69},{38,70},{39,71},{4... | collective-permute-start | bytes 196616 | tf_op jit(solution)/shard_map/ppermute | solution.py:709
  55.8 5.7 %collective-permute-start.3 = (f32[8,8,128]{2,1,0:T(8,128)S(1)}, f32[8,8,128]{2,1,0:T(8,128)S(1)}, u32[]{:S(2)}, u32[]{:S(2)}) collective-permute-start(f32[8,8,128]{2,1,0:T(8,128)S(1)} %get-tuple-element.66), channel_id=1, source_target_pairs={{1,4},{33,36},{65,68},{97,100},{129,132},{161,164},{193,196},{225,... | collective-permute-start | bytes 98312 | tf_op jit(solution)/shard_map/ppermute | solution.py:720
  68.5 22.4 %all-to-all-start.2 = ((f32[256,1,128]{2,1,0:T(1,128)}), f32[256,1,128]{2,1,0:T(1,128)S(1)}, u32[]{:S(2)}, u32[]{:S(2)}) async-start(f32[256,1,128]{2,1,0:T(1,128)} %bitcast.10), calls=%async_computation.2 | async-start | bytes 262144 | tf_op jit(solution)/shard_map/all_to_all | solution.py:688
  77.6 8.0 %collective-permute-start.5 = (f32[16,8,128]{2,1,0:T(8,128)S(1)}, f32[16,8,128]{2,1,0:T(8,128)S(1)}, u32[]{:S(2)}, u32[]{:S(2)}) collective-permute-start(f32[16,8,128]{2,1,0:T(8,128)S(1)} %get-tuple-element.72), channel_id=1, source_target_pairs={{0,32},{1,33},{2,34},{3,35},{4,36},{5,37},{6,38},{7,39},{8,40},{9,... | collective-permute-start | bytes 196616 | tf_op jit(solution)/shard_map/ppermute | solution.py:709
  79.2 6.4 %collective-permute-start.6 = (f32[16,8,128]{2,1,0:T(8,128)S(1)}, f32[16,8,128]{2,1,0:T(8,128)S(1)}, u32[]{:S(2)}, u32[]{:S(2)}) collective-permute-start(f32[16,8,128]{2,1,0:T(8,128)S(1)} %get-tuple-element.73), channel_id=1, source_target_pairs={{32,64},{33,65},{34,66},{35,67},{36,68},{37,69},{38,70},{39,71},{4... | collective-permute-start | bytes 196616 | tf_op jit(solution)/shard_map/ppermute | solution.py:709
  79.8 5.7 %collective-permute-start.7 = (f32[8,8,128]{2,1,0:T(8,128)S(1)}, f32[8,8,128]{2,1,0:T(8,128)S(1)}, u32[]{:S(2)}, u32[]{:S(2)}) collective-permute-start(f32[8,8,128]{2,1,0:T(8,128)S(1)} %get-tuple-element.74), channel_id=1, source_target_pairs={{1,4},{33,36},{65,68},{97,100},{129,132},{161,164},{193,196},{225,... | collective-permute-start | bytes 98312 | tf_op jit(solution)/shard_map/ppermute | solution.py:720
  91.9 6.7 %collective-permute-start.9 = (f32[16,8,128]{2,1,0:T(8,128)S(1)}, f32[16,8,128]{2,1,0:T(8,128)S(1)}, u32[]{:S(2)}, u32[]{:S(2)}) collective-permute-start(f32[16,8,128]{2,1,0:T(8,128)S(1)} %get-tuple-element.79), channel_id=1, source_target_pairs={{0,32},{1,33},{2,34},{3,35},{4,36},{5,37},{6,38},{7,39},{8,40},{9,... | collective-permute-start | bytes 196616 | tf_op jit(solution)/shard_map/ppermute | solution.py:709
  92.7 5.9 %collective-permute-start.10 = (f32[16,8,128]{2,1,0:T(8,128)S(1)}, f32[16,8,128]{2,1,0:T(8,128)S(1)}, u32[]{:S(2)}, u32[]{:S(2)}) collective-permute-start(f32[16,8,128]{2,1,0:T(8,128)S(1)} %get-tuple-element.80), channel_id=1, source_target_pairs={{32,64},{33,65},{34,66},{35,67},{36,68},{37,69},{38,70},{39,71},{4... | collective-permute-start | bytes 196616 | tf_op jit(solution)/shard_map/ppermute | solution.py:709
  93.4 5.2 %collective-permute-start.11 = (f32[8,8,128]{2,1,0:T(8,128)S(1)}, f32[8,8,128]{2,1,0:T(8,128)S(1)}, u32[]{:S(2)}, u32[]{:S(2)}) collective-permute-start(f32[8,8,128]{2,1,0:T(8,128)S(1)} %get-tuple-element.81), channel_id=1, source_target_pairs={{1,4},{33,36},{65,68},{97,100},{129,132},{161,164},{193,196},{225,... | collective-permute-start | bytes 98312 | tf_op jit(solution)/shard_map/ppermute | solution.py:720
  127.3 18.9 %all-to-all-start.4 = ((f32[256,1,128]{2,1,0:T(1,128)}), f32[256,1,128]{2,1,0:T(1,128)S(1)}, u32[]{:S(2)}, u32[]{:S(2)}) async-start(f32[256,1,128]{2,1,0:T(1,128)} %bitcast.16), calls=%async_computation.4 | async-start | bytes 262144 | tf_op jit(solution)/shard_map/all_to_all | solution.py:688
  132.7 8.1 %collective-permute-start.13 = (f32[16,8,128]{2,1,0:T(8,128)S(1)}, f32[16,8,128]{2,1,0:T(8,128)S(1)}, u32[]{:S(2)}, u32[]{:S(2)}) collective-permute-start(f32[16,8,128]{2,1,0:T(8,128)S(1)} %get-tuple-element.90), channel_id=1, source_target_pairs={{0,32},{1,33},{2,34},{3,35},{4,36},{5,37},{6,38},{7,39},{8,40},{9,... | collective-permute-start | bytes 196616 | tf_op jit(solution)/shard_map/ppermute | solution.py:709
  134.5 6.4 %collective-permute-start.14 = (f32[16,8,128]{2,1,0:T(8,128)S(1)}, f32[16,8,128]{2,1,0:T(8,128)S(1)}, u32[]{:S(2)}, u32[]{:S(2)}) collective-permute-start(f32[16,8,128]{2,1,0:T(8,128)S(1)} %get-tuple-element.91), channel_id=1, source_target_pairs={{32,64},{33,65},{34,66},{35,67},{36,68},{37,69},{38,70},{39,71},{4... | collective-permute-start | bytes 196616 | tf_op jit(solution)/shard_map/ppermute | solution.py:709
  135.1 5.7 %collective-permute-start.15 = (f32[8,8,128]{2,1,0:T(8,128)S(1)}, f32[8,8,128]{2,1,0:T(8,128)S(1)}, u32[]{:S(2)}, u32[]{:S(2)}) collective-permute-start(f32[8,8,128]{2,1,0:T(8,128)S(1)} %get-tuple-element.92), channel_id=1, source_target_pairs={{1,4},{33,36},{65,68},{97,100},{129,132},{161,164},{193,196},{225,... | collective-permute-start | bytes 98312 | tf_op jit(solution)/shard_map/ppermute | solution.py:720
  147.9 22.4 %all-to-all-start.5 = ((f32[256,1,128]{2,1,0:T(1,128)}), f32[256,1,128]{2,1,0:T(1,128)S(1)}, u32[]{:S(2)}, u32[]{:S(2)}) async-start(f32[256,1,128]{2,1,0:T(1,128)} %bitcast.19), calls=%async_computation.5 | async-start | bytes 262144 | tf_op jit(solution)/shard_map/all_to_all | solution.py:688
  157.0 8.0 %collective-permute-start.17 = (f32[16,8,128]{2,1,0:T(8,128)S(1)}, f32[16,8,128]{2,1,0:T(8,128)S(1)}, u32[]{:S(2)}, u32[]{:S(2)}) collective-permute-start(f32[16,8,128]{2,1,0:T(8,128)S(1)} %get-tuple-element.98), channel_id=1, source_target_pairs={{0,32},{1,33},{2,34},{3,35},{4,36},{5,37},{6,38},{7,39},{8,40},{9,... | collective-permute-start | bytes 196616 | tf_op jit(solution)/shard_map/ppermute | solution.py:709
  158.5 6.4 %collective-permute-start.18 = (f32[16,8,128]{2,1,0:T(8,128)S(1)}, f32[16,8,128]{2,1,0:T(8,128)S(1)}, u32[]{:S(2)}, u32[]{:S(2)}) collective-permute-start(f32[16,8,128]{2,1,0:T(8,128)S(1)} %get-tuple-element.99), channel_id=1, source_target_pairs={{32,64},{33,65},{34,66},{35,67},{36,68},{37,69},{38,70},{39,71},{4... | collective-permute-start | bytes 196616 | tf_op jit(solution)/shard_map/ppermute | solution.py:709
  159.2 5.7 %collective-permute-start.19 = (f32[8,8,128]{2,1,0:T(8,128)S(1)}, f32[8,8,128]{2,1,0:T(8,128)S(1)}, u32[]{:S(2)}, u32[]{:S(2)}) collective-permute-start(f32[8,8,128]{2,1,0:T(8,128)S(1)} %get-tuple-element.100), channel_id=1, source_target_pairs={{1,4},{33,36},{65,68},{97,100},{129,132},{161,164},{193,196},{225,... | collective-permute-start | bytes 98312 | tf_op jit(solution)/shard_map/ppermute | solution.py:720
  171.2 6.7 %collective-permute-start.21 = (f32[16,8,128]{2,1,0:T(8,128)S(1)}, f32[16,8,128]{2,1,0:T(8,128)S(1)}, u32[]{:S(2)}, u32[]{:S(2)}) collective-permute-start(f32[16,8,128]{2,1,0:T(8,128)S(1)} %get-tuple-element.105), channel_id=1, source_target_pairs={{0,32},{1,33},{2,34},{3,35},{4,36},{5,37},{6,38},{7,39},{8,40},{9,... | collective-permute-start | bytes 196616 | tf_op jit(solution)/shard_map/ppermute | solution.py:709
  172.1 5.9 %collective-permute-start.22 = (f32[16,8,128]{2,1,0:T(8,128)S(1)}, f32[16,8,128]{2,1,0:T(8,128)S(1)}, u32[]{:S(2)}, u32[]{:S(2)}) collective-permute-start(f32[16,8,128]{2,1,0:T(8,128)S(1)} %get-tuple-element.106), channel_id=1, source_target_pairs={{32,64},{33,65},{34,66},{35,67},{36,68},{37,69},{38,70},{39,71},{4... | collective-permute-start | bytes 196616 | tf_op jit(solution)/shard_map/ppermute | solution.py:709
  172.7 5.2 %collective-permute-start.23 = (f32[8,8,128]{2,1,0:T(8,128)S(1)}, f32[8,8,128]{2,1,0:T(8,128)S(1)}, u32[]{:S(2)}, u32[]{:S(2)}) collective-permute-start(f32[8,8,128]{2,1,0:T(8,128)S(1)} %get-tuple-element.107), channel_id=1, source_target_pairs={{1,4},{33,36},{65,68},{97,100},{129,132},{161,164},{193,196},{225,... | collective-permute-start | bytes 98312 | tf_op jit(solution)/shard_map/ppermute | solution.py:720
  200.8 14.1 %all-to-all-start.7 = ((f32[8,1,128]{2,1,0:T(1,128)}), f32[8,1,128]{2,1,0:T(1,128)S(1)}, u32[]{:S(2)}, u32[]{:S(2)}) async-start(f32[8,1,128]{2,1,0:T(1,128)} %bitcast.26), calls=%async_computation.7 | async-start | bytes 8192 | tf_op jit(solution)/shard_map/all_to_all | solution.py:694
  (10 other events, 49.0 us)
